TPU v7x, 256 devices: a whole 4x4x8 slice. The times are simulated.
256 devices in a mesh: row: 16 (over z, x_lo), col: 16 (over x_hi, y, core).
Axes of the slice: x: 4 (x_hi: 2, x_lo: 2; x = x_hi * 2 + x_lo), y: 4, z: 8, core: 2. Of those that a mesh axis runs over, the one named last changes fastest.
Arguments:
- patches: bfloat16 [512, 256, 768], P('row', 'col'), may hold values from -6 to 6
- norm_gain: float32 [768], replicated, may hold values from 0.25 to 1.75
- w_qkv: bfloat16 [768, 2304], replicated, may hold values from -0.21875 to 0.21875
- pool_q: float32 [9, 768], replicated, may hold values from -30 to 30, as said below
- pool_kv: float32 [9, 1536], replicated, may hold values from -2 to 2
- w_out: bfloat16 [768, 768], replicated, may hold values from -0.21875 to 0.21875
Outputs:
- mixed: bfloat16 [256, 128, 768], P('row', 'col')
Inputs may be any that keep to these rules, and one draw needn't show every extreme that they name: `pool_q`: query pooling taps, nonzero, of either sign.
All inputs are finite; a program needn't handle non-finite values.
Results may differ from a plain program's by a relative error of at most 0.017.
The roundings to bfloat16 on the way count: a program that leaves them out, or rounds other values in their place, can miss the bound.
Values may be sent and summed in bfloat16 or wider, within the bound.
No kernel may reach another device: no remote copies, remote signals or barrier semaphores. Data moves between devices by JAX's collectives and lax.ppermute only.
A program may use at most 128 MiB of HBM per device.

v0:
```python
import functools
import math

import jax
import jax.numpy as jnp
from jax import lax
from jax.experimental import pallas as pl
from jax.experimental.pallas import tpu as pltpu
from jax.sharding import Mesh
from jax.sharding import PartitionSpec as P

AXES = ("zq", "zc", "xl", "xh", "y", "core")
ROW = ("zq", "zc", "xl")
COL = ("xh", "y", "core")
HEAD = 64
GROUP = 3
WIDE = GROUP * HEAD
SCALE = HEAD**-0.5 * math.log2(math.e)
STATS = 16
bf16, f32 = jnp.bfloat16, jnp.float32


def shifted(block, axis, distance):
    count = lax.axis_size(axis)
    return lax.ppermute(block, axis, [(i, (i + distance) % count) for i in range(count)])


def shifted_x(block, distance):
    place = lambda i: (i % 2) * 2 + i // 2
    route = [(place(i), place((i + distance) % 4)) for i in range(4)]
    return lax.ppermute(block, ("xl", "xh"), route)


def passed_along(block, axis):
    count = lax.axis_size(axis)
    return lax.ppermute(block, axis, [(i - 1, i) for i in range(1, count)])


def corner(block):
    rows, cols = lax.axis_size(ROW), lax.axis_size(COL)
    route = [((r - 1) * cols + c - 1, r * cols + c) for r in range(1, rows) for c in range(1, cols)]
    return lax.ppermute(block, AXES, route)


def normalised(values, gain):
    center = values - jnp.mean(values, axis=-1, keepdims=True)
    spread = jnp.mean(center * center, axis=-1, keepdims=True)
    return center * lax.rsqrt(spread + 1e-06) * gain


def project(tokens, weights):
    return jnp.dot(tokens, weights, preferred_element_type=f32).astype(bf16)


ORDER = (0, 1, 3, 4, 5, 7, 8, 9, 11, 12, 13, 2, 6, 10, 14, 15)
KEY_COLUMNS = 11


def keep(plain, values):
    for k in range(plain.shape[0]):
        plain[k] = values[:, 128 * k : 128 * (k + 1)]


def every_nth(plain, start, step):
    picked = [plain[k, pl.ds(start, 8, stride=step), :] for k in range(plain.shape[0])]
    return jnp.concatenate(picked, 1)


def tokens_kernel(patches_ref, gain_ref, tokens_ref, column_ref, row_ref, corner_ref, plain):
    rows, cols, width = patches_ref.shape
    keep(plain, patches_ref[...].astype(f32).reshape(rows * cols, width))
    gain = gain_ref[...].reshape(1, width)
    last = [None] * cols
    for place, c in enumerate(ORDER):
        parts = [every_nth(plain, cols * r + c, 4 * cols) for r in range(4)]
        column = normalised(jnp.concatenate(parts, 0), gain)
        tokens_ref[pl.ds(32 * place, 32), :] = column.astype(bf16)
        last[c] = column[31:]
    column_ref[...] = column.astype(bf16)
    row_ref[...] = jnp.concatenate(last, 0).astype(bf16)
    corner_ref[...] = last[-1].astype(bf16)


def whole(shape):
    return pl.BlockSpec(shape, lambda *_: (0,) * len(shape))


def normalised_tokens(patches, gain):
    rows, cols, width = patches.shape
    shapes = [(rows * cols, width), (rows, width), (cols, width), (1, width)]
    return pl.pallas_call(
        tokens_kernel,
        in_specs=[pl.BlockSpec(memory_space=pltpu.VMEM)] * 2,
        out_specs=[pl.BlockSpec(memory_space=pltpu.VMEM)] * 4,
        out_shape=[jax.ShapeDtypeStruct(s, bf16) for s in shapes],
        scratch_shapes=[pltpu.VMEM((width // 128, rows * cols, 128), f32)],
        compiler_params=pltpu.CompilerParams(vmem_limit_bytes=16 * 2**20),
        cost_estimate=pl.CostEstimate(flops=4_000_000_000, bytes_accessed=1_000_000, transcendentals=0),
    )(patches, gain)


def halo_tokens(upper_ref, left_ref, corner_ref):
    rest = jnp.zeros((15, left_ref.shape[1]), f32)
    every = [left_ref[...].astype(f32), upper_ref[...].astype(f32), corner_ref[...].astype(f32), rest]
    return jnp.concatenate(every, 0).astype(bf16)


def columns_of(own, halo, columns):
    first = lax.broadcasted_iota(jnp.int32, (8, own.shape[1]), 0) == 0
    groups = {}
    for c in columns:
        if c < 0:
            block, above = halo[0:32], halo[48:49]
        else:
            place = ORDER.index(c)
            block, above = own[32 * place : 32 * place + 32].astype(f32), halo[32 + c : 33 + c]
        four = [block[8 * r : 8 * r + 8] for r in range(4)]
        groups[c] = [jnp.where(first, above, pltpu.roll(four[3], 1, 0))] + four
    return groups


def pooled(groups, taps, column, row):
    total = None
    for a in range(3):
        for b in range(3):
            term = taps[3 * a + b] * groups[column + b - 1][row + a]
            total = term if total is None else total + term
    return total


def keyvals_kernel(here_ref, tokens_ref, upper_ref, left_ref, corner_ref, w_ref, pool_ref, *refs):
    out_refs, parts = refs[:-1], refs[-1]
    halo_in = halo_tokens(upper_ref, left_ref, corner_ref)
    width = tokens_ref.shape[1]
    both = []
    for part in range(2):
        cols = pl.ds(part * width, width)
        weights = w_ref[:, (part + 1) * width : (part + 2) * width]
        halo = project(halo_in, weights).astype(f32)
        own = project(tokens_ref[: 32 * KEY_COLUMNS], weights)
        taps = [pool_ref[t : t + 1, cols] for t in range(9)]
        groups = columns_of(own, halo, (-1,) + ORDER[:KEY_COLUMNS])
        both.append(jnp.concatenate([pooled(groups, taps, 4 * j, 0) for j in range(4)], 0))
    count = width // WIDE
    for g in range(count):
        lanes = slice(g * WIDE, (g + 1) * WIDE)
        parts[g] = jnp.concatenate([p[:, lanes] for p in both], 1).astype(bf16)
    here = here_ref[0]
    for distance, out_ref in enumerate(out_refs):
        out_ref[...] = parts[lax.rem(here + distance, count)]


def queries_kernel(tokens_ref, upper_ref, left_ref, corner_ref, w_ref, pool_ref, out_ref):
    width = tokens_ref.shape[1]
    weights = w_ref[:, :width]
    halo = project(halo_tokens(upper_ref, left_ref, corner_ref), weights).astype(f32)
    own = project(tokens_ref[...], weights)
    taps = [pool_ref[t : t + 1, :] for t in range(9)]
    groups = columns_of(own, halo, range(-1, 16))
    rows = [pooled(groups, taps, 2 * j, 2 * p) for j in range(8) for p in range(2)]
    turned = jnp.concatenate(rows, 0).T.astype(bf16)
    count = width // WIDE
    for g in range(count):
        block = turned[g * WIDE : (g + 1) * WIDE]
        for copy in range(out_ref.shape[0] // count):
            out_ref[copy * count + g] = block


def pool_call(kernel, tokens, halo, w_qkv, taps, out_shapes, scratch=(), scalars=()):
    return pl.pallas_call(
        kernel,
        in_specs=[pl.BlockSpec(memory_space=pltpu.SMEM)] * len(scalars)
        + [pl.BlockSpec(memory_space=pltpu.VMEM)] * (3 + len(halo)),
        out_specs=[pl.BlockSpec(memory_space=pltpu.VMEM)] * len(out_shapes),
        out_shape=[jax.ShapeDtypeStruct(s, bf16) for s in out_shapes],
        scratch_shapes=[pltpu.VMEM(s, bf16) for s in scratch],
        compiler_params=pltpu.CompilerParams(vmem_limit_bytes=24 * 2**20),
        cost_estimate=pl.CostEstimate(flops=1_500_000_000, bytes_accessed=4_000_000, transcendentals=0),
    )(*scalars, tokens, *halo, w_qkv, taps)


def attend_kernel(first, last, qb, blocks, q_ref, *refs):
    block_refs, refs = refs[:blocks], refs[blocks:]
    if first:
        stat_in, acc_in = None, None
    else:
        stat_in, acc_in, *refs = refs
    if last:
        out_ref, qz, stat, acc = refs
    else:
        stat, acc, qz = refs
    tiles = q_ref.shape[0]
    count = tiles * 128
    zero = jnp.zeros((HEAD, 128), bf16)
    for t in range(tiles):
        lanes = slice(t * 128, (t + 1) * 128)
        for h in range(GROUP):
            here = HEAD * (h % 2)
            qz[h, here : here + HEAD, lanes] = q_ref[t, HEAD * h : HEAD * (h + 1)]
            qz[h, HEAD - here : 2 * HEAD - here, lanes] = zero

    jobs = [(j, h) for j in range(count // qb) for h in range(GROUP)]

    def operands():
        block = jnp.concatenate([r[...] for r in block_refs], 0)
        values = block[:, 128:].T
        ones = jnp.ones((16, block.shape[0]), bf16)
        lefts = [jnp.concatenate([values[HEAD * h : HEAD * (h + 1)], ones], 0) for h in range(1, GROUP + 1)]
        return block, lefts

    def scores(block, j, h):
        keys = block[:, 128 * (h // 2) : 128 * (h // 2) + 128]
        return jnp.dot(keys, qz[h, :, j * qb : (j + 1) * qb], preferred_element_type=f32)

    def fold_lazily():
        block, lefts = operands()
        rise = jnp.zeros((1, qb), f32)
        ready = scores(block, *jobs[0])
        for place, (j, h) in enumerate(jobs):
            now = ready
            if place + 1 < len(jobs):
                ready = scores(block, *jobs[place + 1])
            lanes = slice(j * qb, (j + 1) * qb)
            rows = slice(HEAD * h, HEAD * (h + 1))
            old = stat_in[h : h + 1, lanes]
            new = jnp.maximum(old, jnp.max(now, axis=0, keepdims=True))
            rise = jnp.maximum(rise, new - old)
            weights = jnp.exp2((now - old) * SCALE).astype(bf16)
            part = jnp.dot(lefts[h], weights, preferred_element_type=f32)
            factor = jnp.exp2((old - new) * SCALE)
            stat[h : h + 1, lanes] = new
            stat[8 + h : 9 + h, lanes] = (stat_in[8 + h : 9 + h, lanes] + part[HEAD : HEAD + 1]) * factor
            acc[rows, lanes] = (acc_in[rows, lanes] + part[:HEAD]) * factor
        return rise

    def fold(wide):
        @pl.loop(0, count // wide)
        def _(t):
            lanes = pl.ds(pl.multiple_of(t * wide, wide), wide)
            block, lefts = operands()
            for h in range(GROUP):
                rows = slice(HEAD * h, HEAD * (h + 1))
                keys = block[:, 128 * (h // 2) : 128 * (h // 2) + 128]
                now = jnp.dot(keys, qz[h, :, lanes], preferred_element_type=f32)
                new = jnp.max(now, axis=0, keepdims=True)
                if not first:
                    old = stat_in[h : h + 1, lanes]
                    new = jnp.maximum(old, new)
                weights = jnp.exp2((now - new) * SCALE).astype(bf16)
                part = jnp.dot(lefts[h], weights, preferred_element_type=f32)
                total, numer = part[HEAD : HEAD + 1], part[:HEAD]
                if not first:
                    factor = jnp.exp2((old - new) * SCALE)
                    total = stat_in[8 + h : 9 + h, lanes] * factor + total
                    numer = acc_in[rows, lanes] * factor + numer
                stat[h : h + 1, lanes] = new
                stat[8 + h : 9 + h, lanes] = total
                acc[rows, lanes] = numer

    if first:
        fold(qb)
    else:
        rise = fold_lazily()

        @pl.when(jnp.logical_not(jnp.max(rise) * SCALE < 60.0))
        def _():
            fold(128)

    if last:
        total = stat[8 : 8 + GROUP]
        logs = stat[0:GROUP] * SCALE + jnp.log2(total)
        high = logs.astype(bf16)
        left = logs - high.astype(f32)
        middle = left.astype(bf16)
        low = left - middle.astype(f32)
        three = [high.astype(f32), middle.astype(f32), low]
        packed = jnp.concatenate(three + [jnp.zeros((STATS - 9, count), f32)], 0).astype(bf16)
        for t in range(tiles):
            lanes = slice(t * 128, (t + 1) * 128)
            for h in range(GROUP):
                rows = slice(HEAD * h, HEAD * (h + 1))
                out_ref[t, rows] = (acc[rows, lanes] / total[h : h + 1, lanes]).astype(bf16)
            out_ref[t, WIDE:] = packed[:, lanes]


def attend(queries, blocks, carry, last=False, qb=512):
    tiles = queries.shape[0]
    count = tiles * 128
    keys = sum(b.shape[0] for b in blocks)
    carry_shapes = [(16, count), (WIDE, count)]
    if last:
        out_shape = [jax.ShapeDtypeStruct((tiles, WIDE + STATS, 128), bf16)]
        scratch = [pltpu.VMEM(s, f32) for s in carry_shapes]
    else:
        out_shape = [jax.ShapeDtypeStruct(s, f32) for s in carry_shapes]
        scratch = []
    carry = [] if carry is None else carry
    work = GROUP * count * keys
    outs = pl.pallas_call(
        functools.partial(attend_kernel, not carry, last, qb, len(blocks)),
        in_specs=[pl.BlockSpec(memory_space=pltpu.VMEM)] * (1 + len(blocks) + len(carry)),
        out_specs=[pl.BlockSpec(memory_space=pltpu.VMEM)] * len(out_shape),
        out_shape=out_shape,
        scratch_shapes=[pltpu.VMEM((GROUP, 128, count), bf16)] + scratch,
        compiler_params=pltpu.CompilerParams(vmem_limit_bytes=24 * 2**20),
        cost_estimate=pl.CostEstimate(
            flops=work * 1, bytes_accessed=1024, transcendentals=0
        ),
    )(queries, *blocks, *carry)
    return outs[0] if last else outs


def finish_kernel(parts_ref, w_ref, out_ref, rows):
    groups = parts_ref.shape[0] // 2
    pieces = []
    for g in range(groups):
        pair = [parts_ref[g], parts_ref[groups + g]]
        logs = []
        for p in pair:
            s = p[WIDE:].astype(f32)
            logs.append((s[0:3] + s[3:6]) + s[6:9])
        top = jnp.maximum(logs[0], logs[1])
        shares = [jnp.exp2(a - top) for a in logs]
        total = shares[0] + shares[1]
        for h in range(GROUP):
            head = slice(HEAD * h, HEAD * (h + 1))
            both = [p[head].astype(f32) * (s[h : h + 1] / total[h : h + 1]) for p, s in zip(pair, shares)]
            pieces.append(both[0] + both[1])
    attended = jnp.concatenate(pieces, 0).T.astype(bf16)
    keep(rows, jnp.dot(attended, w_ref[...], preferred_element_type=f32))
    for r in range(out_ref.shape[0]):
        start = 8 * (r % 2) + r // 2
        out_ref[r] = every_nth(rows, start, 16).astype(bf16)


def finish(parts, w_out):
    shape = (parts.shape[2], w_out.shape[1])
    return pl.pallas_call(
        finish_kernel,
        out_shape=jax.ShapeDtypeStruct((16, 8, shape[1]), bf16),
        scratch_shapes=[pltpu.VMEM((shape[1] // 128, shape[0], 128), f32)],
        compiler_params=pltpu.CompilerParams(vmem_limit_bytes=24 * 2**20),
    )(parts, w_out)


def on_device(patches, norm_gain, w_qkv, pool_q, pool_kv, w_out):
    tokens, last_column, last_row, last_token = normalised_tokens(patches, norm_gain)
    halo = (passed_along(last_row, ROW), passed_along(last_column, COL), corner(last_token))
    groups = lax.axis_size("y")
    part = (32, 2 * WIDE)
    here = [lax.axis_index("y").reshape(1)]
    parts = pool_call(keyvals_kernel, tokens, halo, w_qkv, pool_kv, [part] * groups, [(groups, *part)], here)
    own = [parts[0]] + [shifted(part, "y", d) for d, part in enumerate(parts) if d]
    own = jnp.concatenate(own, 0)
    (turned,) = pool_call(queries_kernel, tokens, halo, w_qkv, pool_q, [(2 * groups, WIDE, 128)])
    every_query = lax.all_to_all(turned, ("zc", "y"), 0, 0, tiled=True)
    tie = lax.optimization_barrier
    line = [own, shifted(own, "zq", 2), shifted(own, "zq", 1), shifted(own, "zq", -1)]
    line = jnp.concatenate(line, 0)
    after, before = shifted_x(line, 1), shifted_x(line, -1)
    swap = lambda block: shifted(block, "core", 1)
    carry = attend(every_query, [line], None)
    carry = attend(every_query, [swap(line)], carry)
    after, before, carry = tie((after, before, carry))
    half = line.shape[0] // 2
    far = [shifted_x(after[:half], 1), shifted_x(before[half:], -1)]
    for block in (after, swap(after), before, swap(before)):
        carry = attend(every_query, [block], carry)
    far, carry = tie((far, carry))
    swapped = [swap(block) for block in far]
    carry = attend(every_query, far, carry)
    partial = attend(every_query, swapped, carry, last=True)
    parts = lax.all_to_all(partial, ("zc", "y"), 0, 0, tiled=True)
    return finish(parts, w_out)


def solution(mesh):
    fine = Mesh(mesh.devices.reshape(4, 2, 2, 2, 4, 2), AXES)
    tiles = P(ROW, COL, None)
    return jax.shard_map(
        on_device,
        mesh=fine,
        in_specs=(tiles, P(), P(), P(), P(), P()),
        out_specs=tiles,
        check_vma=False,
    )
```

profile of v0, /device:TPU:1, one launch (start us, length us, event | category | flops | bytes accessed | tf_op | source)
XLA Modules:
  0.0 145.7 jit_solution(8352231563480037896)
XLA Ops:
  0.0 1.3 copy-done.3
  2.0 2.4 %shard_map.64 = (bf16[512,768]{1,0:T(8,128)(2,1)S(1)}, bf16[32,768]{1,0:T(8,128)(2,1)}, bf16[16,768]{1,0:T(8,128)(2,1)}, bf16[1,768]{1,0:T(2,128)(2,1)S(1)}) custom-call(bf16[32,16,768]{2,1,0:T(8,128)(2,1)S(1)} %copy-done.3, f32[768]{0:T(1024)S(1)} %copy-done.6), custom_call_target="tpu_custom_call" | custom-call | flops 4000000000 | bytes 1000000 | tf_op jit(solution)/shard_map/pallas_call | solution.py:91
  4.4 0.9 copy-done.7
  5.2 4.6 %collective-permute-start.1 = (bf16[32,768]{1,0:T(8,128)(2,1)}, bf16[32,768]{1,0:T(8,128)(2,1)}, u32[]{:S(2)}, u32[]{:S(2)}) collective-permute-start(bf16[32,768]{1,0:T(8,128)(2,1)} %get-tuple-element.37), channel_id=1, source_target_pairs={{0,1},{1,2},{2,3},{3,4},{4,5},{5,6},{6,7},{7,8},{8,9},{9,10},{10,1... | collective-permute-start | bytes 147464 | tf_op jit(solution)/shard_map/ppermute | solution.py:36
  9.8 3.7 %collective-permute-start = (bf16[16,768]{1,0:T(8,128)(2,1)}, bf16[16,768]{1,0:T(8,128)(2,1)}, u32[]{:S(2)}, u32[]{:S(2)}) collective-permute-start(bf16[16,768]{1,0:T(8,128)(2,1)} %get-tuple-element.36), channel_id=1, source_target_pairs={{0,16},{16,32},{32,48},{48,64},{64,80},{80,96},{96,112},{112,128},... | collective-permute-start | bytes 73736 | tf_op jit(solution)/shard_map/ppermute | solution.py:36
  13.6 2.9 %collective-permute-start.2 = (bf16[1,768]{1,0:T(2,128)(2,1)S(1)}, bf16[1,768]{1,0:T(2,128)(2,1)S(1)}, u32[]{:S(2)}, u32[]{:S(2)}) collective-permute-start(bf16[1,768]{1,0:T(2,128)(2,1)S(1)} %get-tuple-element.38), channel_id=1, source_target_pairs={{0,17},{1,18},{2,19},{3,20},{4,21},{5,22},{6,23},{7,24},{8,25},{9,... | collective-permute-start | bytes 4616 | tf_op jit(solution)/shard_map/ppermute | solution.py:42
  17.2 1.2 copy-done.4
  18.5 1.1 copy-done.8
  19.6 2.3 %shard_map.66 = (bf16[32,384]{1,0:T(8,128)(2,1)S(1)}, bf16[32,384]{1,0:T(8,128)(2,1)S(1)}, bf16[32,384]{1,0:T(8,128)(2,1)S(1)}, bf16[32,384]{1,0:T(8,128)(2,1)S(1)}) custom-call(s32[1]{0:T(128)} %bitcast.here_ref, bf16[512,768]{1,0:T(8,128)(2,1)S(1)} %copy-done.8, bf16[16,768]{1,0:T(8,128)(2,1)} %collective-permute-done.upper_ref, ...), custom_call_target="tpu_custom_call" | custom-call | flops 1500000000 | bytes 4000000 | tf_op jit(solution)/shard_map/pallas_call | solution.py:170
  21.9 1.4 collective-permute-start.3
  23.3 2.8 %collective-permute-start.4 = (bf16[32,384]{1,0:T(8,128)(2,1)S(1)}, bf16[32,384]{1,0:T(8,128)(2,1)S(1)}, u32[]{:S(2)}, u32[]{:S(2)}) collective-permute-start(bf16[32,384]{1,0:T(8,128)(2,1)S(1)} %get-tuple-element.41), channel_id=1, source_target_pairs={{0,4},{2,6},{4,0},{6,2},{1,5},{3,7},{5,1},{7,3},{8,12},{10,14},{12... | collective-permute-start | bytes 73736 | tf_op jit(solution)/shard_map/ppermute | solution.py:25
  26.7 0.9 collective-permute-done.4
  27.6 1.7 %collective-permute-done.5 = bf16[32,384]{1,0:T(8,128)(2,1)S(1)} collective-permute-done((bf16[32,384]{1,0:T(8,128)(2,1)S(1)}, bf16[32,384]{1,0:T(8,128)(2,1)S(1)}, u32[]{:S(2)}, u32[]{:S(2)}) %collective-permute-start.5) | collective-permute-done | bytes 24608 | tf_op jit(solution)/shard_map/ppermute | solution.py:25
  29.4 8.9 %collective-permute-start.6 = (bf16[128,384]{1,0:T(8,128)(2,1)S(1)}, bf16[128,384]{1,0:T(8,128)(2,1)S(1)}, u32[]{:S(2)}, u32[]{:S(2)}) collective-permute-start(bf16[128,384]{1,0:T(8,128)(2,1)S(1)} %get-tuple-element.65), channel_id=1, source_target_pairs={{0,128},{64,192},{128,0},{192,64},{1,129},{65,193},{129,1},{193,65... | collective-permute-start | bytes 294920 | tf_op jit(solution)/shard_map/ppermute | solution.py:25
  38.3 2.8 %shard_map.65 = bf16[8,192,128]{2,1,0:T(8,128)(2,1)} custom-call(bf16[512,768]{1,0:T(8,128)(2,1)S(1)} %copy-done.8, bf16[16,768]{1,0:T(8,128)(2,1)} %collective-permute-done.upper_ref, bf16[32,768]{1,0:T(8,128)(2,1)} %collective-permute-done.1.left_ref, bf16[1,768]{1,0:T(2,128)(2,1)S(1)} %collective-permute-done.2.corner_ref, ...), custom_call_target="tpu_custom_call" | custom-call | flops 1500000000 | bytes 4000000 | tf_op jit(solution)/shard_map/pallas_call | solution.py:170
  41.0 3.5 %all-to-all-start = ((bf16[8,192,128]{2,1,0:T(8,128)(2,1)}), bf16[8,192,128]{2,1,0:T(8,128)(2,1)S(1)}, u32[]{:S(2)}, u32[]{:S(2)}) async-start(bf16[8,192,128]{2,1,0:T(8,128)(2,1)} %shard_map.65), calls=%async_computation | async-start | bytes 786432 | tf_op jit(solution)/shard_map/all_to_all | solution.py:356
  44.6 2.4 %collective-permute-start.7 = (bf16[128,384]{1,0:T(8,128)(2,1)S(1)}, bf16[128,384]{1,0:T(8,128)(2,1)S(1)}, u32[]{:S(2)}, u32[]{:S(2)}) collective-permute-start(bf16[128,384]{1,0:T(8,128)(2,1)S(1)} %get-tuple-element.65), channel_id=1, source_target_pairs={{0,64},{64,128},{128,192},{192,0},{1,65},{65,129},{129,193},{193,1... | collective-permute-start | bytes 294920 | tf_op jit(solution)/shard_map/ppermute | solution.py:25
  47.0 5.6 %collective-permute-done.7 = bf16[128,384]{1,0:T(8,128)(2,1)S(1)} collective-permute-done((bf16[128,384]{1,0:T(8,128)(2,1)S(1)}, bf16[128,384]{1,0:T(8,128)(2,1)S(1)}, u32[]{:S(2)}, u32[]{:S(2)}) %collective-permute-start.7) | collective-permute-done | bytes 98336 | tf_op jit(solution)/shard_map/ppermute | solution.py:25
  52.6 2.7 %collective-permute-start.11 = (bf16[512,384]{1,0:T(8,128)(2,1)S(1)}, bf16[512,384]{1,0:T(8,128)(2,1)S(1)}, u32[]{:S(2)}, u32[]{:S(2)}) collective-permute-start(bf16[512,384]{1,0:T(8,128)(2,1)S(1)} %constant_dynamic-update-slice_fusion.4.refs_0_), channel_id=1, source_target_pairs={{0,1},{1,0},{2,3},{3,2},{4,5},{5,4},{6,7},{7,6},{8,9},{9,8},{10,11... | collective-permute-start | bytes 1179656 | tf_op jit(solution)/shard_map/ppermute | solution.py:25
  55.3 2.8 %collective-permute-start.10 = (bf16[512,384]{1,0:T(8,128)(2,1)S(1)}, bf16[512,384]{1,0:T(8,128)(2,1)S(1)}, u32[]{:S(2)}, u32[]{:S(2)}) collective-permute-start(bf16[512,384]{1,0:T(8,128)(2,1)S(1)} %constant_dynamic-update-slice_fusion.4.refs_0_), channel_id=1, source_target_pairs={{0,24},{16,0},{8,16},{24,8},{1,25},{17,1},{9,17},{25,9},{2,26},{18... | collective-permute-start | bytes 1179656 | tf_op jit(solution)/shard_map/ppermute | solution.py:31
  58.1 3.3 %shard_map.67 = (f32[16,1024]{1,0:T(8,128)S(1)}, f32[192,1024]{1,0:T(8,128)S(1)}) custom-call(bf16[8,192,128]{2,1,0:T(8,128)(2,1)S(1)} %all-to-all-done.q_ref, bf16[512,384]{1,0:T(8,128)(2,1)S(1)} %constant_dynamic-update-slice_fusion.4.refs_0_), custom_call_target="tpu_custom_call" | custom-call | flops 1572864 | bytes 1024 | tf_op jit(solution)/shard_map/pallas_call | solution.py:299
  61.4 9.3 %shard_map.68 = (f32[16,1024]{1,0:T(8,128)S(1)}, f32[192,1024]{1,0:T(8,128)S(1)}) custom-call(bf16[8,192,128]{2,1,0:T(8,128)(2,1)S(1)} %all-to-all-done.q_ref, bf16[512,384]{1,0:T(8,128)(2,1)S(1)} %collective-permute-done.11.refs_0_, f32[16,1024]{1,0:T(8,128)S(1)} %get-tuple-element.43.refs_1_, f32[192,1024]{1,0:T(8,128)S(1)} %get-tuple-element.44.refs_2_), custom_call_target="tpu_custom_call" | custom-call | flops 1572864 | bytes 1024 | tf_op jit(solution)/shard_map/pallas_call | solution.py:299
  71.4 3.0 %collective-permute-start.13 = (bf16[256,384]{1,0:T(8,128)(2,1)S(1)}, bf16[256,384]{1,0:T(8,128)(2,1)S(1)}, u32[]{:S(2)}, u32[]{:S(2)}) collective-permute-start(bf16[256,384]{1,0:T(8,128)(2,1)S(1)} %slice.7), channel_id=1, source_target_pairs={{0,24},{16,0},{8,16},{24,8},{1,25},{17,1},{9,17},{25,9},{2,26},{18... | collective-permute-start | bytes 589832 | tf_op jit(solution)/shard_map/ppermute | solution.py:31
  74.3 9.3 %shard_map.69 = (f32[16,1024]{1,0:T(8,128)S(1)}, f32[192,1024]{1,0:T(8,128)S(1)}) custom-call(bf16[8,192,128]{2,1,0:T(8,128)(2,1)S(1)} %all-to-all-done.q_ref, bf16[512,384]{1,0:T(8,128)(2,1)S(1)} %collective-permute-done.9.refs_0_, f32[16,1024]{1,0:T(8,128)S(1)} %get-tuple-element.49.refs_1_, f32[192,1024]{1,0:T(8,128)S(1)} %get-tuple-element.50.refs_2_), custom_call_target="tpu_custom_call" | custom-call | flops 1572864 | bytes 1024 | tf_op jit(solution)/shard_map/pallas_call | solution.py:299
  83.6 9.3 %shard_map.70 = (f32[16,1024]{1,0:T(8,128)S(1)}, f32[192,1024]{1,0:T(8,128)S(1)}) custom-call(bf16[8,192,128]{2,1,0:T(8,128)(2,1)S(1)} %all-to-all-done.q_ref, bf16[512,384]{1,0:T(8,128)(2,1)S(1)} %collective-permute-done.15.refs_0_, f32[16,1024]{1,0:T(8,128)S(1)} %get-tuple-element.51.refs_1_, f32[192,1024]{1,0:T(8,128)S(1)} %get-tuple-element.52.refs_2_), custom_call_target="tpu_custom_call" | custom-call | flops 1572864 | bytes 1024 | tf_op jit(solution)/shard_map/pallas_call | solution.py:299
  92.9 9.5 %shard_map.71 = (f32[16,1024]{1,0:T(8,128)S(1)}, f32[192,1024]{1,0:T(8,128)S(1)}) custom-call(bf16[8,192,128]{2,1,0:T(8,128)(2,1)S(1)} %all-to-all-done.q_ref, bf16[512,384]{1,0:T(8,128)(2,1)S(1)} %collective-permute-done.10.refs_0_, f32[16,1024]{1,0:T(8,128)S(1)} %get-tuple-element.53.refs_1_, f32[192,1024]{1,0:T(8,128)S(1)} %get-tuple-element.54.refs_2_), custom_call_target="tpu_custom_call" | custom-call | flops 1572864 | bytes 1024 | tf_op jit(solution)/shard_map/pallas_call | solution.py:299
  102.4 9.3 %shard_map.72 = (f32[16,1024]{1,0:T(8,128)S(1)}, f32[192,1024]{1,0:T(8,128)S(1)}) custom-call(bf16[8,192,128]{2,1,0:T(8,128)(2,1)S(1)} %all-to-all-done.q_ref, bf16[512,384]{1,0:T(8,128)(2,1)S(1)} %collective-permute-done.14.refs_0_, f32[16,1024]{1,0:T(8,128)S(1)} %get-tuple-element.55.refs_1_, f32[192,1024]{1,0:T(8,128)S(1)} %get-tuple-element.56.refs_2_), custom_call_target="tpu_custom_call" | custom-call | flops 1572864 | bytes 1024 | tf_op jit(solution)/shard_map/pallas_call | solution.py:299
  111.7 0.8 collective-permute-start.16
  112.6 9.3 %shard_map.73 = (f32[16,1024]{1,0:T(8,128)S(1)}, f32[192,1024]{1,0:T(8,128)S(1)}) custom-call(bf16[8,192,128]{2,1,0:T(8,128)(2,1)S(1)} %all-to-all-done.q_ref, bf16[256,384]{1,0:T(8,128)(2,1)S(1)} %collective-permute-done.12.refs_0_, bf16[256,384]{1,0:T(8,128)(2,1)S(1)} %collective-permute-done.13.refs_1_, f32[16,1024]{1,0:T(8,128)S(1)} %get-tuple-element.61.refs_2_, ...), custom_call_target="tpu_custom_call" | custom-call | flops 1572864 | bytes 1024 | tf_op jit(solution)/shard_map/pallas_call | solution.py:299
  121.9 9.3 %shard_map.74 = bf16[8,208,128]{2,1,0:T(8,128)(2,1)S(1)} custom-call(bf16[8,192,128]{2,1,0:T(8,128)(2,1)S(1)} %all-to-all-done.q_ref, bf16[256,384]{1,0:T(8,128)(2,1)S(1)} %collective-permute-done.16.refs_0_, bf16[256,384]{1,0:T(8,128)(2,1)S(1)} %collective-permute-done.17.refs_1_, f32[16,1024]{1,0:T(8,128)S(1)} %get-tuple-element.63.refs_2_, ...), custom_call_target="tpu_custom_call" | custom-call | flops 1572864 | bytes 1024 | tf_op jit(solution)/shard_map/pallas_call | solution.py:299
  131.2 13.4 %all_to_all.10.parts_ref = bf16[8,208,128]{2,1,0:T(8,128)(2,1)S(1)} all-to-all(bf16[8,208,128]{2,1,0:T(8,128)(2,1)S(1)} %shard_map.74), channel_id=1, replica_groups=mesh['zq'=4,'zc'=2,'xl'=2,'xh'=2,'y'=4,'core'=2] {'zc','y'}, dimensions={0} | all-to-all | bytes 851968 | tf_op jit(solution)/shard_map/all_to_all | solution.py:373
  144.6 1.2 shard_map.75
  (46 shorter events, 3.0 us)
Async XLA Ops:
  0.0 17.2 %copy-start.1 = (bf16[768,2304]{1,0:T(8,128)(2,1)S(1)}, bf16[768,2304]{1,0:T(8,128)(2,1)}, u32[]{:S(2)}) copy-start(bf16[768,2304]{1,0:T(8,128)(2,1)} %w_ref.4) | copy-start | bytes 10616836
  0.0 1.3 copy-start.3
  1.3 0.7 copy-start.6
  4.4 0.9 copy-start.7
  5.2 12.0 %collective-permute-start.1 = (bf16[32,768]{1,0:T(8,128)(2,1)}, bf16[32,768]{1,0:T(8,128)(2,1)}, u32[]{:S(2)}, u32[]{:S(2)}) collective-permute-start(bf16[32,768]{1,0:T(8,128)(2,1)} %get-tuple-element.37), channel_id=1, source_target_pairs={{0,1},{1,2},{2,3},{3,4},{4,5},{5,6},{6,7},{7,8},{8,9},{9,10},{10,1... | collective-permute-start | bytes 147464 | tf_op jit(solution)/shard_map/ppermute | solution.py:36
  9.8 7.4 %collective-permute-start = (bf16[16,768]{1,0:T(8,128)(2,1)}, bf16[16,768]{1,0:T(8,128)(2,1)}, u32[]{:S(2)}, u32[]{:S(2)}) collective-permute-start(bf16[16,768]{1,0:T(8,128)(2,1)} %get-tuple-element.36), channel_id=1, source_target_pairs={{0,16},{16,32},{32,48},{48,64},{64,80},{80,96},{96,112},{112,128},... | collective-permute-start | bytes 73736 | tf_op jit(solution)/shard_map/ppermute | solution.py:36
  13.6 3.7 %collective-permute-start.2 = (bf16[1,768]{1,0:T(2,128)(2,1)S(1)}, bf16[1,768]{1,0:T(2,128)(2,1)S(1)}, u32[]{:S(2)}, u32[]{:S(2)}) collective-permute-start(bf16[1,768]{1,0:T(2,128)(2,1)S(1)} %get-tuple-element.38), channel_id=1, source_target_pairs={{0,17},{1,18},{2,19},{3,20},{4,21},{5,22},{6,23},{7,24},{8,25},{9,... | collective-permute-start | bytes 4616 | tf_op jit(solution)/shard_map/ppermute | solution.py:42
  16.5 21.8 %copy-start.2 = (bf16[768,2304]{1,0:T(8,128)(2,1)S(1)}, bf16[768,2304]{1,0:T(8,128)(2,1)}, u32[]{:S(2)}) copy-start(bf16[768,2304]{1,0:T(8,128)(2,1)} %w_ref.4) | copy-start | bytes 10616836
  17.2 1.2 copy-start.4
  18.5 1.1 copy-start.8
  19.6 18.7 %copy-start.5 = (f32[9,768]{1,0:T(8,128)S(1)}, f32[9,768]{1,0:T(8,128)}, u32[]{:S(2)}) copy-start(f32[9,768]{1,0:T(8,128)} %pool_ref.2) | copy-start | bytes 82948
  21.9 4.8 %collective-permute-start.3 = (bf16[32,384]{1,0:T(8,128)(2,1)S(1)}, bf16[32,384]{1,0:T(8,128)(2,1)S(1)}, u32[]{:S(2)}, u32[]{:S(2)}) collective-permute-start(bf16[32,384]{1,0:T(8,128)(2,1)S(1)} %get-tuple-element.40), channel_id=1, source_target_pairs={{0,2},{2,4},{4,6},{6,0},{1,3},{3,5},{5,7},{7,1},{8,10},{10,12},{12... | collective-permute-start | bytes 73736 | tf_op jit(solution)/shard_map/ppermute | solution.py:25
  23.3 4.3 %collective-permute-start.4 = (bf16[32,384]{1,0:T(8,128)(2,1)S(1)}, bf16[32,384]{1,0:T(8,128)(2,1)S(1)}, u32[]{:S(2)}, u32[]{:S(2)}) collective-permute-start(bf16[32,384]{1,0:T(8,128)(2,1)S(1)} %get-tuple-element.41), channel_id=1, source_target_pairs={{0,4},{2,6},{4,0},{6,2},{1,5},{3,7},{5,1},{7,3},{8,12},{10,14},{12... | collective-permute-start | bytes 73736 | tf_op jit(solution)/shard_map/ppermute | solution.py:25
  26.1 3.2 %collective-permute-start.5 = (bf16[32,384]{1,0:T(8,128)(2,1)S(1)}, bf16[32,384]{1,0:T(8,128)(2,1)S(1)}, u32[]{:S(2)}, u32[]{:S(2)}) collective-permute-start(bf16[32,384]{1,0:T(8,128)(2,1)S(1)} %get-tuple-element.42), channel_id=1, source_target_pairs={{0,6},{2,0},{4,2},{6,4},{1,7},{3,1},{5,3},{7,5},{8,14},{10,8},{12,... | collective-permute-start | bytes 73736 | tf_op jit(solution)/shard_map/ppermute | solution.py:25
  29.4 17.6 %collective-permute-start.6 = (bf16[128,384]{1,0:T(8,128)(2,1)S(1)}, bf16[128,384]{1,0:T(8,128)(2,1)S(1)}, u32[]{:S(2)}, u32[]{:S(2)}) collective-permute-start(bf16[128,384]{1,0:T(8,128)(2,1)S(1)} %get-tuple-element.65), channel_id=1, source_target_pairs={{0,128},{64,192},{128,0},{192,64},{1,129},{65,193},{129,1},{193,65... | collective-permute-start | bytes 294920 | tf_op jit(solution)/shard_map/ppermute | solution.py:25
  41.0 17.1 %all-to-all-start = ((bf16[8,192,128]{2,1,0:T(8,128)(2,1)}), bf16[8,192,128]{2,1,0:T(8,128)(2,1)S(1)}, u32[]{:S(2)}, u32[]{:S(2)}) async-start(bf16[8,192,128]{2,1,0:T(8,128)(2,1)} %shard_map.65), calls=%async_computation | async-start | bytes 786432 | tf_op jit(solution)/shard_map/all_to_all | solution.py:356
  44.5 8.1 %collective-permute-start.8 = (bf16[128,384]{1,0:T(8,128)(2,1)S(1)}, bf16[128,384]{1,0:T(8,128)(2,1)S(1)}, u32[]{:S(2)}, u32[]{:S(2)}) collective-permute-start(bf16[128,384]{1,0:T(8,128)(2,1)S(1)} %get-tuple-element.65), channel_id=1, source_target_pairs={{0,192},{64,0},{128,64},{192,128},{1,193},{65,1},{129,65},{193,129... | collective-permute-start | bytes 294920 | tf_op jit(solution)/shard_map/ppermute | solution.py:25
  44.6 8.0 %collective-permute-start.7 = (bf16[128,384]{1,0:T(8,128)(2,1)S(1)}, bf16[128,384]{1,0:T(8,128)(2,1)S(1)}, u32[]{:S(2)}, u32[]{:S(2)}) collective-permute-start(bf16[128,384]{1,0:T(8,128)(2,1)S(1)} %get-tuple-element.65), channel_id=1, source_target_pairs={{0,64},{64,128},{128,192},{192,0},{1,65},{65,129},{129,193},{193,1... | collective-permute-start | bytes 294920 | tf_op jit(solution)/shard_map/ppermute | solution.py:25
  52.6 8.8 %collective-permute-start.11 = (bf16[512,384]{1,0:T(8,128)(2,1)S(1)}, bf16[512,384]{1,0:T(8,128)(2,1)S(1)}, u32[]{:S(2)}, u32[]{:S(2)}) collective-permute-start(bf16[512,384]{1,0:T(8,128)(2,1)S(1)} %constant_dynamic-update-slice_fusion.4.refs_0_), channel_id=1, source_target_pairs={{0,1},{1,0},{2,3},{3,2},{4,5},{5,4},{6,7},{7,6},{8,9},{9,8},{10,11... | collective-permute-start | bytes 1179656 | tf_op jit(solution)/shard_map/ppermute | solution.py:25
  55.3 15.4 %collective-permute-start.10 = (bf16[512,384]{1,0:T(8,128)(2,1)S(1)}, bf16[512,384]{1,0:T(8,128)(2,1)S(1)}, u32[]{:S(2)}, u32[]{:S(2)}) collective-permute-start(bf16[512,384]{1,0:T(8,128)(2,1)S(1)} %constant_dynamic-update-slice_fusion.4.refs_0_), channel_id=1, source_target_pairs={{0,24},{16,0},{8,16},{24,8},{1,25},{17,1},{9,17},{25,9},{2,26},{18... | collective-permute-start | bytes 1179656 | tf_op jit(solution)/shard_map/ppermute | solution.py:31
  58.1 12.6 %collective-permute-start.9 = (bf16[512,384]{1,0:T(8,128)(2,1)S(1)}, bf16[512,384]{1,0:T(8,128)(2,1)S(1)}, u32[]{:S(2)}, u32[]{:S(2)}) collective-permute-start(bf16[512,384]{1,0:T(8,128)(2,1)S(1)} %constant_dynamic-update-slice_fusion.4.refs_0_), channel_id=1, source_target_pairs={{0,16},{16,8},{8,24},{24,0},{1,17},{17,9},{9,25},{25,1},{2,18},{18... | collective-permute-start | bytes 1179656 | tf_op jit(solution)/shard_map/ppermute | solution.py:31
  70.7 12.9 %collective-permute-start.15 = (bf16[512,384]{1,0:T(8,128)(2,1)S(1)}, bf16[512,384]{1,0:T(8,128)(2,1)S(1)}, u32[]{:S(2)}, u32[]{:S(2)}) collective-permute-start(bf16[512,384]{1,0:T(8,128)(2,1)S(1)} %collective-permute-done.9.refs_0_), channel_id=1, source_target_pairs={{0,1},{1,0},{2,3},{3,2},{4,5},{5,4},{6,7},{7,6},{8,9},{9,8},{10,11... | collective-permute-start | bytes 1179656 | tf_op jit(solution)/shard_map/ppermute | solution.py:25
  71.2 31.2 %collective-permute-start.14 = (bf16[512,384]{1,0:T(8,128)(2,1)S(1)}, bf16[512,384]{1,0:T(8,128)(2,1)S(1)}, u32[]{:S(2)}, u32[]{:S(2)}) collective-permute-start(bf16[512,384]{1,0:T(8,128)(2,1)S(1)} %collective-permute-done.10.refs_0_), channel_id=1, source_target_pairs={{0,1},{1,0},{2,3},{3,2},{4,5},{5,4},{6,7},{7,6},{8,9},{9,8},{10,11... | collective-permute-start | bytes 1179656 | tf_op jit(solution)/shard_map/ppermute | solution.py:25
  71.4 40.3 %collective-permute-start.13 = (bf16[256,384]{1,0:T(8,128)(2,1)S(1)}, bf16[256,384]{1,0:T(8,128)(2,1)S(1)}, u32[]{:S(2)}, u32[]{:S(2)}) collective-permute-start(bf16[256,384]{1,0:T(8,128)(2,1)S(1)} %slice.7), channel_id=1, source_target_pairs={{0,24},{16,0},{8,16},{24,8},{1,25},{17,1},{9,17},{25,9},{2,26},{18... | collective-permute-start | bytes 589832 | tf_op jit(solution)/shard_map/ppermute | solution.py:31
  74.3 37.4 %collective-permute-start.12 = (bf16[256,384]{1,0:T(8,128)(2,1)S(1)}, bf16[256,384]{1,0:T(8,128)(2,1)S(1)}, u32[]{:S(2)}, u32[]{:S(2)}) collective-permute-start(bf16[256,384]{1,0:T(8,128)(2,1)S(1)} %slice.6), channel_id=1, source_target_pairs={{0,16},{16,8},{8,24},{24,0},{1,17},{17,9},{9,25},{25,1},{2,18},{18... | collective-permute-start | bytes 589832 | tf_op jit(solution)/shard_map/ppermute | solution.py:31
  92.9 51.7 %copy-start = (bf16[768,768]{1,0:T(8,128)(2,1)S(1)}, bf16[768,768]{1,0:T(8,128)(2,1)}, u32[]{:S(2)}) copy-start(bf16[768,768]{1,0:T(8,128)(2,1)} %w_ref.5) | copy-start | bytes 3538948
  111.7 10.2 %collective-permute-start.16 = (bf16[256,384]{1,0:T(8,128)(2,1)S(1)}, bf16[256,384]{1,0:T(8,128)(2,1)S(1)}, u32[]{:S(2)}, u32[]{:S(2)}) collective-permute-start(bf16[256,384]{1,0:T(8,128)(2,1)S(1)} %collective-permute-done.12.refs_0_), channel_id=1, source_target_pairs={{0,1},{1,0},{2,3},{3,2},{4,5},{5,4},{6,7},{7,6},{8,9},{9,8},{10,11... | collective-permute-start | bytes 589832 | tf_op jit(solution)/shard_map/ppermute | solution.py:25
  112.5 9.4 %collective-permute-start.17 = (bf16[256,384]{1,0:T(8,128)(2,1)S(1)}, bf16[256,384]{1,0:T(8,128)(2,1)S(1)}, u32[]{:S(2)}, u32[]{:S(2)}) collective-permute-start(bf16[256,384]{1,0:T(8,128)(2,1)S(1)} %collective-permute-done.13.refs_1_), channel_id=1, source_target_pairs={{0,1},{1,0},{2,3},{3,2},{4,5},{5,4},{6,7},{7,6},{8,9},{9,8},{10,11... | collective-permute-start | bytes 589832 | tf_op jit(solution)/shard_map/ppermute | solution.py:25
where the time goes:
time: 147 us; the launch traced here: 146 us
  Pallas kernels  77.1 us (52%)
  starting transfers between devices  40.7 us (28%)
  blocking collectives  13.4 us (9%)
  waiting for transfers between devices  8.96 us (6%)
  local copies, waits for them, and re-layouts  5.38 us (4%)
    pallas_call x8, Pallas kernels, attend(): pl.pallas_call(functools.partial(attend_kernel, not carry, last, qb, len(...  68.5 us
    ppermute x11, starting transfers between devices, shifted(): lax.ppermute(block, axis, [(i, (i + distance) % count) for i in range(cou...  20.3 us
    all_to_all x1, blocking collectives, on_device(): parts = lax.all_to_all(partial, ('zc', 'y'), 0, 0, tiled=True)  13.4 us
    ppermute x2, starting transfers between devices, passed_along(): return lax.ppermute(block, axis, [(i - 1, i) for i in range(1, count)])  8.31 us
    ppermute x11, waiting for transfers between devices, shifted(): lax.ppermute(block, axis, [(i, (i + distance) % count) for i in range(cou...  8.23 us
    ppermute x4, starting transfers between devices, shifted_x(): return lax.ppermute(block, ('xl', 'xh'), route)  5.73 us
    unnamed x23, local copies, waits for them, and re-layouts  5.31 us
    pallas_call x2, Pallas kernels, pool_call(): pl.pallas_call(kernel, in_specs=[pl.BlockSpec(memory_space=pltpu.SMEM)] *...  5.08 us
  transfers between devices with their start and end apart: 19, of which 4 were waited for; matrix products, arithmetic and copies ran while one was open for 0% of the time, Pallas kernels for 42%

commit v1 on v0

--- a/solution.py
+++ b/solution.py
@@ -99,6 +99,28 @@
     )(patches, gain)
 
 
+def own_kernel(tokens_ref, w_ref, q_ref, kv_ref):
+    width = tokens_ref.shape[1]
+    few = kv_ref.shape[0]
+    for part in range(2):
+        cols = slice(part * width, (part + 1) * width)
+        kv_ref[:, cols] = project(tokens_ref[:few], w_ref[:, (part + 1) * width : (part + 2) * width])
+    q_ref[...] = project(tokens_ref[...], w_ref[:, :width])
+
+
+def project_own(tokens, w_qkv):
+    count, width = tokens.shape
+    shapes = [(count, width), (32 * KEY_COLUMNS, 2 * width)]
+    return pl.pallas_call(
+        own_kernel,
+        in_specs=[pl.BlockSpec(memory_space=pltpu.VMEM)] * 2,
+        out_specs=[pl.BlockSpec(memory_space=pltpu.VMEM)] * 2,
+        out_shape=[jax.ShapeDtypeStruct(s, bf16) for s in shapes],
+        compiler_params=pltpu.CompilerParams(vmem_limit_bytes=16 * 2**20),
+        cost_estimate=pl.CostEstimate(flops=1_500_000_000, bytes_accessed=4_000_000, transcendentals=0),
+    )(tokens, w_qkv)
+
+
 def halo_tokens(upper_ref, left_ref, corner_ref):
     rest = jnp.zeros((15, left_ref.shape[1]), f32)
     every = [left_ref[...].astype(f32), upper_ref[...].astype(f32), corner_ref[...].astype(f32), rest]
@@ -128,33 +150,31 @@
     return total
 
 
-def keyvals_kernel(here_ref, tokens_ref, upper_ref, left_ref, corner_ref, w_ref, pool_ref, *refs):
-    out_refs, parts = refs[:-1], refs[-1]
+def keyvals_kernel(own_ref, upper_ref, left_ref, corner_ref, w_ref, pool_ref, out_ref):
     halo_in = halo_tokens(upper_ref, left_ref, corner_ref)
-    width = tokens_ref.shape[1]
+    width = own_ref.shape[1] // 2
     both = []
     for part in range(2):
         cols = pl.ds(part * width, width)
         weights = w_ref[:, (part + 1) * width : (part + 2) * width]
         halo = project(halo_in, weights).astype(f32)
-        own = project(tokens_ref[: 32 * KEY_COLUMNS], weights)
+        own = own_ref[:, part * width : (part + 1) * width]
         taps = [pool_ref[t : t + 1, cols] for t in range(9)]
         groups = columns_of(own, halo, (-1,) + ORDER[:KEY_COLUMNS])
         both.append(jnp.concatenate([pooled(groups, taps, 4 * j, 0) for j in range(4)], 0))
     count = width // WIDE
     for g in range(count):
         lanes = slice(g * WIDE, (g + 1) * WIDE)
-        parts[g] = jnp.concatenate([p[:, lanes] for p in both], 1).astype(bf16)
-    here = here_ref[0]
-    for distance, out_ref in enumerate(out_refs):
-        out_ref[...] = parts[lax.rem(here + distance, count)]
-
-
-def queries_kernel(tokens_ref, upper_ref, left_ref, corner_ref, w_ref, pool_ref, out_ref):
-    width = tokens_ref.shape[1]
+        block = jnp.concatenate([p[:, lanes] for p in both], 1).astype(bf16)
+        for copy in range(out_ref.shape[0] // count):
+            out_ref[copy * count + g] = block
+
+
+def queries_kernel(own_ref, upper_ref, left_ref, corner_ref, w_ref, pool_ref, out_ref):
+    width = own_ref.shape[1]
     weights = w_ref[:, :width]
     halo = project(halo_tokens(upper_ref, left_ref, corner_ref), weights).astype(f32)
-    own = project(tokens_ref[...], weights)
+    own = own_ref[...]
     taps = [pool_ref[t : t + 1, :] for t in range(9)]
     groups = columns_of(own, halo, range(-1, 16))
     rows = [pooled(groups, taps, 2 * j, 2 * p) for j in range(8) for p in range(2)]
@@ -166,17 +186,15 @@
             out_ref[copy * count + g] = block
 
 
-def pool_call(kernel, tokens, halo, w_qkv, taps, out_shapes, scratch=(), scalars=()):
+def pool_call(kernel, own, halo, w_qkv, taps, out_shape):
     return pl.pallas_call(
         kernel,
-        in_specs=[pl.BlockSpec(memory_space=pltpu.SMEM)] * len(scalars)
-        + [pl.BlockSpec(memory_space=pltpu.VMEM)] * (3 + len(halo)),
-        out_specs=[pl.BlockSpec(memory_space=pltpu.VMEM)] * len(out_shapes),
-        out_shape=[jax.ShapeDtypeStruct(s, bf16) for s in out_shapes],
-        scratch_shapes=[pltpu.VMEM(s, bf16) for s in scratch],
+        in_specs=[pl.BlockSpec(memory_space=pltpu.VMEM)] * (3 + len(halo)),
+        out_specs=pl.BlockSpec(memory_space=pltpu.VMEM),
+        out_shape=jax.ShapeDtypeStruct(out_shape, bf16),
         compiler_params=pltpu.CompilerParams(vmem_limit_bytes=24 * 2**20),
-        cost_estimate=pl.CostEstimate(flops=1_500_000_000, bytes_accessed=4_000_000, transcendentals=0),
-    )(*scalars, tokens, *halo, w_qkv, taps)
+        cost_estimate=pl.CostEstimate(flops=200_000_000, bytes_accessed=4_000_000, transcendentals=0),
+    )(own, *halo, w_qkv, taps)
 
 
 def attend_kernel(first, last, qb, blocks, q_ref, *refs):
@@ -346,16 +364,15 @@
 def on_device(patches, norm_gain, w_qkv, pool_q, pool_kv, w_out):
     tokens, last_column, last_row, last_token = normalised_tokens(patches, norm_gain)
     halo = (passed_along(last_row, ROW), passed_along(last_column, COL), corner(last_token))
+    own_q, own_kv = project_own(tokens, w_qkv)
     groups = lax.axis_size("y")
-    part = (32, 2 * WIDE)
-    here = [lax.axis_index("y").reshape(1)]
-    parts = pool_call(keyvals_kernel, tokens, halo, w_qkv, pool_kv, [part] * groups, [(groups, *part)], here)
-    own = [parts[0]] + [shifted(part, "y", d) for d, part in enumerate(parts) if d]
-    own = jnp.concatenate(own, 0)
-    (turned,) = pool_call(queries_kernel, tokens, halo, w_qkv, pool_q, [(2 * groups, WIDE, 128)])
+    flat = pool_call(keyvals_kernel, own_kv, halo, w_qkv, pool_kv, (groups, 32, 2 * WIDE))
+    own = lax.all_to_all(flat, "y", 0, 0, tiled=True).reshape(-1, 2 * WIDE)
+    tie = lax.optimization_barrier
+    own, own_q = tie((own, own_q))
+    line = [own, shifted(own, "zq", 2), shifted(own, "zq", 1), shifted(own, "zq", -1)]
+    turned = pool_call(queries_kernel, own_q, halo, w_qkv, pool_q, (2 * groups, WIDE, 128))
     every_query = lax.all_to_all(turned, ("zc", "y"), 0, 0, tiled=True)
-    tie = lax.optimization_barrier
-    line = [own, shifted(own, "zq", 2), shifted(own, "zq", 1), shifted(own, "zq", -1)]
     line = jnp.concatenate(line, 0)
     after, before = shifted_x(line, 1), shifted_x(line, -1)
     swap = lambda block: shifted(block, "core", 1)

time: 147 us -> 137 us (0.932)
  waiting for transfers between devices: 8.96 us -> 1.72 us
  blocking collectives: 13.4 us -> 20.3 us
  starting transfers between devices: 40.7 us -> 36.2 us
  local copies, waits for them, and re-layouts: 5.38 us -> 2.12 us
  Pallas kernels: 77.1 us -> 75 us
    all_to_all x0 -> x1, blocking collectives: none -> 9.75 us  [on_device(): own = lax.all_to_all(flat, 'y', 0, 0, tiled=True).reshape(-1, 2 * WIDE)]
    ppermute x11 -> x8, starting transfers between devices: 20.3 us -> 12.7 us  [shifted(): lax.ppermute(block, axis, [(i, (i + distance) % count) for i in range(cou...]
    ppermute x11 -> x8, waiting for transfers between devices: 8.23 us -> 1.7 us  [shifted(): lax.ppermute(block, axis, [(i, (i + distance) % count) for i in range(cou...]
    unnamed x23 -> x15, local copies, waits for them, and re-layouts: 5.31 us -> 2.05 us
    ppermute x4, starting transfers between devices: 5.73 us -> 8.9 us  [shifted_x(): return lax.ppermute(block, ('xl', 'xh'), route)]
    all_to_all x1, blocking collectives: 13.4 us -> 10.5 us  [on_device(): parts = lax.all_to_all(partial, ('zc', 'y'), 0, 0, tiled=True)]
    ppermute x2, starting transfers between devices: 8.31 us -> 5.71 us  [passed_along(): return lax.ppermute(block, axis, [(i - 1, i) for i in range(1, count)])]
    ppermute x1, starting transfers between devices: 2.92 us -> 5.52 us  [corner(): return lax.ppermute(block, AXES, route)]
  transfers between devices with their start and end apart: 19 -> 16, of which waited for: 4 -> 1; matrix products, arithmetic and copies ran while one was open for 0% -> 0% of each run, Pallas kernels for 42% -> 46%
where the time goes in v1:
time: 137 us; the launch traced here: 136 us
  Pallas kernels  75 us (55%)
  starting transfers between devices  36.2 us (26%)
  blocking collectives  20.3 us (15%)
  local copies, waits for them, and re-layouts  2.12 us (2%)
  waiting for transfers between devices  1.72 us (1%)
    pallas_call x8, Pallas kernels, attend(): pl.pallas_call(functools.partial(attend_kernel, not carry, last, qb, len(...  68.4 us
    ppermute x8, starting transfers between devices, shifted(): lax.ppermute(block, axis, [(i, (i + distance) % count) for i in range(cou...  12.7 us
    all_to_all x1, blocking collectives, on_device(): parts = lax.all_to_all(partial, ('zc', 'y'), 0, 0, tiled=True)  10.5 us
    all_to_all x1, blocking collectives, on_device(): own = lax.all_to_all(flat, 'y', 0, 0, tiled=True).reshape(-1, 2 * WIDE)  9.75 us
    ppermute x4, starting transfers between devices, shifted_x(): return lax.ppermute(block, ('xl', 'xh'), route)  8.9 us
    ppermute x2, starting transfers between devices, passed_along(): return lax.ppermute(block, axis, [(i - 1, i) for i in range(1, count)])  5.71 us
    ppermute x1, starting transfers between devices, corner(): return lax.ppermute(block, AXES, route)  5.52 us
    all_to_all x1, starting transfers between devices, on_device(): every_query = lax.all_to_all(turned, ('zc', 'y'), 0, 0, tiled=True)  3.45 us
  transfers between devices with their start and end apart: 16, of which 1 were waited for; matrix products, arithmetic and copies ran while one was open for 0% of the time, Pallas kernels for 46%

profile of v1, /device:TPU:1, one launch (start us, length us, event | category | flops | bytes accessed | tf_op | source)
XLA Modules:
  0.0 135.7 jit_solution(882815249197822994)
XLA Ops:
  0.0 1.3 copy-done.4
  1.3 0.7 copy-done.5
  2.0 1.8 %shard_map.64 = (bf16[512,768]{1,0:T(8,128)(2,1)S(1)}, bf16[32,768]{1,0:T(8,128)(2,1)S(1)}, bf16[16,768]{1,0:T(8,128)(2,1)S(1)}, bf16[1,768]{1,0:T(2,128)(2,1)S(1)}) custom-call(bf16[32,16,768]{2,1,0:T(8,128)(2,1)S(1)} %copy-done.4, f32[768]{0:T(1024)S(1)} %copy-done.5), custom_call_target="tpu_custom_call" | custom-call | flops 4000000000 | bytes 1000000 | tf_op jit(solution)/shard_map/pallas_call | solution.py:91
  3.8 5.5 %collective-permute-start.2 = (bf16[1,768]{1,0:T(2,128)(2,1)S(1)}, bf16[1,768]{1,0:T(2,128)(2,1)S(1)}, u32[]{:S(2)}, u32[]{:S(2)}) collective-permute-start(bf16[1,768]{1,0:T(2,128)(2,1)S(1)} %get-tuple-element.39), channel_id=1, source_target_pairs={{0,17},{1,18},{2,19},{3,20},{4,21},{5,22},{6,23},{7,24},{8,25},{9,... | collective-permute-start | bytes 4616 | tf_op jit(solution)/shard_map/ppermute | solution.py:42
  9.3 3.5 %collective-permute-start = (bf16[16,768]{1,0:T(8,128)(2,1)S(1)}, bf16[16,768]{1,0:T(8,128)(2,1)S(1)}, u32[]{:S(2)}, u32[]{:S(2)}) collective-permute-start(bf16[16,768]{1,0:T(8,128)(2,1)S(1)} %get-tuple-element.37), channel_id=1, source_target_pairs={{0,16},{16,32},{32,48},{48,64},{64,80},{80,96},{96,112},{112,128},... | collective-permute-start | bytes 73736 | tf_op jit(solution)/shard_map/ppermute | solution.py:36
  12.8 2.2 %collective-permute-start.1 = (bf16[32,768]{1,0:T(8,128)(2,1)S(1)}, bf16[32,768]{1,0:T(8,128)(2,1)S(1)}, u32[]{:S(2)}, u32[]{:S(2)}) collective-permute-start(bf16[32,768]{1,0:T(8,128)(2,1)S(1)} %get-tuple-element.38), channel_id=1, source_target_pairs={{0,1},{1,2},{2,3},{3,4},{4,5},{5,6},{6,7},{7,8},{8,9},{9,10},{10,1... | collective-permute-start | bytes 147464 | tf_op jit(solution)/shard_map/ppermute | solution.py:36
  15.0 0.0 copy-start.2
  15.0 1.6 %shard_map.65 = (bf16[512,768]{1,0:T(8,128)(2,1)S(1)}, bf16[352,1536]{1,0:T(8,128)(2,1)S(1)}) custom-call(bf16[512,768]{1,0:T(8,128)(2,1)S(1)} %get-tuple-element.35.tokens_ref, bf16[768,2304]{1,0:T(8,128)(2,1)S(1)} %copy-done), custom_call_target="tpu_custom_call" | custom-call | flops 1500000000 | bytes 4000000 | tf_op jit(solution)/shard_map/pallas_call | solution.py:114
  16.7 0.7 shard_map.66
  17.4 9.8 %all_to_all.15 = bf16[4,32,384]{2,1,0:T(8,128)(2,1)S(1)} all-to-all(bf16[4,32,384]{2,1,0:T(8,128)(2,1)S(1)} %shard_map.66), channel_id=1, replica_groups=mesh['zq'=4,'zc'=2,'xl'=2,'xh'=2,'y'=4,'core'=2] {'y'}, dimensions={0} | all-to-all | bytes 196608 | tf_op jit(solution)/shard_map/all_to_all | solution.py:370
  27.2 5.1 %collective-permute-start.5 = (bf16[128,384]{1,0:T(8,128)(2,1)S(1)}, bf16[128,384]{1,0:T(8,128)(2,1)S(1)}, u32[]{:S(2)}, u32[]{:S(2)}) collective-permute-start(bf16[128,384]{1,0:T(8,128)(2,1)S(1)} %bitcast.1), channel_id=1, source_target_pairs={{0,192},{64,0},{128,64},{192,128},{1,193},{65,1},{129,65},{193,129... | collective-permute-start | bytes 294920 | tf_op jit(solution)/shard_map/ppermute | solution.py:25
  32.3 3.3 %collective-permute-start.3 = (bf16[128,384]{1,0:T(8,128)(2,1)S(1)}, bf16[128,384]{1,0:T(8,128)(2,1)S(1)}, u32[]{:S(2)}, u32[]{:S(2)}) collective-permute-start(bf16[128,384]{1,0:T(8,128)(2,1)S(1)} %bitcast.3), channel_id=1, source_target_pairs={{0,128},{64,192},{128,0},{192,64},{1,129},{65,193},{129,1},{193,65... | collective-permute-start | bytes 294920 | tf_op jit(solution)/shard_map/ppermute | solution.py:25
  35.6 1.4 %shard_map.67 = bf16[8,192,128]{2,1,0:T(8,128)(2,1)} custom-call(bf16[512,768]{1,0:T(8,128)(2,1)S(1)} %get-tuple-element.41.own_ref, bf16[16,768]{1,0:T(8,128)(2,1)S(1)} %collective-permute-done.upper_ref, bf16[32,768]{1,0:T(8,128)(2,1)S(1)} %collective-permute-done.1.left_ref, bf16[1,768]{1,0:T(2,128)(2,1)S(1)} %collective-permute-done.2.corner_ref, ...), custom_call_target="tpu_custom_call" | custom-call | flops 200000000 | bytes 4000000 | tf_op jit(solution)/shard_map/pallas_call | solution.py:190
  36.9 3.5 %all-to-all-start.1 = ((bf16[8,192,128]{2,1,0:T(8,128)(2,1)}), bf16[8,192,128]{2,1,0:T(8,128)(2,1)S(1)}, u32[]{:S(2)}, u32[]{:S(2)}) async-start(bf16[8,192,128]{2,1,0:T(8,128)(2,1)} %shard_map.67), calls=%async_computation.1 | async-start | bytes 786432 | tf_op jit(solution)/shard_map/all_to_all | solution.py:375
  40.4 1.7 %collective-permute-done.3 = bf16[128,384]{1,0:T(8,128)(2,1)S(1)} collective-permute-done((bf16[128,384]{1,0:T(8,128)(2,1)S(1)}, bf16[128,384]{1,0:T(8,128)(2,1)S(1)}, u32[]{:S(2)}, u32[]{:S(2)}) %collective-permute-start.3) | collective-permute-done | bytes 98336 | tf_op jit(solution)/shard_map/ppermute | solution.py:25
  42.2 2.3 %collective-permute-start.8 = (bf16[512,384]{1,0:T(8,128)(2,1)S(1)}, bf16[512,384]{1,0:T(8,128)(2,1)S(1)}, u32[]{:S(2)}, u32[]{:S(2)}) collective-permute-start(bf16[512,384]{1,0:T(8,128)(2,1)S(1)} %constant_dynamic-update-slice_fusion.refs_0_), channel_id=1, source_target_pairs={{0,1},{1,0},{2,3},{3,2},{4,5},{5,4},{6,7},{7,6},{8,9},{9,8},{10,11... | collective-permute-start | bytes 1179656 | tf_op jit(solution)/shard_map/ppermute | solution.py:25
  44.5 4.7 %collective-permute-start.7 = (bf16[512,384]{1,0:T(8,128)(2,1)S(1)}, bf16[512,384]{1,0:T(8,128)(2,1)S(1)}, u32[]{:S(2)}, u32[]{:S(2)}) collective-permute-start(bf16[512,384]{1,0:T(8,128)(2,1)S(1)} %constant_dynamic-update-slice_fusion.refs_0_), channel_id=1, source_target_pairs={{0,24},{16,0},{8,16},{24,8},{1,25},{17,1},{9,17},{25,9},{2,26},{18... | collective-permute-start | bytes 1179656 | tf_op jit(solution)/shard_map/ppermute | solution.py:31
  49.2 3.3 %shard_map.68 = (f32[16,1024]{1,0:T(8,128)S(1)}, f32[192,1024]{1,0:T(8,128)S(1)}) custom-call(bf16[8,192,128]{2,1,0:T(8,128)(2,1)S(1)} %all-to-all-done.1.q_ref, bf16[512,384]{1,0:T(8,128)(2,1)S(1)} %constant_dynamic-update-slice_fusion.refs_0_), custom_call_target="tpu_custom_call" | custom-call | flops 1572864 | bytes 1024 | tf_op jit(solution)/shard_map/pallas_call | solution.py:317
  52.6 9.4 %shard_map.69 = (f32[16,1024]{1,0:T(8,128)S(1)}, f32[192,1024]{1,0:T(8,128)S(1)}) custom-call(bf16[8,192,128]{2,1,0:T(8,128)(2,1)S(1)} %all-to-all-done.1.q_ref, bf16[512,384]{1,0:T(8,128)(2,1)S(1)} %collective-permute-done.8.refs_0_, f32[16,1024]{1,0:T(8,128)S(1)} %get-tuple-element.43.refs_1_, f32[192,1024]{1,0:T(8,128)S(1)} %get-tuple-element.44.refs_2_), custom_call_target="tpu_custom_call" | custom-call | flops 1572864 | bytes 1024 | tf_op jit(solution)/shard_map/pallas_call | solution.py:317
  62.0 0.8 collective-permute-start.12
  62.8 0.1 collective-permute-start.11
  63.0 4.2 %collective-permute-start.10 = (bf16[256,384]{1,0:T(8,128)(2,1)S(1)}, bf16[256,384]{1,0:T(8,128)(2,1)S(1)}, u32[]{:S(2)}, u32[]{:S(2)}) collective-permute-start(bf16[256,384]{1,0:T(8,128)(2,1)S(1)} %slice.7), channel_id=1, source_target_pairs={{0,24},{16,0},{8,16},{24,8},{1,25},{17,1},{9,17},{25,9},{2,26},{18... | collective-permute-start | bytes 589832 | tf_op jit(solution)/shard_map/ppermute | solution.py:31
  67.1 9.3 %shard_map.70 = (f32[16,1024]{1,0:T(8,128)S(1)}, f32[192,1024]{1,0:T(8,128)S(1)}) custom-call(bf16[8,192,128]{2,1,0:T(8,128)(2,1)S(1)} %all-to-all-done.1.q_ref, bf16[512,384]{1,0:T(8,128)(2,1)S(1)} %collective-permute-done.6.refs_0_, f32[16,1024]{1,0:T(8,128)S(1)} %get-tuple-element.49.refs_1_, f32[192,1024]{1,0:T(8,128)S(1)} %get-tuple-element.50.refs_2_), custom_call_target="tpu_custom_call" | custom-call | flops 1572864 | bytes 1024 | tf_op jit(solution)/shard_map/pallas_call | solution.py:317
  76.4 9.3 %shard_map.71 = (f32[16,1024]{1,0:T(8,128)S(1)}, f32[192,1024]{1,0:T(8,128)S(1)}) custom-call(bf16[8,192,128]{2,1,0:T(8,128)(2,1)S(1)} %all-to-all-done.1.q_ref, bf16[512,384]{1,0:T(8,128)(2,1)S(1)} %collective-permute-done.12.refs_0_, f32[16,1024]{1,0:T(8,128)S(1)} %get-tuple-element.51.refs_1_, f32[192,1024]{1,0:T(8,128)S(1)} %get-tuple-element.52.refs_2_), custom_call_target="tpu_custom_call" | custom-call | flops 1572864 | bytes 1024 | tf_op jit(solution)/shard_map/pallas_call | solution.py:317
  85.7 9.3 %shard_map.72 = (f32[16,1024]{1,0:T(8,128)S(1)}, f32[192,1024]{1,0:T(8,128)S(1)}) custom-call(bf16[8,192,128]{2,1,0:T(8,128)(2,1)S(1)} %all-to-all-done.1.q_ref, bf16[512,384]{1,0:T(8,128)(2,1)S(1)} %collective-permute-done.7.refs_0_, f32[16,1024]{1,0:T(8,128)S(1)} %get-tuple-element.53.refs_1_, f32[192,1024]{1,0:T(8,128)S(1)} %get-tuple-element.54.refs_2_), custom_call_target="tpu_custom_call" | custom-call | flops 1572864 | bytes 1024 | tf_op jit(solution)/shard_map/pallas_call | solution.py:317
  95.0 9.3 %shard_map.73 = (f32[16,1024]{1,0:T(8,128)S(1)}, f32[192,1024]{1,0:T(8,128)S(1)}) custom-call(bf16[8,192,128]{2,1,0:T(8,128)(2,1)S(1)} %all-to-all-done.1.q_ref, bf16[512,384]{1,0:T(8,128)(2,1)S(1)} %collective-permute-done.11.refs_0_, f32[16,1024]{1,0:T(8,128)S(1)} %get-tuple-element.55.refs_1_, f32[192,1024]{1,0:T(8,128)S(1)} %get-tuple-element.56.refs_2_), custom_call_target="tpu_custom_call" | custom-call | flops 1572864 | bytes 1024 | tf_op jit(solution)/shard_map/pallas_call | solution.py:317
  104.3 0.8 collective-permute-start.13
  105.1 0.3 collective-permute-start.14
  105.4 9.3 %shard_map.74 = (f32[16,1024]{1,0:T(8,128)S(1)}, f32[192,1024]{1,0:T(8,128)S(1)}) custom-call(bf16[8,192,128]{2,1,0:T(8,128)(2,1)S(1)} %all-to-all-done.1.q_ref, bf16[256,384]{1,0:T(8,128)(2,1)S(1)} %collective-permute-done.9.refs_0_, bf16[256,384]{1,0:T(8,128)(2,1)S(1)} %collective-permute-done.10.refs_1_, f32[16,1024]{1,0:T(8,128)S(1)} %get-tuple-element.61.refs_2_, ...), custom_call_target="tpu_custom_call" | custom-call | flops 1572864 | bytes 1024 | tf_op jit(solution)/shard_map/pallas_call | solution.py:317
  114.7 9.3 %shard_map.75 = bf16[8,208,128]{2,1,0:T(8,128)(2,1)S(1)} custom-call(bf16[8,192,128]{2,1,0:T(8,128)(2,1)S(1)} %all-to-all-done.1.q_ref, bf16[256,384]{1,0:T(8,128)(2,1)S(1)} %collective-permute-done.13.refs_0_, bf16[256,384]{1,0:T(8,128)(2,1)S(1)} %collective-permute-done.14.refs_1_, f32[16,1024]{1,0:T(8,128)S(1)} %get-tuple-element.63.refs_2_, ...), custom_call_target="tpu_custom_call" | custom-call | flops 1572864 | bytes 1024 | tf_op jit(solution)/shard_map/pallas_call | solution.py:317
  124.0 10.5 %all_to_all.16.parts_ref = bf16[8,208,128]{2,1,0:T(8,128)(2,1)S(1)} all-to-all(bf16[8,208,128]{2,1,0:T(8,128)(2,1)S(1)} %shard_map.75), channel_id=1, replica_groups=mesh['zq'=4,'zc'=2,'xl'=2,'xh'=2,'y'=4,'core'=2] {'zc','y'}, dimensions={0} | all-to-all | bytes 851968 | tf_op jit(solution)/shard_map/all_to_all | solution.py:390
  134.5 1.1 shard_map.76
  (33 shorter events, 0.2 us)
Async XLA Ops:
  0.0 15.0 %copy-start = (bf16[768,2304]{1,0:T(8,128)(2,1)S(1)}, bf16[768,2304]{1,0:T(8,128)(2,1)}, u32[]{:S(2)}) copy-start(bf16[768,2304]{1,0:T(8,128)(2,1)} %w_ref.6) | copy-start | bytes 10616836
  0.0 1.3 copy-start.4
  1.3 0.7 copy-start.5
  3.8 12.9 %collective-permute-start.2 = (bf16[1,768]{1,0:T(2,128)(2,1)S(1)}, bf16[1,768]{1,0:T(2,128)(2,1)S(1)}, u32[]{:S(2)}, u32[]{:S(2)}) collective-permute-start(bf16[1,768]{1,0:T(2,128)(2,1)S(1)} %get-tuple-element.39), channel_id=1, source_target_pairs={{0,17},{1,18},{2,19},{3,20},{4,21},{5,22},{6,23},{7,24},{8,25},{9,... | collective-permute-start | bytes 4616 | tf_op jit(solution)/shard_map/ppermute | solution.py:42
  9.3 7.4 %collective-permute-start = (bf16[16,768]{1,0:T(8,128)(2,1)S(1)}, bf16[16,768]{1,0:T(8,128)(2,1)S(1)}, u32[]{:S(2)}, u32[]{:S(2)}) collective-permute-start(bf16[16,768]{1,0:T(8,128)(2,1)S(1)} %get-tuple-element.37), channel_id=1, source_target_pairs={{0,16},{16,32},{32,48},{48,64},{64,80},{80,96},{96,112},{112,128},... | collective-permute-start | bytes 73736 | tf_op jit(solution)/shard_map/ppermute | solution.py:36
  12.8 3.9 %collective-permute-start.1 = (bf16[32,768]{1,0:T(8,128)(2,1)S(1)}, bf16[32,768]{1,0:T(8,128)(2,1)S(1)}, u32[]{:S(2)}, u32[]{:S(2)}) collective-permute-start(bf16[32,768]{1,0:T(8,128)(2,1)S(1)} %get-tuple-element.38), channel_id=1, source_target_pairs={{0,1},{1,2},{2,3},{3,4},{4,5},{5,6},{6,7},{7,8},{8,9},{9,10},{10,1... | collective-permute-start | bytes 147464 | tf_op jit(solution)/shard_map/ppermute | solution.py:36
  15.0 1.7 %copy-start.2 = (f32[9,1536]{1,0:T(8,128)S(1)}, f32[9,1536]{1,0:T(8,128)}, u32[]{:S(2)}) copy-start(f32[9,1536]{1,0:T(8,128)} %pool_ref.2) | copy-start | bytes 165892
  16.7 18.8 %copy-start.3 = (f32[9,768]{1,0:T(8,128)S(1)}, f32[9,768]{1,0:T(8,128)}, u32[]{:S(2)}) copy-start(f32[9,768]{1,0:T(8,128)} %pool_ref.3) | copy-start | bytes 82948
  27.2 15.0 %collective-permute-start.5 = (bf16[128,384]{1,0:T(8,128)(2,1)S(1)}, bf16[128,384]{1,0:T(8,128)(2,1)S(1)}, u32[]{:S(2)}, u32[]{:S(2)}) collective-permute-start(bf16[128,384]{1,0:T(8,128)(2,1)S(1)} %bitcast.1), channel_id=1, source_target_pairs={{0,192},{64,0},{128,64},{192,128},{1,193},{65,1},{129,65},{193,129... | collective-permute-start | bytes 294920 | tf_op jit(solution)/shard_map/ppermute | solution.py:25
  32.3 9.8 %collective-permute-start.4 = (bf16[128,384]{1,0:T(8,128)(2,1)S(1)}, bf16[128,384]{1,0:T(8,128)(2,1)S(1)}, u32[]{:S(2)}, u32[]{:S(2)}) collective-permute-start(bf16[128,384]{1,0:T(8,128)(2,1)S(1)} %bitcast.2), channel_id=1, source_target_pairs={{0,64},{64,128},{128,192},{192,0},{1,65},{65,129},{129,193},{193,1... | collective-permute-start | bytes 294920 | tf_op jit(solution)/shard_map/ppermute | solution.py:25
  32.3 9.8 %collective-permute-start.3 = (bf16[128,384]{1,0:T(8,128)(2,1)S(1)}, bf16[128,384]{1,0:T(8,128)(2,1)S(1)}, u32[]{:S(2)}, u32[]{:S(2)}) collective-permute-start(bf16[128,384]{1,0:T(8,128)(2,1)S(1)} %bitcast.3), channel_id=1, source_target_pairs={{0,128},{64,192},{128,0},{192,64},{1,129},{65,193},{129,1},{193,65... | collective-permute-start | bytes 294920 | tf_op jit(solution)/shard_map/ppermute | solution.py:25
  36.9 12.3 %all-to-all-start.1 = ((bf16[8,192,128]{2,1,0:T(8,128)(2,1)}), bf16[8,192,128]{2,1,0:T(8,128)(2,1)S(1)}, u32[]{:S(2)}, u32[]{:S(2)}) async-start(bf16[8,192,128]{2,1,0:T(8,128)(2,1)} %shard_map.67), calls=%async_computation.1 | async-start | bytes 786432 | tf_op jit(solution)/shard_map/all_to_all | solution.py:375
  42.2 10.4 %collective-permute-start.8 = (bf16[512,384]{1,0:T(8,128)(2,1)S(1)}, bf16[512,384]{1,0:T(8,128)(2,1)S(1)}, u32[]{:S(2)}, u32[]{:S(2)}) collective-permute-start(bf16[512,384]{1,0:T(8,128)(2,1)S(1)} %constant_dynamic-update-slice_fusion.refs_0_), channel_id=1, source_target_pairs={{0,1},{1,0},{2,3},{3,2},{4,5},{5,4},{6,7},{7,6},{8,9},{9,8},{10,11... | collective-permute-start | bytes 1179656 | tf_op jit(solution)/shard_map/ppermute | solution.py:25
  44.5 17.5 %collective-permute-start.7 = (bf16[512,384]{1,0:T(8,128)(2,1)S(1)}, bf16[512,384]{1,0:T(8,128)(2,1)S(1)}, u32[]{:S(2)}, u32[]{:S(2)}) collective-permute-start(bf16[512,384]{1,0:T(8,128)(2,1)S(1)} %constant_dynamic-update-slice_fusion.refs_0_), channel_id=1, source_target_pairs={{0,24},{16,0},{8,16},{24,8},{1,25},{17,1},{9,17},{25,9},{2,26},{18... | collective-permute-start | bytes 1179656 | tf_op jit(solution)/shard_map/ppermute | solution.py:31
  49.2 12.8 %collective-permute-start.6 = (bf16[512,384]{1,0:T(8,128)(2,1)S(1)}, bf16[512,384]{1,0:T(8,128)(2,1)S(1)}, u32[]{:S(2)}, u32[]{:S(2)}) collective-permute-start(bf16[512,384]{1,0:T(8,128)(2,1)S(1)} %constant_dynamic-update-slice_fusion.refs_0_), channel_id=1, source_target_pairs={{0,16},{16,8},{8,24},{24,0},{1,17},{17,9},{9,25},{25,1},{2,18},{18... | collective-permute-start | bytes 1179656 | tf_op jit(solution)/shard_map/ppermute | solution.py:31
  62.0 14.4 %collective-permute-start.12 = (bf16[512,384]{1,0:T(8,128)(2,1)S(1)}, bf16[512,384]{1,0:T(8,128)(2,1)S(1)}, u32[]{:S(2)}, u32[]{:S(2)}) collective-permute-start(bf16[512,384]{1,0:T(8,128)(2,1)S(1)} %collective-permute-done.6.refs_0_), channel_id=1, source_target_pairs={{0,1},{1,0},{2,3},{3,2},{4,5},{5,4},{6,7},{7,6},{8,9},{9,8},{10,11... | collective-permute-start | bytes 1179656 | tf_op jit(solution)/shard_map/ppermute | solution.py:25
  62.8 32.2 %collective-permute-start.11 = (bf16[512,384]{1,0:T(8,128)(2,1)S(1)}, bf16[512,384]{1,0:T(8,128)(2,1)S(1)}, u32[]{:S(2)}, u32[]{:S(2)}) collective-permute-start(bf16[512,384]{1,0:T(8,128)(2,1)S(1)} %collective-permute-done.7.refs_0_), channel_id=1, source_target_pairs={{0,1},{1,0},{2,3},{3,2},{4,5},{5,4},{6,7},{7,6},{8,9},{9,8},{10,11... | collective-permute-start | bytes 1179656 | tf_op jit(solution)/shard_map/ppermute | solution.py:25
  63.0 41.3 %collective-permute-start.10 = (bf16[256,384]{1,0:T(8,128)(2,1)S(1)}, bf16[256,384]{1,0:T(8,128)(2,1)S(1)}, u32[]{:S(2)}, u32[]{:S(2)}) collective-permute-start(bf16[256,384]{1,0:T(8,128)(2,1)S(1)} %slice.7), channel_id=1, source_target_pairs={{0,24},{16,0},{8,16},{24,8},{1,25},{17,1},{9,17},{25,9},{2,26},{18... | collective-permute-start | bytes 589832 | tf_op jit(solution)/shard_map/ppermute | solution.py:31
  67.1 37.1 %collective-permute-start.9 = (bf16[256,384]{1,0:T(8,128)(2,1)S(1)}, bf16[256,384]{1,0:T(8,128)(2,1)S(1)}, u32[]{:S(2)}, u32[]{:S(2)}) collective-permute-start(bf16[256,384]{1,0:T(8,128)(2,1)S(1)} %slice.6), channel_id=1, source_target_pairs={{0,16},{16,8},{8,24},{24,0},{1,17},{17,9},{9,25},{25,1},{2,18},{18... | collective-permute-start | bytes 589832 | tf_op jit(solution)/shard_map/ppermute | solution.py:31
  104.3 10.4 %collective-permute-start.13 = (bf16[256,384]{1,0:T(8,128)(2,1)S(1)}, bf16[256,384]{1,0:T(8,128)(2,1)S(1)}, u32[]{:S(2)}, u32[]{:S(2)}) collective-permute-start(bf16[256,384]{1,0:T(8,128)(2,1)S(1)} %collective-permute-done.9.refs_0_), channel_id=1, source_target_pairs={{0,1},{1,0},{2,3},{3,2},{4,5},{5,4},{6,7},{7,6},{8,9},{9,8},{10,11... | collective-permute-start | bytes 589832 | tf_op jit(solution)/shard_map/ppermute | solution.py:25
  105.1 9.6 %collective-permute-start.14 = (bf16[256,384]{1,0:T(8,128)(2,1)S(1)}, bf16[256,384]{1,0:T(8,128)(2,1)S(1)}, u32[]{:S(2)}, u32[]{:S(2)}) collective-permute-start(bf16[256,384]{1,0:T(8,128)(2,1)S(1)} %collective-permute-done.10.refs_1_), channel_id=1, source_target_pairs={{0,1},{1,0},{2,3},{3,2},{4,5},{5,4},{6,7},{7,6},{8,9},{9,8},{10,11... | collective-permute-start | bytes 589832 | tf_op jit(solution)/shard_map/ppermute | solution.py:25
  114.7 19.9 %copy-start.1 = (bf16[768,768]{1,0:T(8,128)(2,1)S(1)}, bf16[768,768]{1,0:T(8,128)(2,1)}, u32[]{:S(2)}) copy-start(bf16[768,768]{1,0:T(8,128)(2,1)} %w_ref.7) | copy-start | bytes 3538948

commit v2 on v1

--- a/solution.py
+++ b/solution.py
@@ -66,10 +66,18 @@
     return jnp.concatenate(picked, 1)
 
 
-def tokens_kernel(patches_ref, gain_ref, tokens_ref, column_ref, row_ref, corner_ref, plain):
-    rows, cols, width = patches_ref.shape
-    keep(plain, patches_ref[...].astype(f32).reshape(rows * cols, width))
-    gain = gain_ref[...].reshape(1, width)
+def tokens_kernel(patches_ref, gain_ref, tokens_ref, column_ref, row_ref, corner_ref, patches, gains, plain, sems):
+    rows, cols, width = patches.shape
+    copies = [
+        pltpu.make_async_copy(patches_ref, patches, sems.at[0]),
+        pltpu.make_async_copy(gain_ref, gains, sems.at[1]),
+    ]
+    for copy in copies:
+        copy.start()
+    for copy in copies:
+        copy.wait()
+    keep(plain, patches[...].astype(f32).reshape(rows * cols, width))
+    gain = gains[...].reshape(1, width)
     last = [None] * cols
     for place, c in enumerate(ORDER):
         parts = [every_nth(plain, cols * r + c, 4 * cols) for r in range(4)]
@@ -90,11 +98,16 @@
     shapes = [(rows * cols, width), (rows, width), (cols, width), (1, width)]
     return pl.pallas_call(
         tokens_kernel,
-        in_specs=[pl.BlockSpec(memory_space=pltpu.VMEM)] * 2,
+        in_specs=[pl.BlockSpec(memory_space=pl.ANY)] * 2,
         out_specs=[pl.BlockSpec(memory_space=pltpu.VMEM)] * 4,
         out_shape=[jax.ShapeDtypeStruct(s, bf16) for s in shapes],
-        scratch_shapes=[pltpu.VMEM((width // 128, rows * cols, 128), f32)],
-        compiler_params=pltpu.CompilerParams(vmem_limit_bytes=16 * 2**20),
+        scratch_shapes=[
+            pltpu.VMEM(patches.shape, bf16),
+            pltpu.VMEM(gain.shape, f32),
+            pltpu.VMEM((width // 128, rows * cols, 128), f32),
+            pltpu.SemaphoreType.DMA((2,)),
+        ],
+        compiler_params=pltpu.CompilerParams(vmem_limit_bytes=57 * 2**20),
         cost_estimate=pl.CostEstimate(flops=4_000_000_000, bytes_accessed=1_000_000, transcendentals=0),
     )(patches, gain)
 
@@ -197,25 +210,30 @@
     )(own, *halo, w_qkv, taps)
 
 
+def pad_queries(q_ref, padded):
+    zero = jnp.zeros((HEAD, 128), bf16)
+    for t in range(q_ref.shape[0]):
+        lanes = slice(t * 128, (t + 1) * 128)
+        for h in range(GROUP):
+            here = HEAD * (h % 2)
+            padded[h, here : here + HEAD, lanes] = q_ref[t, HEAD * h : HEAD * (h + 1)]
+            padded[h, HEAD - here : 2 * HEAD - here, lanes] = zero
+
+
 def attend_kernel(first, last, qb, blocks, q_ref, *refs):
     block_refs, refs = refs[:blocks], refs[blocks:]
     if first:
-        stat_in, acc_in = None, None
+        stat, acc, qz = refs
+        pad_queries(q_ref, qz)
     else:
         stat_in, acc_in, *refs = refs
-    if last:
-        out_ref, qz, stat, acc = refs
-    else:
-        stat, acc, qz = refs
-    tiles = q_ref.shape[0]
-    count = tiles * 128
-    zero = jnp.zeros((HEAD, 128), bf16)
-    for t in range(tiles):
-        lanes = slice(t * 128, (t + 1) * 128)
-        for h in range(GROUP):
-            here = HEAD * (h % 2)
-            qz[h, here : here + HEAD, lanes] = q_ref[t, HEAD * h : HEAD * (h + 1)]
-            qz[h, HEAD - here : 2 * HEAD - here, lanes] = zero
+        qz = q_ref
+        if last:
+            out_ref, stat, acc = refs
+        else:
+            stat, acc = refs
+    count = qz.shape[2]
+    tiles = count // 128
 
     jobs = [(j, h) for j in range(count // qb) for h in range(GROUP)]
 
@@ -302,27 +320,28 @@
 
 
 def attend(queries, blocks, carry, last=False, qb=512):
-    tiles = queries.shape[0]
-    count = tiles * 128
+    first = carry is None
+    carry = [] if first else carry
+    count = queries.shape[0] * 128 if first else queries.shape[2]
     keys = sum(b.shape[0] for b in blocks)
     carry_shapes = [(16, count), (WIDE, count)]
+    scratch = []
     if last:
-        out_shape = [jax.ShapeDtypeStruct((tiles, WIDE + STATS, 128), bf16)]
+        out_shape = [jax.ShapeDtypeStruct((count // 128, WIDE + STATS, 128), bf16)]
         scratch = [pltpu.VMEM(s, f32) for s in carry_shapes]
     else:
         out_shape = [jax.ShapeDtypeStruct(s, f32) for s in carry_shapes]
-        scratch = []
-    carry = [] if carry is None else carry
-    work = GROUP * count * keys
+        if first:
+            out_shape.append(jax.ShapeDtypeStruct((GROUP, 2 * HEAD, count), bf16))
     outs = pl.pallas_call(
-        functools.partial(attend_kernel, not carry, last, qb, len(blocks)),
+        functools.partial(attend_kernel, first, last, qb, len(blocks)),
         in_specs=[pl.BlockSpec(memory_space=pltpu.VMEM)] * (1 + len(blocks) + len(carry)),
         out_specs=[pl.BlockSpec(memory_space=pltpu.VMEM)] * len(out_shape),
         out_shape=out_shape,
-        scratch_shapes=[pltpu.VMEM((GROUP, 128, count), bf16)] + scratch,
+        scratch_shapes=scratch,
         compiler_params=pltpu.CompilerParams(vmem_limit_bytes=24 * 2**20),
         cost_estimate=pl.CostEstimate(
-            flops=work * 1, bytes_accessed=1024, transcendentals=0
+            flops=GROUP * count * keys * 1, bytes_accessed=1024, transcendentals=0
         ),
     )(queries, *blocks, *carry)
     return outs[0] if last else outs
@@ -376,17 +395,17 @@
     line = jnp.concatenate(line, 0)
     after, before = shifted_x(line, 1), shifted_x(line, -1)
     swap = lambda block: shifted(block, "core", 1)
-    carry = attend(every_query, [line], None)
-    carry = attend(every_query, [swap(line)], carry)
+    *carry, padded = attend(every_query, [line], None)
+    carry = attend(padded, [swap(line)], carry)
     after, before, carry = tie((after, before, carry))
     half = line.shape[0] // 2
     far = [shifted_x(after[:half], 1), shifted_x(before[half:], -1)]
     for block in (after, swap(after), before, swap(before)):
-        carry = attend(every_query, [block], carry)
+        carry = attend(padded, [block], carry)
     far, carry = tie((far, carry))
     swapped = [swap(block) for block in far]
-    carry = attend(every_query, far, carry)
-    partial = attend(every_query, swapped, carry, last=True)
+    carry = attend(padded, far, carry)
+    partial = attend(padded, swapped, carry, last=True)
     parts = lax.all_to_all(partial, ("zc", "y"), 0, 0, tiled=True)
     return finish(parts, w_out)
 

time: 137 us -> 137 us (level)
    ppermute x4, starting transfers between devices: 8.9 us -> 4.83 us  [shifted_x(): return lax.ppermute(block, ('xl', 'xh'), route)]
    ppermute x8, starting transfers between devices: 12.7 us -> 16.6 us  [shifted(): lax.ppermute(block, axis, [(i, (i + distance) % count) for i in range(cou...]
    ppermute x8, waiting for transfers between devices: 1.7 us -> 0.02 us  [shifted(): lax.ppermute(block, axis, [(i, (i + distance) % count) for i in range(cou...]
  transfers between devices with their start and end apart: 16 -> 16, of which waited for: 1 -> 1; matrix products, arithmetic and copies ran while one was open for 0% -> 0% of each run, Pallas kernels for 46% -> 45%
where the time goes in v2:
time: 137 us; the launch traced here: 135 us
  Pallas kernels  76.3 us (56%)
  starting transfers between devices  36.1 us (26%)
  blocking collectives  20.4 us (15%)
    pallas_call x8, Pallas kernels, attend(): pl.pallas_call(functools.partial(attend_kernel, first, last, qb, len(bloc...  67.6 us
    ppermute x8, starting transfers between devices, shifted(): lax.ppermute(block, axis, [(i, (i + distance) % count) for i in range(cou...  16.6 us
    all_to_all x1, blocking collectives, on_device(): parts = lax.all_to_all(partial, ('zc', 'y'), 0, 0, tiled=True)  10.5 us
    all_to_all x1, blocking collectives, on_device(): own = lax.all_to_all(flat, 'y', 0, 0, tiled=True).reshape(-1, 2 * WIDE)  9.88 us
    ppermute x2, starting transfers between devices, passed_along(): return lax.ppermute(block, axis, [(i - 1, i) for i in range(1, count)])  5.71 us
    ppermute x1, starting transfers between devices, corner(): return lax.ppermute(block, AXES, route)  5.52 us
    ppermute x4, starting transfers between devices, shifted_x(): return lax.ppermute(block, ('xl', 'xh'), route)  4.83 us
    pallas_call x1, Pallas kernels, normalised_tokens(): pl.pallas_call(tokens_kernel, in_specs=[pl.BlockSpec(memory_space=pl.ANY)...  3.95 us
  transfers between devices with their start and end apart: 16, of which 1 were waited for; matrix products, arithmetic and copies ran while one was open for 0% of the time, Pallas kernels for 45%

profile of v2, /device:TPU:1, one launch (start us, length us, event | category | flops | bytes accessed | tf_op | source)
XLA Modules:
  0.0 135.4 jit_solution(14855932210835192638)
XLA Ops:
  0.0 4.0 %shard_map.64 = (bf16[512,768]{1,0:T(8,128)(2,1)}, bf16[32,768]{1,0:T(8,128)(2,1)}, bf16[16,768]{1,0:T(8,128)(2,1)}, bf16[1,768]{1,0:T(2,128)(2,1)}) custom-call(bf16[32,16,768]{2,1,0:T(8,128)(2,1)} %patches_ref.1, f32[768]{0:T(1024)} %gain_ref.1), custom_call_target="tpu_custom_call" | custom-call | flops 4000000000 | bytes 1000000 | tf_op jit(solution)/shard_map/pallas_call | solution.py:99
  4.0 5.5 %collective-permute-start.2 = (bf16[1,768]{1,0:T(2,128)(2,1)}, bf16[1,768]{1,0:T(2,128)(2,1)S(1)}, u32[]{:S(2)}, u32[]{:S(2)}) collective-permute-start(bf16[1,768]{1,0:T(2,128)(2,1)} %get-tuple-element.40), channel_id=1, source_target_pairs={{0,17},{1,18},{2,19},{3,20},{4,21},{5,22},{6,23},{7,24},{8,25},{9,... | collective-permute-start | bytes 4616 | tf_op jit(solution)/shard_map/ppermute | solution.py:42
  9.5 3.5 %collective-permute-start = (bf16[16,768]{1,0:T(8,128)(2,1)}, bf16[16,768]{1,0:T(8,128)(2,1)S(1)}, u32[]{:S(2)}, u32[]{:S(2)}) collective-permute-start(bf16[16,768]{1,0:T(8,128)(2,1)} %get-tuple-element.38), channel_id=1, source_target_pairs={{0,16},{16,32},{32,48},{48,64},{64,80},{80,96},{96,112},{112,128},... | collective-permute-start | bytes 73736 | tf_op jit(solution)/shard_map/ppermute | solution.py:36
  13.0 2.2 %collective-permute-start.1 = (bf16[32,768]{1,0:T(8,128)(2,1)}, bf16[32,768]{1,0:T(8,128)(2,1)S(1)}, u32[]{:S(2)}, u32[]{:S(2)}) collective-permute-start(bf16[32,768]{1,0:T(8,128)(2,1)} %get-tuple-element.39), channel_id=1, source_target_pairs={{0,1},{1,2},{2,3},{3,4},{4,5},{5,6},{6,7},{7,8},{8,9},{9,10},{10,1... | collective-permute-start | bytes 147464 | tf_op jit(solution)/shard_map/ppermute | solution.py:36
  15.2 1.1 copy-done.4
  16.4 1.6 %shard_map.65 = (bf16[512,768]{1,0:T(8,128)(2,1)S(1)}, bf16[352,1536]{1,0:T(8,128)(2,1)S(1)}) custom-call(bf16[512,768]{1,0:T(8,128)(2,1)S(1)} %copy-done.4, bf16[768,2304]{1,0:T(8,128)(2,1)S(1)} %copy-done), custom_call_target="tpu_custom_call" | custom-call | flops 1500000000 | bytes 4000000 | tf_op jit(solution)/shard_map/pallas_call | solution.py:127
  18.0 0.0 copy-start.3
  18.1 0.7 shard_map.66
  18.7 9.9 %all_to_all.15 = bf16[4,32,384]{2,1,0:T(8,128)(2,1)S(1)} all-to-all(bf16[4,32,384]{2,1,0:T(8,128)(2,1)S(1)} %shard_map.66), channel_id=1, replica_groups=mesh['zq'=4,'zc'=2,'xl'=2,'xh'=2,'y'=4,'core'=2] {'y'}, dimensions={0} | all-to-all | bytes 196608 | tf_op jit(solution)/shard_map/all_to_all | solution.py:389
  28.6 5.1 %collective-permute-start.5 = (bf16[128,384]{1,0:T(8,128)(2,1)S(1)}, bf16[128,384]{1,0:T(8,128)(2,1)S(1)}, u32[]{:S(2)}, u32[]{:S(2)}) collective-permute-start(bf16[128,384]{1,0:T(8,128)(2,1)S(1)} %bitcast.1), channel_id=1, source_target_pairs={{0,192},{64,0},{128,64},{192,128},{1,193},{65,1},{129,65},{193,129... | collective-permute-start | bytes 294920 | tf_op jit(solution)/shard_map/ppermute | solution.py:25
  33.7 3.3 %collective-permute-start.3 = (bf16[128,384]{1,0:T(8,128)(2,1)S(1)}, bf16[128,384]{1,0:T(8,128)(2,1)S(1)}, u32[]{:S(2)}, u32[]{:S(2)}) collective-permute-start(bf16[128,384]{1,0:T(8,128)(2,1)S(1)} %bitcast.3), channel_id=1, source_target_pairs={{0,128},{64,192},{128,0},{192,64},{1,129},{65,193},{129,1},{193,65... | collective-permute-start | bytes 294920 | tf_op jit(solution)/shard_map/ppermute | solution.py:25
  37.0 1.4 %shard_map.67 = bf16[8,192,128]{2,1,0:T(8,128)(2,1)} custom-call(bf16[512,768]{1,0:T(8,128)(2,1)S(1)} %get-tuple-element.42.own_ref, bf16[16,768]{1,0:T(8,128)(2,1)S(1)} %collective-permute-done.upper_ref, bf16[32,768]{1,0:T(8,128)(2,1)S(1)} %collective-permute-done.1.left_ref, bf16[1,768]{1,0:T(2,128)(2,1)S(1)} %collective-permute-done.2.corner_ref, ...), custom_call_target="tpu_custom_call" | custom-call | flops 200000000 | bytes 4000000 | tf_op jit(solution)/shard_map/pallas_call | solution.py:203
  38.3 3.5 %all-to-all-start.1 = ((bf16[8,192,128]{2,1,0:T(8,128)(2,1)}), bf16[8,192,128]{2,1,0:T(8,128)(2,1)S(1)}, u32[]{:S(2)}, u32[]{:S(2)}) async-start(bf16[8,192,128]{2,1,0:T(8,128)(2,1)} %shard_map.67), calls=%async_computation.1 | async-start | bytes 786432 | tf_op jit(solution)/shard_map/all_to_all | solution.py:394
  41.9 4.0 %collective-permute-start.8 = (bf16[512,384]{1,0:T(8,128)(2,1)S(1)}, bf16[512,384]{1,0:T(8,128)(2,1)S(1)}, u32[]{:S(2)}, u32[]{:S(2)}) collective-permute-start(bf16[512,384]{1,0:T(8,128)(2,1)S(1)} %constant_dynamic-update-slice_fusion.refs_0_), channel_id=1, source_target_pairs={{0,1},{1,0},{2,3},{3,2},{4,5},{5,4},{6,7},{7,6},{8,9},{9,8},{10,11... | collective-permute-start | bytes 1179656 | tf_op jit(solution)/shard_map/ppermute | solution.py:25
  46.0 1.4 %collective-permute-start.7 = (bf16[512,384]{1,0:T(8,128)(2,1)S(1)}, bf16[512,384]{1,0:T(8,128)(2,1)S(1)}, u32[]{:S(2)}, u32[]{:S(2)}) collective-permute-start(bf16[512,384]{1,0:T(8,128)(2,1)S(1)} %constant_dynamic-update-slice_fusion.refs_0_), channel_id=1, source_target_pairs={{0,24},{16,0},{8,16},{24,8},{1,25},{17,1},{9,17},{25,9},{2,26},{18... | collective-permute-start | bytes 1179656 | tf_op jit(solution)/shard_map/ppermute | solution.py:31
  47.4 0.0 collective-permute-start.6
  47.4 1.0 all-to-all-done.1.q_ref
  48.4 3.3 %shard_map.68 = (f32[16,1024]{1,0:T(8,128)S(1)}, f32[192,1024]{1,0:T(8,128)S(1)}, bf16[3,128,1024]{2,1,0:T(8,128)(2,1)S(1)}) custom-call(bf16[8,192,128]{2,1,0:T(8,128)(2,1)S(1)} %all-to-all-done.1.q_ref, bf16[512,384]{1,0:T(8,128)(2,1)S(1)} %constant_dynamic-update-slice_fusion.refs_0_), custom_call_target="tpu_custom_call" | custom-call | flops 1572864 | bytes 1024 | tf_op jit(solution)/shard_map/pallas_call | solution.py:336
  51.7 9.2 %shard_map.69 = (f32[16,1024]{1,0:T(8,128)S(1)}, f32[192,1024]{1,0:T(8,128)S(1)}) custom-call(bf16[3,128,1024]{2,1,0:T(8,128)(2,1)S(1)} %get-tuple-element.44.q_ref, bf16[512,384]{1,0:T(8,128)(2,1)S(1)} %collective-permute-done.8.refs_0_, f32[16,1024]{1,0:T(8,128)S(1)} %get-tuple-element.45.refs_1_, f32[192,1024]{1,0:T(8,128)S(1)} %get-tuple-element.46.refs_2_), custom_call_target="tpu_custom_call" | custom-call | flops 1572864 | bytes 1024 | tf_op jit(solution)/shard_map/pallas_call | solution.py:336
  60.9 3.0 %collective-permute-start.12 = (bf16[512,384]{1,0:T(8,128)(2,1)S(1)}, bf16[512,384]{1,0:T(8,128)(2,1)S(1)}, u32[]{:S(2)}, u32[]{:S(2)}) collective-permute-start(bf16[512,384]{1,0:T(8,128)(2,1)S(1)} %collective-permute-done.6.refs_0_), channel_id=1, source_target_pairs={{0,1},{1,0},{2,3},{3,2},{4,5},{5,4},{6,7},{7,6},{8,9},{9,8},{10,11... | collective-permute-start | bytes 1179656 | tf_op jit(solution)/shard_map/ppermute | solution.py:25
  63.9 0.1 collective-permute-start.11
  64.1 3.3 %collective-permute-start.10 = (bf16[256,384]{1,0:T(8,128)(2,1)S(1)}, bf16[256,384]{1,0:T(8,128)(2,1)S(1)}, u32[]{:S(2)}, u32[]{:S(2)}) collective-permute-start(bf16[256,384]{1,0:T(8,128)(2,1)S(1)} %slice.7), channel_id=1, source_target_pairs={{0,24},{16,0},{8,16},{24,8},{1,25},{17,1},{9,17},{25,9},{2,26},{18... | collective-permute-start | bytes 589832 | tf_op jit(solution)/shard_map/ppermute | solution.py:31
  67.4 9.2 %shard_map.70 = (f32[16,1024]{1,0:T(8,128)S(1)}, f32[192,1024]{1,0:T(8,128)S(1)}) custom-call(bf16[3,128,1024]{2,1,0:T(8,128)(2,1)S(1)} %get-tuple-element.44.q_ref, bf16[512,384]{1,0:T(8,128)(2,1)S(1)} %collective-permute-done.6.refs_0_, f32[16,1024]{1,0:T(8,128)S(1)} %get-tuple-element.51.refs_1_, f32[192,1024]{1,0:T(8,128)S(1)} %get-tuple-element.52.refs_2_), custom_call_target="tpu_custom_call" | custom-call | flops 1572864 | bytes 1024 | tf_op jit(solution)/shard_map/pallas_call | solution.py:336
  76.6 9.2 %shard_map.71 = (f32[16,1024]{1,0:T(8,128)S(1)}, f32[192,1024]{1,0:T(8,128)S(1)}) custom-call(bf16[3,128,1024]{2,1,0:T(8,128)(2,1)S(1)} %get-tuple-element.44.q_ref, bf16[512,384]{1,0:T(8,128)(2,1)S(1)} %collective-permute-done.12.refs_0_, f32[16,1024]{1,0:T(8,128)S(1)} %get-tuple-element.53.refs_1_, f32[192,1024]{1,0:T(8,128)S(1)} %get-tuple-element.54.refs_2_), custom_call_target="tpu_custom_call" | custom-call | flops 1572864 | bytes 1024 | tf_op jit(solution)/shard_map/pallas_call | solution.py:336
  85.8 9.2 %shard_map.72 = (f32[16,1024]{1,0:T(8,128)S(1)}, f32[192,1024]{1,0:T(8,128)S(1)}) custom-call(bf16[3,128,1024]{2,1,0:T(8,128)(2,1)S(1)} %get-tuple-element.44.q_ref, bf16[512,384]{1,0:T(8,128)(2,1)S(1)} %collective-permute-done.7.refs_0_, f32[16,1024]{1,0:T(8,128)S(1)} %get-tuple-element.55.refs_1_, f32[192,1024]{1,0:T(8,128)S(1)} %get-tuple-element.56.refs_2_), custom_call_target="tpu_custom_call" | custom-call | flops 1572864 | bytes 1024 | tf_op jit(solution)/shard_map/pallas_call | solution.py:336
  95.0 9.2 %shard_map.73 = (f32[16,1024]{1,0:T(8,128)S(1)}, f32[192,1024]{1,0:T(8,128)S(1)}) custom-call(bf16[3,128,1024]{2,1,0:T(8,128)(2,1)S(1)} %get-tuple-element.44.q_ref, bf16[512,384]{1,0:T(8,128)(2,1)S(1)} %collective-permute-done.11.refs_0_, f32[16,1024]{1,0:T(8,128)S(1)} %get-tuple-element.57.refs_1_, f32[192,1024]{1,0:T(8,128)S(1)} %get-tuple-element.58.refs_2_), custom_call_target="tpu_custom_call" | custom-call | flops 1572864 | bytes 1024 | tf_op jit(solution)/shard_map/pallas_call | solution.py:336
  104.2 0.8 collective-permute-start.13
  104.9 0.3 collective-permute-start.14
  105.3 9.2 %shard_map.74 = (f32[16,1024]{1,0:T(8,128)S(1)}, f32[192,1024]{1,0:T(8,128)S(1)}) custom-call(bf16[3,128,1024]{2,1,0:T(8,128)(2,1)S(1)} %get-tuple-element.44.q_ref, bf16[256,384]{1,0:T(8,128)(2,1)S(1)} %collective-permute-done.9.refs_0_, bf16[256,384]{1,0:T(8,128)(2,1)S(1)} %collective-permute-done.10.refs_1_, f32[16,1024]{1,0:T(8,128)S(1)} %get-tuple-element.63.refs_2_, ...), custom_call_target="tpu_custom_call" | custom-call | flops 1572864 | bytes 1024 | tf_op jit(solution)/shard_map/pallas_call | solution.py:336
  114.5 9.3 %shard_map.75 = bf16[8,208,128]{2,1,0:T(8,128)(2,1)S(1)} custom-call(bf16[3,128,1024]{2,1,0:T(8,128)(2,1)S(1)} %get-tuple-element.44.q_ref, bf16[256,384]{1,0:T(8,128)(2,1)S(1)} %collective-permute-done.13.refs_0_, bf16[256,384]{1,0:T(8,128)(2,1)S(1)} %collective-permute-done.14.refs_1_, f32[16,1024]{1,0:T(8,128)S(1)} %get-tuple-element.65.refs_2_, ...), custom_call_target="tpu_custom_call" | custom-call | flops 1572864 | bytes 1024 | tf_op jit(solution)/shard_map/pallas_call | solution.py:336
  123.7 10.5 %all_to_all.16.parts_ref = bf16[8,208,128]{2,1,0:T(8,128)(2,1)S(1)} all-to-all(bf16[8,208,128]{2,1,0:T(8,128)(2,1)S(1)} %shard_map.75), channel_id=1, replica_groups=mesh['zq'=4,'zc'=2,'xl'=2,'xh'=2,'y'=4,'core'=2] {'zc','y'}, dimensions={0} | all-to-all | bytes 851968 | tf_op jit(solution)/shard_map/all_to_all | solution.py:409
  134.2 1.2 shard_map.76
  (31 shorter events, 0.2 us)
Async XLA Ops:
  0.0 15.2 %copy-start = (bf16[768,2304]{1,0:T(8,128)(2,1)S(1)}, bf16[768,2304]{1,0:T(8,128)(2,1)}, u32[]{:S(2)}) copy-start(bf16[768,2304]{1,0:T(8,128)(2,1)} %w_ref.6) | copy-start | bytes 10616836
  4.0 14.0 %collective-permute-start.2 = (bf16[1,768]{1,0:T(2,128)(2,1)}, bf16[1,768]{1,0:T(2,128)(2,1)S(1)}, u32[]{:S(2)}, u32[]{:S(2)}) collective-permute-start(bf16[1,768]{1,0:T(2,128)(2,1)} %get-tuple-element.40), channel_id=1, source_target_pairs={{0,17},{1,18},{2,19},{3,20},{4,21},{5,22},{6,23},{7,24},{8,25},{9,... | collective-permute-start | bytes 4616 | tf_op jit(solution)/shard_map/ppermute | solution.py:42
  9.5 8.5 %collective-permute-start = (bf16[16,768]{1,0:T(8,128)(2,1)}, bf16[16,768]{1,0:T(8,128)(2,1)S(1)}, u32[]{:S(2)}, u32[]{:S(2)}) collective-permute-start(bf16[16,768]{1,0:T(8,128)(2,1)} %get-tuple-element.38), channel_id=1, source_target_pairs={{0,16},{16,32},{32,48},{48,64},{64,80},{80,96},{96,112},{112,128},... | collective-permute-start | bytes 73736 | tf_op jit(solution)/shard_map/ppermute | solution.py:36
  13.0 5.0 %collective-permute-start.1 = (bf16[32,768]{1,0:T(8,128)(2,1)}, bf16[32,768]{1,0:T(8,128)(2,1)S(1)}, u32[]{:S(2)}, u32[]{:S(2)}) collective-permute-start(bf16[32,768]{1,0:T(8,128)(2,1)} %get-tuple-element.39), channel_id=1, source_target_pairs={{0,1},{1,2},{2,3},{3,4},{4,5},{5,6},{6,7},{7,8},{8,9},{9,10},{10,1... | collective-permute-start | bytes 147464 | tf_op jit(solution)/shard_map/ppermute | solution.py:36
  15.2 1.1 copy-start.4
  16.4 1.7 %copy-start.2 = (f32[9,1536]{1,0:T(8,128)S(1)}, f32[9,1536]{1,0:T(8,128)}, u32[]{:S(2)}) copy-start(f32[9,1536]{1,0:T(8,128)} %pool_ref.2) | copy-start | bytes 165892
  18.0 18.9 %copy-start.3 = (f32[9,768]{1,0:T(8,128)S(1)}, f32[9,768]{1,0:T(8,128)}, u32[]{:S(2)}) copy-start(f32[9,768]{1,0:T(8,128)} %pool_ref.3) | copy-start | bytes 82948
  28.6 13.3 %collective-permute-start.5 = (bf16[128,384]{1,0:T(8,128)(2,1)S(1)}, bf16[128,384]{1,0:T(8,128)(2,1)S(1)}, u32[]{:S(2)}, u32[]{:S(2)}) collective-permute-start(bf16[128,384]{1,0:T(8,128)(2,1)S(1)} %bitcast.1), channel_id=1, source_target_pairs={{0,192},{64,0},{128,64},{192,128},{1,193},{65,1},{129,65},{193,129... | collective-permute-start | bytes 294920 | tf_op jit(solution)/shard_map/ppermute | solution.py:25
  33.7 8.2 %collective-permute-start.4 = (bf16[128,384]{1,0:T(8,128)(2,1)S(1)}, bf16[128,384]{1,0:T(8,128)(2,1)S(1)}, u32[]{:S(2)}, u32[]{:S(2)}) collective-permute-start(bf16[128,384]{1,0:T(8,128)(2,1)S(1)} %bitcast.2), channel_id=1, source_target_pairs={{0,64},{64,128},{128,192},{192,0},{1,65},{65,129},{129,193},{193,1... | collective-permute-start | bytes 294920 | tf_op jit(solution)/shard_map/ppermute | solution.py:25
  33.7 8.1 %collective-permute-start.3 = (bf16[128,384]{1,0:T(8,128)(2,1)S(1)}, bf16[128,384]{1,0:T(8,128)(2,1)S(1)}, u32[]{:S(2)}, u32[]{:S(2)}) collective-permute-start(bf16[128,384]{1,0:T(8,128)(2,1)S(1)} %bitcast.3), channel_id=1, source_target_pairs={{0,128},{64,192},{128,0},{192,64},{1,129},{65,193},{129,1},{193,65... | collective-permute-start | bytes 294920 | tf_op jit(solution)/shard_map/ppermute | solution.py:25
  38.3 10.1 %all-to-all-start.1 = ((bf16[8,192,128]{2,1,0:T(8,128)(2,1)}), bf16[8,192,128]{2,1,0:T(8,128)(2,1)S(1)}, u32[]{:S(2)}, u32[]{:S(2)}) async-start(bf16[8,192,128]{2,1,0:T(8,128)(2,1)} %shard_map.67), calls=%async_computation.1 | async-start | bytes 786432 | tf_op jit(solution)/shard_map/all_to_all | solution.py:394
  41.9 9.8 %collective-permute-start.8 = (bf16[512,384]{1,0:T(8,128)(2,1)S(1)}, bf16[512,384]{1,0:T(8,128)(2,1)S(1)}, u32[]{:S(2)}, u32[]{:S(2)}) collective-permute-start(bf16[512,384]{1,0:T(8,128)(2,1)S(1)} %constant_dynamic-update-slice_fusion.refs_0_), channel_id=1, source_target_pairs={{0,1},{1,0},{2,3},{3,2},{4,5},{5,4},{6,7},{7,6},{8,9},{9,8},{10,11... | collective-permute-start | bytes 1179656 | tf_op jit(solution)/shard_map/ppermute | solution.py:25
  46.0 15.0 %collective-permute-start.7 = (bf16[512,384]{1,0:T(8,128)(2,1)S(1)}, bf16[512,384]{1,0:T(8,128)(2,1)S(1)}, u32[]{:S(2)}, u32[]{:S(2)}) collective-permute-start(bf16[512,384]{1,0:T(8,128)(2,1)S(1)} %constant_dynamic-update-slice_fusion.refs_0_), channel_id=1, source_target_pairs={{0,24},{16,0},{8,16},{24,8},{1,25},{17,1},{9,17},{25,9},{2,26},{18... | collective-permute-start | bytes 1179656 | tf_op jit(solution)/shard_map/ppermute | solution.py:31
  47.4 13.5 %collective-permute-start.6 = (bf16[512,384]{1,0:T(8,128)(2,1)S(1)}, bf16[512,384]{1,0:T(8,128)(2,1)S(1)}, u32[]{:S(2)}, u32[]{:S(2)}) collective-permute-start(bf16[512,384]{1,0:T(8,128)(2,1)S(1)} %constant_dynamic-update-slice_fusion.refs_0_), channel_id=1, source_target_pairs={{0,16},{16,8},{8,24},{24,0},{1,17},{17,9},{9,25},{25,1},{2,18},{18... | collective-permute-start | bytes 1179656 | tf_op jit(solution)/shard_map/ppermute | solution.py:31
  60.9 15.7 %collective-permute-start.12 = (bf16[512,384]{1,0:T(8,128)(2,1)S(1)}, bf16[512,384]{1,0:T(8,128)(2,1)S(1)}, u32[]{:S(2)}, u32[]{:S(2)}) collective-permute-start(bf16[512,384]{1,0:T(8,128)(2,1)S(1)} %collective-permute-done.6.refs_0_), channel_id=1, source_target_pairs={{0,1},{1,0},{2,3},{3,2},{4,5},{5,4},{6,7},{7,6},{8,9},{9,8},{10,11... | collective-permute-start | bytes 1179656 | tf_op jit(solution)/shard_map/ppermute | solution.py:25
  63.9 31.0 %collective-permute-start.11 = (bf16[512,384]{1,0:T(8,128)(2,1)S(1)}, bf16[512,384]{1,0:T(8,128)(2,1)S(1)}, u32[]{:S(2)}, u32[]{:S(2)}) collective-permute-start(bf16[512,384]{1,0:T(8,128)(2,1)S(1)} %collective-permute-done.7.refs_0_), channel_id=1, source_target_pairs={{0,1},{1,0},{2,3},{3,2},{4,5},{5,4},{6,7},{7,6},{8,9},{9,8},{10,11... | collective-permute-start | bytes 1179656 | tf_op jit(solution)/shard_map/ppermute | solution.py:25
  64.1 40.1 %collective-permute-start.10 = (bf16[256,384]{1,0:T(8,128)(2,1)S(1)}, bf16[256,384]{1,0:T(8,128)(2,1)S(1)}, u32[]{:S(2)}, u32[]{:S(2)}) collective-permute-start(bf16[256,384]{1,0:T(8,128)(2,1)S(1)} %slice.7), channel_id=1, source_target_pairs={{0,24},{16,0},{8,16},{24,8},{1,25},{17,1},{9,17},{25,9},{2,26},{18... | collective-permute-start | bytes 589832 | tf_op jit(solution)/shard_map/ppermute | solution.py:31
  67.4 36.7 %collective-permute-start.9 = (bf16[256,384]{1,0:T(8,128)(2,1)S(1)}, bf16[256,384]{1,0:T(8,128)(2,1)S(1)}, u32[]{:S(2)}, u32[]{:S(2)}) collective-permute-start(bf16[256,384]{1,0:T(8,128)(2,1)S(1)} %slice.6), channel_id=1, source_target_pairs={{0,16},{16,8},{8,24},{24,0},{1,17},{17,9},{9,25},{25,1},{2,18},{18... | collective-permute-start | bytes 589832 | tf_op jit(solution)/shard_map/ppermute | solution.py:31
  104.2 10.3 %collective-permute-start.13 = (bf16[256,384]{1,0:T(8,128)(2,1)S(1)}, bf16[256,384]{1,0:T(8,128)(2,1)S(1)}, u32[]{:S(2)}, u32[]{:S(2)}) collective-permute-start(bf16[256,384]{1,0:T(8,128)(2,1)S(1)} %collective-permute-done.9.refs_0_), channel_id=1, source_target_pairs={{0,1},{1,0},{2,3},{3,2},{4,5},{5,4},{6,7},{7,6},{8,9},{9,8},{10,11... | collective-permute-start | bytes 589832 | tf_op jit(solution)/shard_map/ppermute | solution.py:25
  104.9 9.5 %collective-permute-start.14 = (bf16[256,384]{1,0:T(8,128)(2,1)S(1)}, bf16[256,384]{1,0:T(8,128)(2,1)S(1)}, u32[]{:S(2)}, u32[]{:S(2)}) collective-permute-start(bf16[256,384]{1,0:T(8,128)(2,1)S(1)} %collective-permute-done.10.refs_1_), channel_id=1, source_target_pairs={{0,1},{1,0},{2,3},{3,2},{4,5},{5,4},{6,7},{7,6},{8,9},{9,8},{10,11... | collective-permute-start | bytes 589832 | tf_op jit(solution)/shard_map/ppermute | solution.py:25
  114.5 19.8 %copy-start.1 = (bf16[768,768]{1,0:T(8,128)(2,1)S(1)}, bf16[768,768]{1,0:T(8,128)(2,1)}, u32[]{:S(2)}) copy-start(bf16[768,768]{1,0:T(8,128)(2,1)} %w_ref.7) | copy-start | bytes 3538948

commit v3 on v2

--- a/solution.py
+++ b/solution.py
@@ -66,18 +66,10 @@
     return jnp.concatenate(picked, 1)
 
 
-def tokens_kernel(patches_ref, gain_ref, tokens_ref, column_ref, row_ref, corner_ref, patches, gains, plain, sems):
-    rows, cols, width = patches.shape
-    copies = [
-        pltpu.make_async_copy(patches_ref, patches, sems.at[0]),
-        pltpu.make_async_copy(gain_ref, gains, sems.at[1]),
-    ]
-    for copy in copies:
-        copy.start()
-    for copy in copies:
-        copy.wait()
-    keep(plain, patches[...].astype(f32).reshape(rows * cols, width))
-    gain = gains[...].reshape(1, width)
+def tokens_kernel(patches_ref, gain_ref, tokens_ref, column_ref, row_ref, corner_ref, plain):
+    rows, cols, width = patches_ref.shape
+    keep(plain, patches_ref[...].astype(f32).reshape(rows * cols, width))
+    gain = gain_ref[...].reshape(1, width)
     last = [None] * cols
     for place, c in enumerate(ORDER):
         parts = [every_nth(plain, cols * r + c, 4 * cols) for r in range(4)]
@@ -89,25 +81,16 @@
     corner_ref[...] = last[-1].astype(bf16)
 
 
-def whole(shape):
-    return pl.BlockSpec(shape, lambda *_: (0,) * len(shape))
-
-
 def normalised_tokens(patches, gain):
     rows, cols, width = patches.shape
     shapes = [(rows * cols, width), (rows, width), (cols, width), (1, width)]
     return pl.pallas_call(
         tokens_kernel,
-        in_specs=[pl.BlockSpec(memory_space=pl.ANY)] * 2,
+        in_specs=[pl.BlockSpec(memory_space=pltpu.VMEM)] * 2,
         out_specs=[pl.BlockSpec(memory_space=pltpu.VMEM)] * 4,
         out_shape=[jax.ShapeDtypeStruct(s, bf16) for s in shapes],
-        scratch_shapes=[
-            pltpu.VMEM(patches.shape, bf16),
-            pltpu.VMEM(gain.shape, f32),
-            pltpu.VMEM((width // 128, rows * cols, 128), f32),
-            pltpu.SemaphoreType.DMA((2,)),
-        ],
-        compiler_params=pltpu.CompilerParams(vmem_limit_bytes=57 * 2**20),
+        scratch_shapes=[pltpu.VMEM((width // 128, rows * cols, 128), f32)],
+        compiler_params=pltpu.CompilerParams(vmem_limit_bytes=16 * 2**20),
         cost_estimate=pl.CostEstimate(flops=4_000_000_000, bytes_accessed=1_000_000, transcendentals=0),
     )(patches, gain)
 

time: 137 us -> 136 us (level)
  Pallas kernels: 76.3 us -> 74.2 us
    ppermute x4, starting transfers between devices: 4.83 us -> 8.89 us  [shifted_x(): return lax.ppermute(block, ('xl', 'xh'), route)]
    ppermute x8, starting transfers between devices: 16.6 us -> 12.9 us  [shifted(): lax.ppermute(block, axis, [(i, (i + distance) % count) for i in range(cou...]
    pallas_call x1, Pallas kernels: 3.95 us -> 1.76 us  [normalised_tokens(): pl.pallas_call(tokens_kernel, in_specs=[pl.BlockSpec(memory_space=pltpu.V...]
    ppermute x8, waiting for transfers between devices: 0.02 us -> 1.7 us  [shifted(): lax.ppermute(block, axis, [(i, (i + distance) % count) for i in range(cou...]
where the time goes in v3:
time: 136 us; the launch traced here: 135 us
  Pallas kernels  74.2 us (55%)
  starting transfers between devices  36.4 us (27%)
  blocking collectives  20.3 us (15%)
  local copies, waits for them, and re-layouts  2.12 us (2%)
  waiting for transfers between devices  1.72 us (1%)
    pallas_call x8, Pallas kernels, attend(): pl.pallas_call(functools.partial(attend_kernel, first, last, qb, len(bloc...  67.6 us
    ppermute x8, starting transfers between devices, shifted(): lax.ppermute(block, axis, [(i, (i + distance) % count) for i in range(cou...  12.9 us
    all_to_all x1, blocking collectives, on_device(): parts = lax.all_to_all(partial, ('zc', 'y'), 0, 0, tiled=True)  10.5 us
    all_to_all x1, blocking collectives, on_device(): own = lax.all_to_all(flat, 'y', 0, 0, tiled=True).reshape(-1, 2 * WIDE)  9.75 us
    ppermute x4, starting transfers between devices, shifted_x(): return lax.ppermute(block, ('xl', 'xh'), route)  8.89 us
    ppermute x2, starting transfers between devices, passed_along(): return lax.ppermute(block, axis, [(i - 1, i) for i in range(1, count)])  5.71 us
    ppermute x1, starting transfers between devices, corner(): return lax.ppermute(block, AXES, route)  5.52 us
    all_to_all x1, starting transfers between devices, on_device(): every_query = lax.all_to_all(turned, ('zc', 'y'), 0, 0, tiled=True)  3.45 us
  transfers between devices with their start and end apart: 16, of which 1 were waited for; matrix products, arithmetic and copies ran while one was open for 0% of the time, Pallas kernels for 45%

profile of v3, /device:TPU:1, one launch (start us, length us, event | category | flops | bytes accessed | tf_op | source)
XLA Modules:
  0.0 135.0 jit_solution(5988437302157941857)
XLA Ops:
  0.0 1.3 copy-done.4
  1.3 0.7 copy-done.5
  2.0 1.8 %shard_map.64 = (bf16[512,768]{1,0:T(8,128)(2,1)S(1)}, bf16[32,768]{1,0:T(8,128)(2,1)S(1)}, bf16[16,768]{1,0:T(8,128)(2,1)S(1)}, bf16[1,768]{1,0:T(2,128)(2,1)S(1)}) custom-call(bf16[32,16,768]{2,1,0:T(8,128)(2,1)S(1)} %copy-done.4, f32[768]{0:T(1024)S(1)} %copy-done.5), custom_call_target="tpu_custom_call" | custom-call | flops 4000000000 | bytes 1000000 | tf_op jit(solution)/shard_map/pallas_call | solution.py:87
  3.8 5.5 %collective-permute-start.2 = (bf16[1,768]{1,0:T(2,128)(2,1)S(1)}, bf16[1,768]{1,0:T(2,128)(2,1)S(1)}, u32[]{:S(2)}, u32[]{:S(2)}) collective-permute-start(bf16[1,768]{1,0:T(2,128)(2,1)S(1)} %get-tuple-element.40), channel_id=1, source_target_pairs={{0,17},{1,18},{2,19},{3,20},{4,21},{5,22},{6,23},{7,24},{8,25},{9,... | collective-permute-start | bytes 4616 | tf_op jit(solution)/shard_map/ppermute | solution.py:42
  9.3 3.5 %collective-permute-start = (bf16[16,768]{1,0:T(8,128)(2,1)S(1)}, bf16[16,768]{1,0:T(8,128)(2,1)S(1)}, u32[]{:S(2)}, u32[]{:S(2)}) collective-permute-start(bf16[16,768]{1,0:T(8,128)(2,1)S(1)} %get-tuple-element.38), channel_id=1, source_target_pairs={{0,16},{16,32},{32,48},{48,64},{64,80},{80,96},{96,112},{112,128},... | collective-permute-start | bytes 73736 | tf_op jit(solution)/shard_map/ppermute | solution.py:36
  12.8 2.2 %collective-permute-start.1 = (bf16[32,768]{1,0:T(8,128)(2,1)S(1)}, bf16[32,768]{1,0:T(8,128)(2,1)S(1)}, u32[]{:S(2)}, u32[]{:S(2)}) collective-permute-start(bf16[32,768]{1,0:T(8,128)(2,1)S(1)} %get-tuple-element.39), channel_id=1, source_target_pairs={{0,1},{1,2},{2,3},{3,4},{4,5},{5,6},{6,7},{7,8},{8,9},{9,10},{10,1... | collective-permute-start | bytes 147464 | tf_op jit(solution)/shard_map/ppermute | solution.py:36
  15.0 0.0 copy-start.2
  15.0 1.6 %shard_map.65 = (bf16[512,768]{1,0:T(8,128)(2,1)S(1)}, bf16[352,1536]{1,0:T(8,128)(2,1)S(1)}) custom-call(bf16[512,768]{1,0:T(8,128)(2,1)S(1)} %get-tuple-element.36.tokens_ref, bf16[768,2304]{1,0:T(8,128)(2,1)S(1)} %copy-done), custom_call_target="tpu_custom_call" | custom-call | flops 1500000000 | bytes 4000000 | tf_op jit(solution)/shard_map/pallas_call | solution.py:110
  16.7 0.7 shard_map.66
  17.4 9.8 %all_to_all.15 = bf16[4,32,384]{2,1,0:T(8,128)(2,1)S(1)} all-to-all(bf16[4,32,384]{2,1,0:T(8,128)(2,1)S(1)} %shard_map.66), channel_id=1, replica_groups=mesh['zq'=4,'zc'=2,'xl'=2,'xh'=2,'y'=4,'core'=2] {'y'}, dimensions={0} | all-to-all | bytes 196608 | tf_op jit(solution)/shard_map/all_to_all | solution.py:372
  27.2 5.1 %collective-permute-start.5 = (bf16[128,384]{1,0:T(8,128)(2,1)S(1)}, bf16[128,384]{1,0:T(8,128)(2,1)S(1)}, u32[]{:S(2)}, u32[]{:S(2)}) collective-permute-start(bf16[128,384]{1,0:T(8,128)(2,1)S(1)} %bitcast.1), channel_id=1, source_target_pairs={{0,192},{64,0},{128,64},{192,128},{1,193},{65,1},{129,65},{193,129... | collective-permute-start | bytes 294920 | tf_op jit(solution)/shard_map/ppermute | solution.py:25
  32.3 3.3 %collective-permute-start.3 = (bf16[128,384]{1,0:T(8,128)(2,1)S(1)}, bf16[128,384]{1,0:T(8,128)(2,1)S(1)}, u32[]{:S(2)}, u32[]{:S(2)}) collective-permute-start(bf16[128,384]{1,0:T(8,128)(2,1)S(1)} %bitcast.3), channel_id=1, source_target_pairs={{0,128},{64,192},{128,0},{192,64},{1,129},{65,193},{129,1},{193,65... | collective-permute-start | bytes 294920 | tf_op jit(solution)/shard_map/ppermute | solution.py:25
  35.6 1.4 %shard_map.67 = bf16[8,192,128]{2,1,0:T(8,128)(2,1)} custom-call(bf16[512,768]{1,0:T(8,128)(2,1)S(1)} %get-tuple-element.42.own_ref, bf16[16,768]{1,0:T(8,128)(2,1)S(1)} %collective-permute-done.upper_ref, bf16[32,768]{1,0:T(8,128)(2,1)S(1)} %collective-permute-done.1.left_ref, bf16[1,768]{1,0:T(2,128)(2,1)S(1)} %collective-permute-done.2.corner_ref, ...), custom_call_target="tpu_custom_call" | custom-call | flops 200000000 | bytes 4000000 | tf_op jit(solution)/shard_map/pallas_call | solution.py:186
  36.9 3.5 %all-to-all-start.1 = ((bf16[8,192,128]{2,1,0:T(8,128)(2,1)}), bf16[8,192,128]{2,1,0:T(8,128)(2,1)S(1)}, u32[]{:S(2)}, u32[]{:S(2)}) async-start(bf16[8,192,128]{2,1,0:T(8,128)(2,1)} %shard_map.67), calls=%async_computation.1 | async-start | bytes 786432 | tf_op jit(solution)/shard_map/all_to_all | solution.py:377
  40.4 1.7 %collective-permute-done.3 = bf16[128,384]{1,0:T(8,128)(2,1)S(1)} collective-permute-done((bf16[128,384]{1,0:T(8,128)(2,1)S(1)}, bf16[128,384]{1,0:T(8,128)(2,1)S(1)}, u32[]{:S(2)}, u32[]{:S(2)}) %collective-permute-start.3) | collective-permute-done | bytes 98336 | tf_op jit(solution)/shard_map/ppermute | solution.py:25
  42.2 2.3 %collective-permute-start.8 = (bf16[512,384]{1,0:T(8,128)(2,1)S(1)}, bf16[512,384]{1,0:T(8,128)(2,1)S(1)}, u32[]{:S(2)}, u32[]{:S(2)}) collective-permute-start(bf16[512,384]{1,0:T(8,128)(2,1)S(1)} %constant_dynamic-update-slice_fusion.refs_0_), channel_id=1, source_target_pairs={{0,1},{1,0},{2,3},{3,2},{4,5},{5,4},{6,7},{7,6},{8,9},{9,8},{10,11... | collective-permute-start | bytes 1179656 | tf_op jit(solution)/shard_map/ppermute | solution.py:25
  44.5 4.7 %collective-permute-start.7 = (bf16[512,384]{1,0:T(8,128)(2,1)S(1)}, bf16[512,384]{1,0:T(8,128)(2,1)S(1)}, u32[]{:S(2)}, u32[]{:S(2)}) collective-permute-start(bf16[512,384]{1,0:T(8,128)(2,1)S(1)} %constant_dynamic-update-slice_fusion.refs_0_), channel_id=1, source_target_pairs={{0,24},{16,0},{8,16},{24,8},{1,25},{17,1},{9,17},{25,9},{2,26},{18... | collective-permute-start | bytes 1179656 | tf_op jit(solution)/shard_map/ppermute | solution.py:31
  49.2 3.3 %shard_map.68 = (f32[16,1024]{1,0:T(8,128)S(1)}, f32[192,1024]{1,0:T(8,128)S(1)}, bf16[3,128,1024]{2,1,0:T(8,128)(2,1)S(1)}) custom-call(bf16[8,192,128]{2,1,0:T(8,128)(2,1)S(1)} %all-to-all-done.1.q_ref, bf16[512,384]{1,0:T(8,128)(2,1)S(1)} %constant_dynamic-update-slice_fusion.refs_0_), custom_call_target="tpu_custom_call" | custom-call | flops 1572864 | bytes 1024 | tf_op jit(solution)/shard_map/pallas_call | solution.py:319
  52.6 9.2 %shard_map.69 = (f32[16,1024]{1,0:T(8,128)S(1)}, f32[192,1024]{1,0:T(8,128)S(1)}) custom-call(bf16[3,128,1024]{2,1,0:T(8,128)(2,1)S(1)} %get-tuple-element.44.q_ref, bf16[512,384]{1,0:T(8,128)(2,1)S(1)} %collective-permute-done.8.refs_0_, f32[16,1024]{1,0:T(8,128)S(1)} %get-tuple-element.45.refs_1_, f32[192,1024]{1,0:T(8,128)S(1)} %get-tuple-element.46.refs_2_), custom_call_target="tpu_custom_call" | custom-call | flops 1572864 | bytes 1024 | tf_op jit(solution)/shard_map/pallas_call | solution.py:319
  61.8 1.0 collective-permute-start.12
  62.7 0.1 collective-permute-start.11
  62.9 4.2 %collective-permute-start.10 = (bf16[256,384]{1,0:T(8,128)(2,1)S(1)}, bf16[256,384]{1,0:T(8,128)(2,1)S(1)}, u32[]{:S(2)}, u32[]{:S(2)}) collective-permute-start(bf16[256,384]{1,0:T(8,128)(2,1)S(1)} %slice.7), channel_id=1, source_target_pairs={{0,24},{16,0},{8,16},{24,8},{1,25},{17,1},{9,17},{25,9},{2,26},{18... | collective-permute-start | bytes 589832 | tf_op jit(solution)/shard_map/ppermute | solution.py:31
  67.0 9.2 %shard_map.70 = (f32[16,1024]{1,0:T(8,128)S(1)}, f32[192,1024]{1,0:T(8,128)S(1)}) custom-call(bf16[3,128,1024]{2,1,0:T(8,128)(2,1)S(1)} %get-tuple-element.44.q_ref, bf16[512,384]{1,0:T(8,128)(2,1)S(1)} %collective-permute-done.6.refs_0_, f32[16,1024]{1,0:T(8,128)S(1)} %get-tuple-element.51.refs_1_, f32[192,1024]{1,0:T(8,128)S(1)} %get-tuple-element.52.refs_2_), custom_call_target="tpu_custom_call" | custom-call | flops 1572864 | bytes 1024 | tf_op jit(solution)/shard_map/pallas_call | solution.py:319
  76.2 9.2 %shard_map.71 = (f32[16,1024]{1,0:T(8,128)S(1)}, f32[192,1024]{1,0:T(8,128)S(1)}) custom-call(bf16[3,128,1024]{2,1,0:T(8,128)(2,1)S(1)} %get-tuple-element.44.q_ref, bf16[512,384]{1,0:T(8,128)(2,1)S(1)} %collective-permute-done.12.refs_0_, f32[16,1024]{1,0:T(8,128)S(1)} %get-tuple-element.53.refs_1_, f32[192,1024]{1,0:T(8,128)S(1)} %get-tuple-element.54.refs_2_), custom_call_target="tpu_custom_call" | custom-call | flops 1572864 | bytes 1024 | tf_op jit(solution)/shard_map/pallas_call | solution.py:319
  85.4 9.2 %shard_map.72 = (f32[16,1024]{1,0:T(8,128)S(1)}, f32[192,1024]{1,0:T(8,128)S(1)}) custom-call(bf16[3,128,1024]{2,1,0:T(8,128)(2,1)S(1)} %get-tuple-element.44.q_ref, bf16[512,384]{1,0:T(8,128)(2,1)S(1)} %collective-permute-done.7.refs_0_, f32[16,1024]{1,0:T(8,128)S(1)} %get-tuple-element.55.refs_1_, f32[192,1024]{1,0:T(8,128)S(1)} %get-tuple-element.56.refs_2_), custom_call_target="tpu_custom_call" | custom-call | flops 1572864 | bytes 1024 | tf_op jit(solution)/shard_map/pallas_call | solution.py:319
  94.6 9.2 %shard_map.73 = (f32[16,1024]{1,0:T(8,128)S(1)}, f32[192,1024]{1,0:T(8,128)S(1)}) custom-call(bf16[3,128,1024]{2,1,0:T(8,128)(2,1)S(1)} %get-tuple-element.44.q_ref, bf16[512,384]{1,0:T(8,128)(2,1)S(1)} %collective-permute-done.11.refs_0_, f32[16,1024]{1,0:T(8,128)S(1)} %get-tuple-element.57.refs_1_, f32[192,1024]{1,0:T(8,128)S(1)} %get-tuple-element.58.refs_2_), custom_call_target="tpu_custom_call" | custom-call | flops 1572864 | bytes 1024 | tf_op jit(solution)/shard_map/pallas_call | solution.py:319
  103.8 0.8 collective-permute-start.13
  104.6 0.3 collective-permute-start.14
  104.9 9.2 %shard_map.74 = (f32[16,1024]{1,0:T(8,128)S(1)}, f32[192,1024]{1,0:T(8,128)S(1)}) custom-call(bf16[3,128,1024]{2,1,0:T(8,128)(2,1)S(1)} %get-tuple-element.44.q_ref, bf16[256,384]{1,0:T(8,128)(2,1)S(1)} %collective-permute-done.9.refs_0_, bf16[256,384]{1,0:T(8,128)(2,1)S(1)} %collective-permute-done.10.refs_1_, f32[16,1024]{1,0:T(8,128)S(1)} %get-tuple-element.63.refs_2_, ...), custom_call_target="tpu_custom_call" | custom-call | flops 1572864 | bytes 1024 | tf_op jit(solution)/shard_map/pallas_call | solution.py:319
  114.1 9.3 %shard_map.75 = bf16[8,208,128]{2,1,0:T(8,128)(2,1)S(1)} custom-call(bf16[3,128,1024]{2,1,0:T(8,128)(2,1)S(1)} %get-tuple-element.44.q_ref, bf16[256,384]{1,0:T(8,128)(2,1)S(1)} %collective-permute-done.13.refs_0_, bf16[256,384]{1,0:T(8,128)(2,1)S(1)} %collective-permute-done.14.refs_1_, f32[16,1024]{1,0:T(8,128)S(1)} %get-tuple-element.65.refs_2_, ...), custom_call_target="tpu_custom_call" | custom-call | flops 1572864 | bytes 1024 | tf_op jit(solution)/shard_map/pallas_call | solution.py:319
  123.3 10.5 %all_to_all.16.parts_ref = bf16[8,208,128]{2,1,0:T(8,128)(2,1)S(1)} all-to-all(bf16[8,208,128]{2,1,0:T(8,128)(2,1)S(1)} %shard_map.75), channel_id=1, replica_groups=mesh['zq'=4,'zc'=2,'xl'=2,'xh'=2,'y'=4,'core'=2] {'zc','y'}, dimensions={0} | all-to-all | bytes 851968 | tf_op jit(solution)/shard_map/all_to_all | solution.py:392
  133.9 1.2 shard_map.76
  (33 shorter events, 0.2 us)
Async XLA Ops:
  0.0 15.0 %copy-start = (bf16[768,2304]{1,0:T(8,128)(2,1)S(1)}, bf16[768,2304]{1,0:T(8,128)(2,1)}, u32[]{:S(2)}) copy-start(bf16[768,2304]{1,0:T(8,128)(2,1)} %w_ref.6) | copy-start | bytes 10616836
  0.0 1.3 copy-start.4
  1.3 0.7 copy-start.5
  3.8 12.9 %collective-permute-start.2 = (bf16[1,768]{1,0:T(2,128)(2,1)S(1)}, bf16[1,768]{1,0:T(2,128)(2,1)S(1)}, u32[]{:S(2)}, u32[]{:S(2)}) collective-permute-start(bf16[1,768]{1,0:T(2,128)(2,1)S(1)} %get-tuple-element.40), channel_id=1, source_target_pairs={{0,17},{1,18},{2,19},{3,20},{4,21},{5,22},{6,23},{7,24},{8,25},{9,... | collective-permute-start | bytes 4616 | tf_op jit(solution)/shard_map/ppermute | solution.py:42
  9.3 7.4 %collective-permute-start = (bf16[16,768]{1,0:T(8,128)(2,1)S(1)}, bf16[16,768]{1,0:T(8,128)(2,1)S(1)}, u32[]{:S(2)}, u32[]{:S(2)}) collective-permute-start(bf16[16,768]{1,0:T(8,128)(2,1)S(1)} %get-tuple-element.38), channel_id=1, source_target_pairs={{0,16},{16,32},{32,48},{48,64},{64,80},{80,96},{96,112},{112,128},... | collective-permute-start | bytes 73736 | tf_op jit(solution)/shard_map/ppermute | solution.py:36
  12.8 3.9 %collective-permute-start.1 = (bf16[32,768]{1,0:T(8,128)(2,1)S(1)}, bf16[32,768]{1,0:T(8,128)(2,1)S(1)}, u32[]{:S(2)}, u32[]{:S(2)}) collective-permute-start(bf16[32,768]{1,0:T(8,128)(2,1)S(1)} %get-tuple-element.39), channel_id=1, source_target_pairs={{0,1},{1,2},{2,3},{3,4},{4,5},{5,6},{6,7},{7,8},{8,9},{9,10},{10,1... | collective-permute-start | bytes 147464 | tf_op jit(solution)/shard_map/ppermute | solution.py:36
  15.0 1.7 %copy-start.2 = (f32[9,1536]{1,0:T(8,128)S(1)}, f32[9,1536]{1,0:T(8,128)}, u32[]{:S(2)}) copy-start(f32[9,1536]{1,0:T(8,128)} %pool_ref.2) | copy-start | bytes 165892
  16.7 18.8 %copy-start.3 = (f32[9,768]{1,0:T(8,128)S(1)}, f32[9,768]{1,0:T(8,128)}, u32[]{:S(2)}) copy-start(f32[9,768]{1,0:T(8,128)} %pool_ref.3) | copy-start | bytes 82948
  27.2 15.0 %collective-permute-start.5 = (bf16[128,384]{1,0:T(8,128)(2,1)S(1)}, bf16[128,384]{1,0:T(8,128)(2,1)S(1)}, u32[]{:S(2)}, u32[]{:S(2)}) collective-permute-start(bf16[128,384]{1,0:T(8,128)(2,1)S(1)} %bitcast.1), channel_id=1, source_target_pairs={{0,192},{64,0},{128,64},{192,128},{1,193},{65,1},{129,65},{193,129... | collective-permute-start | bytes 294920 | tf_op jit(solution)/shard_map/ppermute | solution.py:25
  32.3 9.8 %collective-permute-start.4 = (bf16[128,384]{1,0:T(8,128)(2,1)S(1)}, bf16[128,384]{1,0:T(8,128)(2,1)S(1)}, u32[]{:S(2)}, u32[]{:S(2)}) collective-permute-start(bf16[128,384]{1,0:T(8,128)(2,1)S(1)} %bitcast.2), channel_id=1, source_target_pairs={{0,64},{64,128},{128,192},{192,0},{1,65},{65,129},{129,193},{193,1... | collective-permute-start | bytes 294920 | tf_op jit(solution)/shard_map/ppermute | solution.py:25
  32.3 9.8 %collective-permute-start.3 = (bf16[128,384]{1,0:T(8,128)(2,1)S(1)}, bf16[128,384]{1,0:T(8,128)(2,1)S(1)}, u32[]{:S(2)}, u32[]{:S(2)}) collective-permute-start(bf16[128,384]{1,0:T(8,128)(2,1)S(1)} %bitcast.3), channel_id=1, source_target_pairs={{0,128},{64,192},{128,0},{192,64},{1,129},{65,193},{129,1},{193,65... | collective-permute-start | bytes 294920 | tf_op jit(solution)/shard_map/ppermute | solution.py:25
  36.9 12.3 %all-to-all-start.1 = ((bf16[8,192,128]{2,1,0:T(8,128)(2,1)}), bf16[8,192,128]{2,1,0:T(8,128)(2,1)S(1)}, u32[]{:S(2)}, u32[]{:S(2)}) async-start(bf16[8,192,128]{2,1,0:T(8,128)(2,1)} %shard_map.67), calls=%async_computation.1 | async-start | bytes 786432 | tf_op jit(solution)/shard_map/all_to_all | solution.py:377
  42.2 10.4 %collective-permute-start.8 = (bf16[512,384]{1,0:T(8,128)(2,1)S(1)}, bf16[512,384]{1,0:T(8,128)(2,1)S(1)}, u32[]{:S(2)}, u32[]{:S(2)}) collective-permute-start(bf16[512,384]{1,0:T(8,128)(2,1)S(1)} %constant_dynamic-update-slice_fusion.refs_0_), channel_id=1, source_target_pairs={{0,1},{1,0},{2,3},{3,2},{4,5},{5,4},{6,7},{7,6},{8,9},{9,8},{10,11... | collective-permute-start | bytes 1179656 | tf_op jit(solution)/shard_map/ppermute | solution.py:25
  44.5 17.2 %collective-permute-start.7 = (bf16[512,384]{1,0:T(8,128)(2,1)S(1)}, bf16[512,384]{1,0:T(8,128)(2,1)S(1)}, u32[]{:S(2)}, u32[]{:S(2)}) collective-permute-start(bf16[512,384]{1,0:T(8,128)(2,1)S(1)} %constant_dynamic-update-slice_fusion.refs_0_), channel_id=1, source_target_pairs={{0,24},{16,0},{8,16},{24,8},{1,25},{17,1},{9,17},{25,9},{2,26},{18... | collective-permute-start | bytes 1179656 | tf_op jit(solution)/shard_map/ppermute | solution.py:31
  49.2 12.5 %collective-permute-start.6 = (bf16[512,384]{1,0:T(8,128)(2,1)S(1)}, bf16[512,384]{1,0:T(8,128)(2,1)S(1)}, u32[]{:S(2)}, u32[]{:S(2)}) collective-permute-start(bf16[512,384]{1,0:T(8,128)(2,1)S(1)} %constant_dynamic-update-slice_fusion.refs_0_), channel_id=1, source_target_pairs={{0,16},{16,8},{8,24},{24,0},{1,17},{17,9},{9,25},{25,1},{2,18},{18... | collective-permute-start | bytes 1179656 | tf_op jit(solution)/shard_map/ppermute | solution.py:31
  61.8 14.5 %collective-permute-start.12 = (bf16[512,384]{1,0:T(8,128)(2,1)S(1)}, bf16[512,384]{1,0:T(8,128)(2,1)S(1)}, u32[]{:S(2)}, u32[]{:S(2)}) collective-permute-start(bf16[512,384]{1,0:T(8,128)(2,1)S(1)} %collective-permute-done.6.refs_0_), channel_id=1, source_target_pairs={{0,1},{1,0},{2,3},{3,2},{4,5},{5,4},{6,7},{7,6},{8,9},{9,8},{10,11... | collective-permute-start | bytes 1179656 | tf_op jit(solution)/shard_map/ppermute | solution.py:25
  62.7 31.9 %collective-permute-start.11 = (bf16[512,384]{1,0:T(8,128)(2,1)S(1)}, bf16[512,384]{1,0:T(8,128)(2,1)S(1)}, u32[]{:S(2)}, u32[]{:S(2)}) collective-permute-start(bf16[512,384]{1,0:T(8,128)(2,1)S(1)} %collective-permute-done.7.refs_0_), channel_id=1, source_target_pairs={{0,1},{1,0},{2,3},{3,2},{4,5},{5,4},{6,7},{7,6},{8,9},{9,8},{10,11... | collective-permute-start | bytes 1179656 | tf_op jit(solution)/shard_map/ppermute | solution.py:25
  62.9 40.9 %collective-permute-start.10 = (bf16[256,384]{1,0:T(8,128)(2,1)S(1)}, bf16[256,384]{1,0:T(8,128)(2,1)S(1)}, u32[]{:S(2)}, u32[]{:S(2)}) collective-permute-start(bf16[256,384]{1,0:T(8,128)(2,1)S(1)} %slice.7), channel_id=1, source_target_pairs={{0,24},{16,0},{8,16},{24,8},{1,25},{17,1},{9,17},{25,9},{2,26},{18... | collective-permute-start | bytes 589832 | tf_op jit(solution)/shard_map/ppermute | solution.py:31
  67.0 36.7 %collective-permute-start.9 = (bf16[256,384]{1,0:T(8,128)(2,1)S(1)}, bf16[256,384]{1,0:T(8,128)(2,1)S(1)}, u32[]{:S(2)}, u32[]{:S(2)}) collective-permute-start(bf16[256,384]{1,0:T(8,128)(2,1)S(1)} %slice.6), channel_id=1, source_target_pairs={{0,16},{16,8},{8,24},{24,0},{1,17},{17,9},{9,25},{25,1},{2,18},{18... | collective-permute-start | bytes 589832 | tf_op jit(solution)/shard_map/ppermute | solution.py:31
  103.8 10.3 %collective-permute-start.13 = (bf16[256,384]{1,0:T(8,128)(2,1)S(1)}, bf16[256,384]{1,0:T(8,128)(2,1)S(1)}, u32[]{:S(2)}, u32[]{:S(2)}) collective-permute-start(bf16[256,384]{1,0:T(8,128)(2,1)S(1)} %collective-permute-done.9.refs_0_), channel_id=1, source_target_pairs={{0,1},{1,0},{2,3},{3,2},{4,5},{5,4},{6,7},{7,6},{8,9},{9,8},{10,11... | collective-permute-start | bytes 589832 | tf_op jit(solution)/shard_map/ppermute | solution.py:25
  104.6 9.5 %collective-permute-start.14 = (bf16[256,384]{1,0:T(8,128)(2,1)S(1)}, bf16[256,384]{1,0:T(8,128)(2,1)S(1)}, u32[]{:S(2)}, u32[]{:S(2)}) collective-permute-start(bf16[256,384]{1,0:T(8,128)(2,1)S(1)} %collective-permute-done.10.refs_1_), channel_id=1, source_target_pairs={{0,1},{1,0},{2,3},{3,2},{4,5},{5,4},{6,7},{7,6},{8,9},{9,8},{10,11... | collective-permute-start | bytes 589832 | tf_op jit(solution)/shard_map/ppermute | solution.py:25
  114.1 19.8 %copy-start.1 = (bf16[768,768]{1,0:T(8,128)(2,1)S(1)}, bf16[768,768]{1,0:T(8,128)(2,1)}, u32[]{:S(2)}) copy-start(bf16[768,768]{1,0:T(8,128)(2,1)} %w_ref.7) | copy-start | bytes 3538948

commit v4 on v3

--- a/solution.py
+++ b/solution.py
@@ -146,7 +146,8 @@
     return total
 
 
-def keyvals_kernel(own_ref, upper_ref, left_ref, corner_ref, w_ref, pool_ref, out_ref):
+def keyvals_kernel(here_ref, own_ref, upper_ref, left_ref, corner_ref, w_ref, pool_ref, *refs):
+    out_refs, parts = refs[:-1], refs[-1]
     halo_in = halo_tokens(upper_ref, left_ref, corner_ref)
     width = own_ref.shape[1] // 2
     both = []
@@ -161,9 +162,10 @@
     count = width // WIDE
     for g in range(count):
         lanes = slice(g * WIDE, (g + 1) * WIDE)
-        block = jnp.concatenate([p[:, lanes] for p in both], 1).astype(bf16)
-        for copy in range(out_ref.shape[0] // count):
-            out_ref[copy * count + g] = block
+        parts[g] = jnp.concatenate([p[:, lanes] for p in both], 1).astype(bf16)
+    here = here_ref[0]
+    for distance, out_ref in enumerate(out_refs):
+        out_ref[...] = parts[lax.rem(here + distance, count)]
 
 
 def queries_kernel(own_ref, upper_ref, left_ref, corner_ref, w_ref, pool_ref, out_ref):
@@ -182,15 +184,17 @@
             out_ref[copy * count + g] = block
 
 
-def pool_call(kernel, own, halo, w_qkv, taps, out_shape):
+def pool_call(kernel, own, halo, w_qkv, taps, out_shapes, scratch=(), scalars=()):
     return pl.pallas_call(
         kernel,
-        in_specs=[pl.BlockSpec(memory_space=pltpu.VMEM)] * (3 + len(halo)),
-        out_specs=pl.BlockSpec(memory_space=pltpu.VMEM),
-        out_shape=jax.ShapeDtypeStruct(out_shape, bf16),
+        in_specs=[pl.BlockSpec(memory_space=pltpu.SMEM)] * len(scalars)
+        + [pl.BlockSpec(memory_space=pltpu.VMEM)] * (3 + len(halo)),
+        out_specs=[pl.BlockSpec(memory_space=pltpu.VMEM)] * len(out_shapes),
+        out_shape=[jax.ShapeDtypeStruct(s, bf16) for s in out_shapes],
+        scratch_shapes=[pltpu.VMEM(s, bf16) for s in scratch],
         compiler_params=pltpu.CompilerParams(vmem_limit_bytes=24 * 2**20),
         cost_estimate=pl.CostEstimate(flops=200_000_000, bytes_accessed=4_000_000, transcendentals=0),
-    )(own, *halo, w_qkv, taps)
+    )(*scalars, own, *halo, w_qkv, taps)
 
 
 def pad_queries(q_ref, padded):
@@ -364,16 +368,19 @@
 
 
 def on_device(patches, norm_gain, w_qkv, pool_q, pool_kv, w_out):
+    here = [lax.axis_index("y").reshape(1)]
+    patches, here = lax.optimization_barrier((patches, here))
     tokens, last_column, last_row, last_token = normalised_tokens(patches, norm_gain)
     halo = (passed_along(last_row, ROW), passed_along(last_column, COL), corner(last_token))
     own_q, own_kv = project_own(tokens, w_qkv)
     groups = lax.axis_size("y")
-    flat = pool_call(keyvals_kernel, own_kv, halo, w_qkv, pool_kv, (groups, 32, 2 * WIDE))
-    own = lax.all_to_all(flat, "y", 0, 0, tiled=True).reshape(-1, 2 * WIDE)
+    part = (32, 2 * WIDE)
+    parts = pool_call(keyvals_kernel, own_kv, halo, w_qkv, pool_kv, [part] * groups, [(groups, *part)], here)
+    own = jnp.concatenate([parts[0]] + [shifted(p, "y", d) for d, p in enumerate(parts) if d], 0)
     tie = lax.optimization_barrier
     own, own_q = tie((own, own_q))
     line = [own, shifted(own, "zq", 2), shifted(own, "zq", 1), shifted(own, "zq", -1)]
-    turned = pool_call(queries_kernel, own_q, halo, w_qkv, pool_q, (2 * groups, WIDE, 128))
+    (turned,) = pool_call(queries_kernel, own_q, halo, w_qkv, pool_q, [(2 * groups, WIDE, 128)])
     every_query = lax.all_to_all(turned, ("zc", "y"), 0, 0, tiled=True)
     line = jnp.concatenate(line, 0)
     after, before = shifted_x(line, 1), shifted_x(line, -1)

time: 136 us -> 135 us (level)
  blocking collectives: 20.3 us -> 10.6 us
  starting transfers between devices: 36.4 us -> 42.1 us
  waiting for transfers between devices: 1.72 us -> 4.32 us
    all_to_all x1 -> x0, blocking collectives: 9.75 us -> none  [on_device(): own = lax.all_to_all(flat, 'y', 0, 0, tiled=True).reshape(-1, 2 * WIDE)]
    ppermute x8 -> x11, starting transfers between devices: 12.9 us -> 19.9 us  [shifted(): lax.ppermute(block, axis, [(i, (i + distance) % count) for i in range(cou...]
    ppermute x8 -> x11, waiting for transfers between devices: 1.7 us -> 4.3 us  [shifted(): lax.ppermute(block, axis, [(i, (i + distance) % count) for i in range(cou...]
    ppermute x4, starting transfers between devices: 8.89 us -> 7.41 us  [shifted_x(): return lax.ppermute(block, ('xl', 'xh'), route)]
  transfers between devices with their start and end apart: 16 -> 19, of which waited for: 1 -> 3; matrix products, arithmetic and copies ran while one was open for 0% -> 0% of each run, Pallas kernels for 45% -> 46%
where the time goes in v4:
time: 135 us; the launch traced here: 134 us
  Pallas kernels  74.4 us (55%)
  starting transfers between devices  42.1 us (31%)
  blocking collectives  10.6 us (8%)
  waiting for transfers between devices  4.32 us (3%)
  local copies, waits for them, and re-layouts  1.95 us (1%)
    pallas_call x8, Pallas kernels, attend(): pl.pallas_call(functools.partial(attend_kernel, first, last, qb, len(bloc...  67.8 us
    ppermute x11, starting transfers between devices, shifted(): lax.ppermute(block, axis, [(i, (i + distance) % count) for i in range(cou...  19.9 us
    all_to_all x1, blocking collectives, on_device(): parts = lax.all_to_all(partial, ('zc', 'y'), 0, 0, tiled=True)  10.6 us
    ppermute x4, starting transfers between devices, shifted_x(): return lax.ppermute(block, ('xl', 'xh'), route)  7.41 us
    ppermute x2, starting transfers between devices, passed_along(): return lax.ppermute(block, axis, [(i - 1, i) for i in range(1, count)])  5.71 us
    ppermute x1, starting transfers between devices, corner(): return lax.ppermute(block, AXES, route)  5.52 us
    ppermute x11, waiting for transfers between devices, shifted(): lax.ppermute(block, axis, [(i, (i + distance) % count) for i in range(cou...  4.3 us
    all_to_all x1, starting transfers between devices, on_device(): every_query = lax.all_to_all(turned, ('zc', 'y'), 0, 0, tiled=True)  3.58 us
  transfers between devices with their start and end apart: 19, of which 3 were waited for; matrix products, arithmetic and copies ran while one was open for 0% of the time, Pallas kernels for 46%

profile of v4, /device:TPU:1, one launch (start us, length us, event | category | flops | bytes accessed | tf_op | source)
XLA Modules:
  0.0 133.6 jit_solution(14959520736301403999)
XLA Ops:
  0.0 1.1 copy-done.4
  1.1 0.7 copy-done.5
  1.8 1.8 %shard_map.64 = (bf16[512,768]{1,0:T(8,128)(2,1)S(1)}, bf16[32,768]{1,0:T(8,128)(2,1)S(1)}, bf16[16,768]{1,0:T(8,128)(2,1)S(1)}, bf16[1,768]{1,0:T(2,128)(2,1)S(1)}) custom-call(bf16[32,16,768]{2,1,0:T(8,128)(2,1)S(1)} %copy-done.4, f32[768]{0:T(1024)S(1)} %copy-done.5), custom_call_target="tpu_custom_call" | custom-call | flops 4000000000 | bytes 1000000 | tf_op jit(solution)/shard_map/pallas_call | solution.py:87
  3.6 5.5 %collective-permute-start.2 = (bf16[1,768]{1,0:T(2,128)(2,1)S(1)}, bf16[1,768]{1,0:T(2,128)(2,1)S(1)}, u32[]{:S(2)}, u32[]{:S(2)}) collective-permute-start(bf16[1,768]{1,0:T(2,128)(2,1)S(1)} %get-tuple-element.48), channel_id=1, source_target_pairs={{0,17},{1,18},{2,19},{3,20},{4,21},{5,22},{6,23},{7,24},{8,25},{9,... | collective-permute-start | bytes 4616 | tf_op jit(solution)/shard_map/ppermute | solution.py:42
  9.1 3.5 %collective-permute-start = (bf16[16,768]{1,0:T(8,128)(2,1)S(1)}, bf16[16,768]{1,0:T(8,128)(2,1)S(1)}, u32[]{:S(2)}, u32[]{:S(2)}) collective-permute-start(bf16[16,768]{1,0:T(8,128)(2,1)S(1)} %get-tuple-element.46), channel_id=1, source_target_pairs={{0,16},{16,32},{32,48},{48,64},{64,80},{80,96},{96,112},{112,128},... | collective-permute-start | bytes 73736 | tf_op jit(solution)/shard_map/ppermute | solution.py:36
  12.7 2.2 %collective-permute-start.1 = (bf16[32,768]{1,0:T(8,128)(2,1)S(1)}, bf16[32,768]{1,0:T(8,128)(2,1)S(1)}, u32[]{:S(2)}, u32[]{:S(2)}) collective-permute-start(bf16[32,768]{1,0:T(8,128)(2,1)S(1)} %get-tuple-element.47), channel_id=1, source_target_pairs={{0,1},{1,2},{2,3},{3,4},{4,5},{5,6},{6,7},{7,8},{8,9},{9,10},{10,1... | collective-permute-start | bytes 147464 | tf_op jit(solution)/shard_map/ppermute | solution.py:36
  14.9 1.6 %shard_map.65 = (bf16[512,768]{1,0:T(8,128)(2,1)S(1)}, bf16[352,1536]{1,0:T(8,128)(2,1)S(1)}) custom-call(bf16[512,768]{1,0:T(8,128)(2,1)S(1)} %get-tuple-element.44.tokens_ref, bf16[768,2304]{1,0:T(8,128)(2,1)S(1)} %copy-done), custom_call_target="tpu_custom_call" | custom-call | flops 1500000000 | bytes 4000000 | tf_op jit(solution)/shard_map/pallas_call | solution.py:110
  16.6 0.7 shard_map.66
  17.2 1.4 %collective-permute-start.3 = (bf16[32,384]{1,0:T(8,128)(2,1)S(1)}, bf16[32,384]{1,0:T(8,128)(2,1)S(1)}, u32[]{:S(2)}, u32[]{:S(2)}) collective-permute-start(bf16[32,384]{1,0:T(8,128)(2,1)S(1)} %get-tuple-element.50), channel_id=1, source_target_pairs={{0,2},{2,4},{4,6},{6,0},{1,3},{3,5},{5,7},{7,1},{8,10},{10,12},{12... | collective-permute-start | bytes 73736 | tf_op jit(solution)/shard_map/ppermute | solution.py:25
  18.6 3.7 %collective-permute-start.4 = (bf16[32,384]{1,0:T(8,128)(2,1)S(1)}, bf16[32,384]{1,0:T(8,128)(2,1)S(1)}, u32[]{:S(2)}, u32[]{:S(2)}) collective-permute-start(bf16[32,384]{1,0:T(8,128)(2,1)S(1)} %get-tuple-element.51), channel_id=1, source_target_pairs={{0,4},{2,6},{4,0},{6,2},{1,5},{3,7},{5,1},{7,3},{8,12},{10,14},{12... | collective-permute-start | bytes 73736 | tf_op jit(solution)/shard_map/ppermute | solution.py:25
  22.4 2.2 %collective-permute-done.4 = bf16[32,384]{1,0:T(8,128)(2,1)S(1)} collective-permute-done((bf16[32,384]{1,0:T(8,128)(2,1)S(1)}, bf16[32,384]{1,0:T(8,128)(2,1)S(1)}, u32[]{:S(2)}, u32[]{:S(2)}) %collective-permute-start.4) | collective-permute-done | bytes 24608 | tf_op jit(solution)/shard_map/ppermute | solution.py:25
  24.6 0.5 collective-permute-done.5
  25.0 5.2 %collective-permute-start.8 = (bf16[128,384]{1,0:T(8,128)(2,1)S(1)}, bf16[128,384]{1,0:T(8,128)(2,1)S(1)}, u32[]{:S(2)}, u32[]{:S(2)}) collective-permute-start(bf16[128,384]{1,0:T(8,128)(2,1)S(1)} %pad_maximum_fusion), channel_id=1, source_target_pairs={{0,192},{64,0},{128,64},{192,128},{1,193},{65,1},{129,65},{193,129... | collective-permute-start | bytes 294920 | tf_op jit(solution)/shard_map/ppermute | solution.py:25
  30.2 3.3 %collective-permute-start.6 = (bf16[128,384]{1,0:T(8,128)(2,1)S(1)}, bf16[128,384]{1,0:T(8,128)(2,1)S(1)}, u32[]{:S(2)}, u32[]{:S(2)}) collective-permute-start(bf16[128,384]{1,0:T(8,128)(2,1)S(1)} %pad_maximum_fusion), channel_id=1, source_target_pairs={{0,128},{64,192},{128,0},{192,64},{1,129},{65,193},{129,1},{193,65... | collective-permute-start | bytes 294920 | tf_op jit(solution)/shard_map/ppermute | solution.py:25
  33.5 1.4 %shard_map.67 = bf16[8,192,128]{2,1,0:T(8,128)(2,1)} custom-call(bf16[512,768]{1,0:T(8,128)(2,1)S(1)} %get-tuple-element.54.own_ref, bf16[16,768]{1,0:T(8,128)(2,1)S(1)} %collective-permute-done.upper_ref, bf16[32,768]{1,0:T(8,128)(2,1)S(1)} %collective-permute-done.1.left_ref, bf16[1,768]{1,0:T(2,128)(2,1)S(1)} %collective-permute-done.2.corner_ref, ...), custom_call_target="tpu_custom_call" | custom-call | flops 200000000 | bytes 4000000 | tf_op jit(solution)/shard_map/pallas_call | solution.py:188
  34.9 3.6 %all-to-all-start = ((bf16[8,192,128]{2,1,0:T(8,128)(2,1)}), bf16[8,192,128]{2,1,0:T(8,128)(2,1)S(1)}, u32[]{:S(2)}, u32[]{:S(2)}) async-start(bf16[8,192,128]{2,1,0:T(8,128)(2,1)} %shard_map.67), calls=%async_computation | async-start | bytes 786432 | tf_op jit(solution)/shard_map/all_to_all | solution.py:384
  38.5 1.6 %collective-permute-done.6 = bf16[128,384]{1,0:T(8,128)(2,1)S(1)} collective-permute-done((bf16[128,384]{1,0:T(8,128)(2,1)S(1)}, bf16[128,384]{1,0:T(8,128)(2,1)S(1)}, u32[]{:S(2)}, u32[]{:S(2)}) %collective-permute-start.6) | collective-permute-done | bytes 98336 | tf_op jit(solution)/shard_map/ppermute | solution.py:25
  40.2 2.3 %collective-permute-start.11 = (bf16[512,384]{1,0:T(8,128)(2,1)S(1)}, bf16[512,384]{1,0:T(8,128)(2,1)S(1)}, u32[]{:S(2)}, u32[]{:S(2)}) collective-permute-start(bf16[512,384]{1,0:T(8,128)(2,1)S(1)} %constant_dynamic-update-slice_fusion.refs_0_), channel_id=1, source_target_pairs={{0,1},{1,0},{2,3},{3,2},{4,5},{5,4},{6,7},{7,6},{8,9},{9,8},{10,11... | collective-permute-start | bytes 1179656 | tf_op jit(solution)/shard_map/ppermute | solution.py:25
  42.4 3.5 %collective-permute-start.10 = (bf16[512,384]{1,0:T(8,128)(2,1)S(1)}, bf16[512,384]{1,0:T(8,128)(2,1)S(1)}, u32[]{:S(2)}, u32[]{:S(2)}) collective-permute-start(bf16[512,384]{1,0:T(8,128)(2,1)S(1)} %constant_dynamic-update-slice_fusion.refs_0_), channel_id=1, source_target_pairs={{0,24},{16,0},{8,16},{24,8},{1,25},{17,1},{9,17},{25,9},{2,26},{18... | collective-permute-start | bytes 1179656 | tf_op jit(solution)/shard_map/ppermute | solution.py:31
  46.0 3.3 %shard_map.68 = (f32[16,1024]{1,0:T(8,128)S(1)}, f32[192,1024]{1,0:T(8,128)S(1)}, bf16[3,128,1024]{2,1,0:T(8,128)(2,1)S(1)}) custom-call(bf16[8,192,128]{2,1,0:T(8,128)(2,1)S(1)} %all-to-all-done.q_ref, bf16[512,384]{1,0:T(8,128)(2,1)S(1)} %constant_dynamic-update-slice_fusion.refs_0_), custom_call_target="tpu_custom_call" | custom-call | flops 1572864 | bytes 1024 | tf_op jit(solution)/shard_map/pallas_call | solution.py:323
  49.3 9.2 %shard_map.69 = (f32[16,1024]{1,0:T(8,128)S(1)}, f32[192,1024]{1,0:T(8,128)S(1)}) custom-call(bf16[3,128,1024]{2,1,0:T(8,128)(2,1)S(1)} %get-tuple-element.56.q_ref, bf16[512,384]{1,0:T(8,128)(2,1)S(1)} %collective-permute-done.11.refs_0_, f32[16,1024]{1,0:T(8,128)S(1)} %get-tuple-element.57.refs_1_, f32[192,1024]{1,0:T(8,128)S(1)} %get-tuple-element.58.refs_2_), custom_call_target="tpu_custom_call" | custom-call | flops 1572864 | bytes 1024 | tf_op jit(solution)/shard_map/pallas_call | solution.py:323
  58.5 3.0 %collective-permute-start.15 = (bf16[512,384]{1,0:T(8,128)(2,1)S(1)}, bf16[512,384]{1,0:T(8,128)(2,1)S(1)}, u32[]{:S(2)}, u32[]{:S(2)}) collective-permute-start(bf16[512,384]{1,0:T(8,128)(2,1)S(1)} %collective-permute-done.9.refs_0_), channel_id=1, source_target_pairs={{0,1},{1,0},{2,3},{3,2},{4,5},{5,4},{6,7},{7,6},{8,9},{9,8},{10,11... | collective-permute-start | bytes 1179656 | tf_op jit(solution)/shard_map/ppermute | solution.py:25
  61.7 3.9 %collective-permute-start.13 = (bf16[256,384]{1,0:T(8,128)(2,1)S(1)}, bf16[256,384]{1,0:T(8,128)(2,1)S(1)}, u32[]{:S(2)}, u32[]{:S(2)}) collective-permute-start(bf16[256,384]{1,0:T(8,128)(2,1)S(1)} %slice.7), channel_id=1, source_target_pairs={{0,24},{16,0},{8,16},{24,8},{1,25},{17,1},{9,17},{25,9},{2,26},{18... | collective-permute-start | bytes 589832 | tf_op jit(solution)/shard_map/ppermute | solution.py:31
  65.6 9.2 %shard_map.70 = (f32[16,1024]{1,0:T(8,128)S(1)}, f32[192,1024]{1,0:T(8,128)S(1)}) custom-call(bf16[3,128,1024]{2,1,0:T(8,128)(2,1)S(1)} %get-tuple-element.56.q_ref, bf16[512,384]{1,0:T(8,128)(2,1)S(1)} %collective-permute-done.9.refs_0_, f32[16,1024]{1,0:T(8,128)S(1)} %get-tuple-element.63.refs_1_, f32[192,1024]{1,0:T(8,128)S(1)} %get-tuple-element.64.refs_2_), custom_call_target="tpu_custom_call" | custom-call | flops 1572864 | bytes 1024 | tf_op jit(solution)/shard_map/pallas_call | solution.py:323
  74.8 9.2 %shard_map.71 = (f32[16,1024]{1,0:T(8,128)S(1)}, f32[192,1024]{1,0:T(8,128)S(1)}) custom-call(bf16[3,128,1024]{2,1,0:T(8,128)(2,1)S(1)} %get-tuple-element.56.q_ref, bf16[512,384]{1,0:T(8,128)(2,1)S(1)} %collective-permute-done.15.refs_0_, f32[16,1024]{1,0:T(8,128)S(1)} %get-tuple-element.65.refs_1_, f32[192,1024]{1,0:T(8,128)S(1)} %get-tuple-element.66.refs_2_), custom_call_target="tpu_custom_call" | custom-call | flops 1572864 | bytes 1024 | tf_op jit(solution)/shard_map/pallas_call | solution.py:323
  83.9 9.4 %shard_map.72 = (f32[16,1024]{1,0:T(8,128)S(1)}, f32[192,1024]{1,0:T(8,128)S(1)}) custom-call(bf16[3,128,1024]{2,1,0:T(8,128)(2,1)S(1)} %get-tuple-element.56.q_ref, bf16[512,384]{1,0:T(8,128)(2,1)S(1)} %collective-permute-done.10.refs_0_, f32[16,1024]{1,0:T(8,128)S(1)} %get-tuple-element.67.refs_1_, f32[192,1024]{1,0:T(8,128)S(1)} %get-tuple-element.68.refs_2_), custom_call_target="tpu_custom_call" | custom-call | flops 1572864 | bytes 1024 | tf_op jit(solution)/shard_map/pallas_call | solution.py:323
  93.3 9.2 %shard_map.73 = (f32[16,1024]{1,0:T(8,128)S(1)}, f32[192,1024]{1,0:T(8,128)S(1)}) custom-call(bf16[3,128,1024]{2,1,0:T(8,128)(2,1)S(1)} %get-tuple-element.56.q_ref, bf16[512,384]{1,0:T(8,128)(2,1)S(1)} %collective-permute-done.14.refs_0_, f32[16,1024]{1,0:T(8,128)S(1)} %get-tuple-element.69.refs_1_, f32[192,1024]{1,0:T(8,128)S(1)} %get-tuple-element.70.refs_2_), custom_call_target="tpu_custom_call" | custom-call | flops 1572864 | bytes 1024 | tf_op jit(solution)/shard_map/pallas_call | solution.py:323
  102.5 0.8 collective-permute-start.16
  103.4 9.2 %shard_map.74 = (f32[16,1024]{1,0:T(8,128)S(1)}, f32[192,1024]{1,0:T(8,128)S(1)}) custom-call(bf16[3,128,1024]{2,1,0:T(8,128)(2,1)S(1)} %get-tuple-element.56.q_ref, bf16[256,384]{1,0:T(8,128)(2,1)S(1)} %collective-permute-done.12.refs_0_, bf16[256,384]{1,0:T(8,128)(2,1)S(1)} %collective-permute-done.13.refs_1_, f32[16,1024]{1,0:T(8,128)S(1)} %get-tuple-element.75.refs_2_, ...), custom_call_target="tpu_custom_call" | custom-call | flops 1572864 | bytes 1024 | tf_op jit(solution)/shard_map/pallas_call | solution.py:323
  112.6 9.3 %shard_map.75 = bf16[8,208,128]{2,1,0:T(8,128)(2,1)S(1)} custom-call(bf16[3,128,1024]{2,1,0:T(8,128)(2,1)S(1)} %get-tuple-element.56.q_ref, bf16[256,384]{1,0:T(8,128)(2,1)S(1)} %collective-permute-done.16.refs_0_, bf16[256,384]{1,0:T(8,128)(2,1)S(1)} %collective-permute-done.17.refs_1_, f32[16,1024]{1,0:T(8,128)S(1)} %get-tuple-element.77.refs_2_, ...), custom_call_target="tpu_custom_call" | custom-call | flops 1572864 | bytes 1024 | tf_op jit(solution)/shard_map/pallas_call | solution.py:323
  121.9 10.6 %all_to_all.10.parts_ref = bf16[8,208,128]{2,1,0:T(8,128)(2,1)S(1)} all-to-all(bf16[8,208,128]{2,1,0:T(8,128)(2,1)S(1)} %shard_map.75), channel_id=1, replica_groups=mesh['zq'=4,'zc'=2,'xl'=2,'xh'=2,'y'=4,'core'=2] {'zc','y'}, dimensions={0} | all-to-all | bytes 851968 | tf_op jit(solution)/shard_map/all_to_all | solution.py:399
  132.5 1.1 shard_map.76
  (39 shorter events, 0.4 us)
Async XLA Ops:
  0.0 1.1 copy-start.4
  1.1 0.7 copy-start.5
  1.8 13.0 %copy-start = (bf16[768,2304]{1,0:T(8,128)(2,1)S(1)}, bf16[768,2304]{1,0:T(8,128)(2,1)}, u32[]{:S(2)}) copy-start(bf16[768,2304]{1,0:T(8,128)(2,1)} %w_ref.6) | copy-start | bytes 10616836
  3.6 12.9 %collective-permute-start.2 = (bf16[1,768]{1,0:T(2,128)(2,1)S(1)}, bf16[1,768]{1,0:T(2,128)(2,1)S(1)}, u32[]{:S(2)}, u32[]{:S(2)}) collective-permute-start(bf16[1,768]{1,0:T(2,128)(2,1)S(1)} %get-tuple-element.48), channel_id=1, source_target_pairs={{0,17},{1,18},{2,19},{3,20},{4,21},{5,22},{6,23},{7,24},{8,25},{9,... | collective-permute-start | bytes 4616 | tf_op jit(solution)/shard_map/ppermute | solution.py:42
  9.1 7.4 %collective-permute-start = (bf16[16,768]{1,0:T(8,128)(2,1)S(1)}, bf16[16,768]{1,0:T(8,128)(2,1)S(1)}, u32[]{:S(2)}, u32[]{:S(2)}) collective-permute-start(bf16[16,768]{1,0:T(8,128)(2,1)S(1)} %get-tuple-element.46), channel_id=1, source_target_pairs={{0,16},{16,32},{32,48},{48,64},{64,80},{80,96},{96,112},{112,128},... | collective-permute-start | bytes 73736 | tf_op jit(solution)/shard_map/ppermute | solution.py:36
  12.7 3.9 %collective-permute-start.1 = (bf16[32,768]{1,0:T(8,128)(2,1)S(1)}, bf16[32,768]{1,0:T(8,128)(2,1)S(1)}, u32[]{:S(2)}, u32[]{:S(2)}) collective-permute-start(bf16[32,768]{1,0:T(8,128)(2,1)S(1)} %get-tuple-element.47), channel_id=1, source_target_pairs={{0,1},{1,2},{2,3},{3,4},{4,5},{5,6},{6,7},{7,8},{8,9},{9,10},{10,1... | collective-permute-start | bytes 147464 | tf_op jit(solution)/shard_map/ppermute | solution.py:36
  14.9 1.7 %copy-start.2 = (f32[9,1536]{1,0:T(8,128)S(1)}, f32[9,1536]{1,0:T(8,128)}, u32[]{:S(2)}) copy-start(f32[9,1536]{1,0:T(8,128)} %pool_ref.2) | copy-start | bytes 165892
  16.6 16.9 %copy-start.3 = (f32[9,768]{1,0:T(8,128)S(1)}, f32[9,768]{1,0:T(8,128)}, u32[]{:S(2)}) copy-start(f32[9,768]{1,0:T(8,128)} %pool_ref.3) | copy-start | bytes 82948
  17.2 5.1 %collective-permute-start.3 = (bf16[32,384]{1,0:T(8,128)(2,1)S(1)}, bf16[32,384]{1,0:T(8,128)(2,1)S(1)}, u32[]{:S(2)}, u32[]{:S(2)}) collective-permute-start(bf16[32,384]{1,0:T(8,128)(2,1)S(1)} %get-tuple-element.50), channel_id=1, source_target_pairs={{0,2},{2,4},{4,6},{6,0},{1,3},{3,5},{5,7},{7,1},{8,10},{10,12},{12... | collective-permute-start | bytes 73736 | tf_op jit(solution)/shard_map/ppermute | solution.py:25
  18.6 5.9 %collective-permute-start.4 = (bf16[32,384]{1,0:T(8,128)(2,1)S(1)}, bf16[32,384]{1,0:T(8,128)(2,1)S(1)}, u32[]{:S(2)}, u32[]{:S(2)}) collective-permute-start(bf16[32,384]{1,0:T(8,128)(2,1)S(1)} %get-tuple-element.51), channel_id=1, source_target_pairs={{0,4},{2,6},{4,0},{6,2},{1,5},{3,7},{5,1},{7,3},{8,12},{10,14},{12... | collective-permute-start | bytes 73736 | tf_op jit(solution)/shard_map/ppermute | solution.py:25
  22.3 2.7 %collective-permute-start.5 = (bf16[32,384]{1,0:T(8,128)(2,1)S(1)}, bf16[32,384]{1,0:T(8,128)(2,1)S(1)}, u32[]{:S(2)}, u32[]{:S(2)}) collective-permute-start(bf16[32,384]{1,0:T(8,128)(2,1)S(1)} %get-tuple-element.52), channel_id=1, source_target_pairs={{0,6},{2,0},{4,2},{6,4},{1,7},{3,1},{5,3},{7,5},{8,14},{10,8},{12,... | collective-permute-start | bytes 73736 | tf_op jit(solution)/shard_map/ppermute | solution.py:25
  25.0 15.1 %collective-permute-start.8 = (bf16[128,384]{1,0:T(8,128)(2,1)S(1)}, bf16[128,384]{1,0:T(8,128)(2,1)S(1)}, u32[]{:S(2)}, u32[]{:S(2)}) collective-permute-start(bf16[128,384]{1,0:T(8,128)(2,1)S(1)} %pad_maximum_fusion), channel_id=1, source_target_pairs={{0,192},{64,0},{128,64},{192,128},{1,193},{65,1},{129,65},{193,129... | collective-permute-start | bytes 294920 | tf_op jit(solution)/shard_map/ppermute | solution.py:25
  30.2 9.8 %collective-permute-start.7 = (bf16[128,384]{1,0:T(8,128)(2,1)S(1)}, bf16[128,384]{1,0:T(8,128)(2,1)S(1)}, u32[]{:S(2)}, u32[]{:S(2)}) collective-permute-start(bf16[128,384]{1,0:T(8,128)(2,1)S(1)} %pad_maximum_fusion), channel_id=1, source_target_pairs={{0,64},{64,128},{128,192},{192,0},{1,65},{65,129},{129,193},{193,1... | collective-permute-start | bytes 294920 | tf_op jit(solution)/shard_map/ppermute | solution.py:25
  30.2 9.8 %collective-permute-start.6 = (bf16[128,384]{1,0:T(8,128)(2,1)S(1)}, bf16[128,384]{1,0:T(8,128)(2,1)S(1)}, u32[]{:S(2)}, u32[]{:S(2)}) collective-permute-start(bf16[128,384]{1,0:T(8,128)(2,1)S(1)} %pad_maximum_fusion), channel_id=1, source_target_pairs={{0,128},{64,192},{128,0},{192,64},{1,129},{65,193},{129,1},{193,65... | collective-permute-start | bytes 294920 | tf_op jit(solution)/shard_map/ppermute | solution.py:25
  34.9 11.1 %all-to-all-start = ((bf16[8,192,128]{2,1,0:T(8,128)(2,1)}), bf16[8,192,128]{2,1,0:T(8,128)(2,1)S(1)}, u32[]{:S(2)}, u32[]{:S(2)}) async-start(bf16[8,192,128]{2,1,0:T(8,128)(2,1)} %shard_map.67), calls=%async_computation | async-start | bytes 786432 | tf_op jit(solution)/shard_map/all_to_all | solution.py:384
  40.2 9.1 %collective-permute-start.11 = (bf16[512,384]{1,0:T(8,128)(2,1)S(1)}, bf16[512,384]{1,0:T(8,128)(2,1)S(1)}, u32[]{:S(2)}, u32[]{:S(2)}) collective-permute-start(bf16[512,384]{1,0:T(8,128)(2,1)S(1)} %constant_dynamic-update-slice_fusion.refs_0_), channel_id=1, source_target_pairs={{0,1},{1,0},{2,3},{3,2},{4,5},{5,4},{6,7},{7,6},{8,9},{9,8},{10,11... | collective-permute-start | bytes 1179656 | tf_op jit(solution)/shard_map/ppermute | solution.py:25
  42.4 16.0 %collective-permute-start.10 = (bf16[512,384]{1,0:T(8,128)(2,1)S(1)}, bf16[512,384]{1,0:T(8,128)(2,1)S(1)}, u32[]{:S(2)}, u32[]{:S(2)}) collective-permute-start(bf16[512,384]{1,0:T(8,128)(2,1)S(1)} %constant_dynamic-update-slice_fusion.refs_0_), channel_id=1, source_target_pairs={{0,24},{16,0},{8,16},{24,8},{1,25},{17,1},{9,17},{25,9},{2,26},{18... | collective-permute-start | bytes 1179656 | tf_op jit(solution)/shard_map/ppermute | solution.py:31
  46.0 12.5 %collective-permute-start.9 = (bf16[512,384]{1,0:T(8,128)(2,1)S(1)}, bf16[512,384]{1,0:T(8,128)(2,1)S(1)}, u32[]{:S(2)}, u32[]{:S(2)}) collective-permute-start(bf16[512,384]{1,0:T(8,128)(2,1)S(1)} %constant_dynamic-update-slice_fusion.refs_0_), channel_id=1, source_target_pairs={{0,16},{16,8},{8,24},{24,0},{1,17},{17,9},{9,25},{25,1},{2,18},{18... | collective-permute-start | bytes 1179656 | tf_op jit(solution)/shard_map/ppermute | solution.py:31
  58.5 16.2 %collective-permute-start.15 = (bf16[512,384]{1,0:T(8,128)(2,1)S(1)}, bf16[512,384]{1,0:T(8,128)(2,1)S(1)}, u32[]{:S(2)}, u32[]{:S(2)}) collective-permute-start(bf16[512,384]{1,0:T(8,128)(2,1)S(1)} %collective-permute-done.9.refs_0_), channel_id=1, source_target_pairs={{0,1},{1,0},{2,3},{3,2},{4,5},{5,4},{6,7},{7,6},{8,9},{9,8},{10,11... | collective-permute-start | bytes 1179656 | tf_op jit(solution)/shard_map/ppermute | solution.py:25
  61.5 31.8 %collective-permute-start.14 = (bf16[512,384]{1,0:T(8,128)(2,1)S(1)}, bf16[512,384]{1,0:T(8,128)(2,1)S(1)}, u32[]{:S(2)}, u32[]{:S(2)}) collective-permute-start(bf16[512,384]{1,0:T(8,128)(2,1)S(1)} %collective-permute-done.10.refs_0_), channel_id=1, source_target_pairs={{0,1},{1,0},{2,3},{3,2},{4,5},{5,4},{6,7},{7,6},{8,9},{9,8},{10,11... | collective-permute-start | bytes 1179656 | tf_op jit(solution)/shard_map/ppermute | solution.py:25
  61.7 40.8 %collective-permute-start.13 = (bf16[256,384]{1,0:T(8,128)(2,1)S(1)}, bf16[256,384]{1,0:T(8,128)(2,1)S(1)}, u32[]{:S(2)}, u32[]{:S(2)}) collective-permute-start(bf16[256,384]{1,0:T(8,128)(2,1)S(1)} %slice.7), channel_id=1, source_target_pairs={{0,24},{16,0},{8,16},{24,8},{1,25},{17,1},{9,17},{25,9},{2,26},{18... | collective-permute-start | bytes 589832 | tf_op jit(solution)/shard_map/ppermute | solution.py:31
  65.6 37.0 %collective-permute-start.12 = (bf16[256,384]{1,0:T(8,128)(2,1)S(1)}, bf16[256,384]{1,0:T(8,128)(2,1)S(1)}, u32[]{:S(2)}, u32[]{:S(2)}) collective-permute-start(bf16[256,384]{1,0:T(8,128)(2,1)S(1)} %slice.6), channel_id=1, source_target_pairs={{0,16},{16,8},{8,24},{24,0},{1,17},{17,9},{9,25},{25,1},{2,18},{18... | collective-permute-start | bytes 589832 | tf_op jit(solution)/shard_map/ppermute | solution.py:31
  102.5 10.1 %collective-permute-start.16 = (bf16[256,384]{1,0:T(8,128)(2,1)S(1)}, bf16[256,384]{1,0:T(8,128)(2,1)S(1)}, u32[]{:S(2)}, u32[]{:S(2)}) collective-permute-start(bf16[256,384]{1,0:T(8,128)(2,1)S(1)} %collective-permute-done.12.refs_0_), channel_id=1, source_target_pairs={{0,1},{1,0},{2,3},{3,2},{4,5},{5,4},{6,7},{7,6},{8,9},{9,8},{10,11... | collective-permute-start | bytes 589832 | tf_op jit(solution)/shard_map/ppermute | solution.py:25
  103.3 9.3 %collective-permute-start.17 = (bf16[256,384]{1,0:T(8,128)(2,1)S(1)}, bf16[256,384]{1,0:T(8,128)(2,1)S(1)}, u32[]{:S(2)}, u32[]{:S(2)}) collective-permute-start(bf16[256,384]{1,0:T(8,128)(2,1)S(1)} %collective-permute-done.13.refs_1_), channel_id=1, source_target_pairs={{0,1},{1,0},{2,3},{3,2},{4,5},{5,4},{6,7},{7,6},{8,9},{9,8},{10,11... | collective-permute-start | bytes 589832 | tf_op jit(solution)/shard_map/ppermute | solution.py:25
  112.6 19.9 %copy-start.1 = (bf16[768,768]{1,0:T(8,128)(2,1)S(1)}, bf16[768,768]{1,0:T(8,128)(2,1)}, u32[]{:S(2)}) copy-start(bf16[768,768]{1,0:T(8,128)(2,1)} %w_ref.7) | copy-start | bytes 3538948

commit v5 on v4

--- a/solution.py
+++ b/solution.py
@@ -378,9 +378,9 @@
     parts = pool_call(keyvals_kernel, own_kv, halo, w_qkv, pool_kv, [part] * groups, [(groups, *part)], here)
     own = jnp.concatenate([parts[0]] + [shifted(p, "y", d) for d, p in enumerate(parts) if d], 0)
     tie = lax.optimization_barrier
-    own, own_q = tie((own, own_q))
+    (turned,) = pool_call(queries_kernel, own_q, halo, w_qkv, pool_q, [(2 * groups, WIDE, 128)])
+    own, turned = tie((own, turned))
     line = [own, shifted(own, "zq", 2), shifted(own, "zq", 1), shifted(own, "zq", -1)]
-    (turned,) = pool_call(queries_kernel, own_q, halo, w_qkv, pool_q, [(2 * groups, WIDE, 128)])
     every_query = lax.all_to_all(turned, ("zc", "y"), 0, 0, tiled=True)
     line = jnp.concatenate(line, 0)
     after, before = shifted_x(line, 1), shifted_x(line, -1)

time: 135 us -> 134 us (level)
  starting transfers between devices: 42.1 us -> 40.7 us
    ppermute x11, starting transfers between devices: 19.9 us -> 17.6 us  [shifted(): lax.ppermute(block, axis, [(i, (i + distance) % count) for i in range(cou...]
  transfers between devices with their start and end apart: 19 -> 19, of which waited for: 3 -> 3; matrix products, arithmetic and copies ran while one was open for 0% -> 0% of each run, Pallas kernels for 46% -> 47%
where the time goes in v5:
time: 134 us; the launch traced here: 132 us
  Pallas kernels  74.4 us (56%)
  starting transfers between devices  40.7 us (30%)
  blocking collectives  10.6 us (8%)
  waiting for transfers between devices  4.32 us (3%)
  local copies, waits for them, and re-layouts  1.95 us (1%)
    pallas_call x8, Pallas kernels, attend(): pl.pallas_call(functools.partial(attend_kernel, first, last, qb, len(bloc...  67.8 us
    ppermute x11, starting transfers between devices, shifted(): lax.ppermute(block, axis, [(i, (i + distance) % count) for i in range(cou...  17.6 us
    all_to_all x1, blocking collectives, on_device(): parts = lax.all_to_all(partial, ('zc', 'y'), 0, 0, tiled=True)  10.6 us
    ppermute x4, starting transfers between devices, shifted_x(): return lax.ppermute(block, ('xl', 'xh'), route)  8.28 us
    ppermute x2, starting transfers between devices, passed_along(): return lax.ppermute(block, axis, [(i - 1, i) for i in range(1, count)])  5.71 us
    ppermute x1, starting transfers between devices, corner(): return lax.ppermute(block, AXES, route)  5.52 us
    ppermute x11, waiting for transfers between devices, shifted(): lax.ppermute(block, axis, [(i, (i + distance) % count) for i in range(cou...  4.3 us
    all_to_all x1, starting transfers between devices, on_device(): every_query = lax.all_to_all(turned, ('zc', 'y'), 0, 0, tiled=True)  3.58 us
  transfers between devices with their start and end apart: 19, of which 3 were waited for; matrix products, arithmetic and copies ran while one was open for 0% of the time, Pallas kernels for 47%

profile of v5, /device:TPU:1, one launch (start us, length us, event | category | flops | bytes accessed | tf_op | source)
XLA Modules:
  0.0 132.3 jit_solution(10604815269259107314)
XLA Ops:
  0.0 1.1 copy-done.4
  1.1 0.7 copy-done.5
  1.8 1.8 %shard_map.64 = (bf16[512,768]{1,0:T(8,128)(2,1)S(1)}, bf16[32,768]{1,0:T(8,128)(2,1)S(1)}, bf16[16,768]{1,0:T(8,128)(2,1)S(1)}, bf16[1,768]{1,0:T(2,128)(2,1)S(1)}) custom-call(bf16[32,16,768]{2,1,0:T(8,128)(2,1)S(1)} %copy-done.4, f32[768]{0:T(1024)S(1)} %copy-done.5), custom_call_target="tpu_custom_call" | custom-call | flops 4000000000 | bytes 1000000 | tf_op jit(solution)/shard_map/pallas_call | solution.py:87
  3.6 5.5 %collective-permute-start.2 = (bf16[1,768]{1,0:T(2,128)(2,1)S(1)}, bf16[1,768]{1,0:T(2,128)(2,1)S(1)}, u32[]{:S(2)}, u32[]{:S(2)}) collective-permute-start(bf16[1,768]{1,0:T(2,128)(2,1)S(1)} %get-tuple-element.48), channel_id=1, source_target_pairs={{0,17},{1,18},{2,19},{3,20},{4,21},{5,22},{6,23},{7,24},{8,25},{9,... | collective-permute-start | bytes 4616 | tf_op jit(solution)/shard_map/ppermute | solution.py:42
  9.1 3.5 %collective-permute-start = (bf16[16,768]{1,0:T(8,128)(2,1)S(1)}, bf16[16,768]{1,0:T(8,128)(2,1)S(1)}, u32[]{:S(2)}, u32[]{:S(2)}) collective-permute-start(bf16[16,768]{1,0:T(8,128)(2,1)S(1)} %get-tuple-element.46), channel_id=1, source_target_pairs={{0,16},{16,32},{32,48},{48,64},{64,80},{80,96},{96,112},{112,128},... | collective-permute-start | bytes 73736 | tf_op jit(solution)/shard_map/ppermute | solution.py:36
  12.7 2.2 %collective-permute-start.1 = (bf16[32,768]{1,0:T(8,128)(2,1)S(1)}, bf16[32,768]{1,0:T(8,128)(2,1)S(1)}, u32[]{:S(2)}, u32[]{:S(2)}) collective-permute-start(bf16[32,768]{1,0:T(8,128)(2,1)S(1)} %get-tuple-element.47), channel_id=1, source_target_pairs={{0,1},{1,2},{2,3},{3,4},{4,5},{5,6},{6,7},{7,8},{8,9},{9,10},{10,1... | collective-permute-start | bytes 147464 | tf_op jit(solution)/shard_map/ppermute | solution.py:36
  14.9 1.6 %shard_map.65 = (bf16[512,768]{1,0:T(8,128)(2,1)S(1)}, bf16[352,1536]{1,0:T(8,128)(2,1)S(1)}) custom-call(bf16[512,768]{1,0:T(8,128)(2,1)S(1)} %get-tuple-element.44.tokens_ref, bf16[768,2304]{1,0:T(8,128)(2,1)S(1)} %copy-done), custom_call_target="tpu_custom_call" | custom-call | flops 1500000000 | bytes 4000000 | tf_op jit(solution)/shard_map/pallas_call | solution.py:110
  16.6 0.7 shard_map.66
  17.2 1.4 %collective-permute-start.3 = (bf16[32,384]{1,0:T(8,128)(2,1)S(1)}, bf16[32,384]{1,0:T(8,128)(2,1)S(1)}, u32[]{:S(2)}, u32[]{:S(2)}) collective-permute-start(bf16[32,384]{1,0:T(8,128)(2,1)S(1)} %get-tuple-element.50), channel_id=1, source_target_pairs={{0,2},{2,4},{4,6},{6,0},{1,3},{3,5},{5,7},{7,1},{8,10},{10,12},{12... | collective-permute-start | bytes 73736 | tf_op jit(solution)/shard_map/ppermute | solution.py:25
  18.6 3.7 %collective-permute-start.4 = (bf16[32,384]{1,0:T(8,128)(2,1)S(1)}, bf16[32,384]{1,0:T(8,128)(2,1)S(1)}, u32[]{:S(2)}, u32[]{:S(2)}) collective-permute-start(bf16[32,384]{1,0:T(8,128)(2,1)S(1)} %get-tuple-element.51), channel_id=1, source_target_pairs={{0,4},{2,6},{4,0},{6,2},{1,5},{3,7},{5,1},{7,3},{8,12},{10,14},{12... | collective-permute-start | bytes 73736 | tf_op jit(solution)/shard_map/ppermute | solution.py:25
  22.4 1.4 %shard_map.67 = bf16[8,192,128]{2,1,0:T(8,128)(2,1)} custom-call(bf16[512,768]{1,0:T(8,128)(2,1)S(1)} %get-tuple-element.53.own_ref, bf16[16,768]{1,0:T(8,128)(2,1)S(1)} %collective-permute-done.upper_ref, bf16[32,768]{1,0:T(8,128)(2,1)S(1)} %collective-permute-done.1.left_ref, bf16[1,768]{1,0:T(2,128)(2,1)S(1)} %collective-permute-done.2.corner_ref, ...), custom_call_target="tpu_custom_call" | custom-call | flops 200000000 | bytes 4000000 | tf_op jit(solution)/shard_map/pallas_call | solution.py:188
  23.7 0.8 collective-permute-done.4
  24.6 0.5 collective-permute-done.5
  25.0 5.2 %collective-permute-start.8 = (bf16[128,384]{1,0:T(8,128)(2,1)S(1)}, bf16[128,384]{1,0:T(8,128)(2,1)S(1)}, u32[]{:S(2)}, u32[]{:S(2)}) collective-permute-start(bf16[128,384]{1,0:T(8,128)(2,1)S(1)} %pad_maximum_fusion), channel_id=1, source_target_pairs={{0,192},{64,0},{128,64},{192,128},{1,193},{65,1},{129,65},{193,129... | collective-permute-start | bytes 294920 | tf_op jit(solution)/shard_map/ppermute | solution.py:25
  30.2 3.3 %collective-permute-start.6 = (bf16[128,384]{1,0:T(8,128)(2,1)S(1)}, bf16[128,384]{1,0:T(8,128)(2,1)S(1)}, u32[]{:S(2)}, u32[]{:S(2)}) collective-permute-start(bf16[128,384]{1,0:T(8,128)(2,1)S(1)} %pad_maximum_fusion), channel_id=1, source_target_pairs={{0,128},{64,192},{128,0},{192,64},{1,129},{65,193},{129,1},{193,65... | collective-permute-start | bytes 294920 | tf_op jit(solution)/shard_map/ppermute | solution.py:25
  33.5 3.6 %all-to-all-start = ((bf16[8,192,128]{2,1,0:T(8,128)(2,1)}), bf16[8,192,128]{2,1,0:T(8,128)(2,1)S(1)}, u32[]{:S(2)}, u32[]{:S(2)}) async-start(bf16[8,192,128]{2,1,0:T(8,128)(2,1)} %shard_map.67), calls=%async_computation | async-start | bytes 786432 | tf_op jit(solution)/shard_map/all_to_all | solution.py:384
  37.1 3.0 %collective-permute-done.6 = bf16[128,384]{1,0:T(8,128)(2,1)S(1)} collective-permute-done((bf16[128,384]{1,0:T(8,128)(2,1)S(1)}, bf16[128,384]{1,0:T(8,128)(2,1)S(1)}, u32[]{:S(2)}, u32[]{:S(2)}) %collective-permute-start.6) | collective-permute-done | bytes 98336 | tf_op jit(solution)/shard_map/ppermute | solution.py:25
  40.2 2.6 %collective-permute-start.11 = (bf16[512,384]{1,0:T(8,128)(2,1)S(1)}, bf16[512,384]{1,0:T(8,128)(2,1)S(1)}, u32[]{:S(2)}, u32[]{:S(2)}) collective-permute-start(bf16[512,384]{1,0:T(8,128)(2,1)S(1)} %constant_dynamic-update-slice_fusion.refs_0_), channel_id=1, source_target_pairs={{0,1},{1,0},{2,3},{3,2},{4,5},{5,4},{6,7},{7,6},{8,9},{9,8},{10,11... | collective-permute-start | bytes 1179656 | tf_op jit(solution)/shard_map/ppermute | solution.py:25
  42.7 4.6 %collective-permute-start.10 = (bf16[512,384]{1,0:T(8,128)(2,1)S(1)}, bf16[512,384]{1,0:T(8,128)(2,1)S(1)}, u32[]{:S(2)}, u32[]{:S(2)}) collective-permute-start(bf16[512,384]{1,0:T(8,128)(2,1)S(1)} %constant_dynamic-update-slice_fusion.refs_0_), channel_id=1, source_target_pairs={{0,24},{16,0},{8,16},{24,8},{1,25},{17,1},{9,17},{25,9},{2,26},{18... | collective-permute-start | bytes 1179656 | tf_op jit(solution)/shard_map/ppermute | solution.py:31
  47.3 3.3 %shard_map.68 = (f32[16,1024]{1,0:T(8,128)S(1)}, f32[192,1024]{1,0:T(8,128)S(1)}, bf16[3,128,1024]{2,1,0:T(8,128)(2,1)S(1)}) custom-call(bf16[8,192,128]{2,1,0:T(8,128)(2,1)S(1)} %all-to-all-done.q_ref, bf16[512,384]{1,0:T(8,128)(2,1)S(1)} %constant_dynamic-update-slice_fusion.refs_0_), custom_call_target="tpu_custom_call" | custom-call | flops 1572864 | bytes 1024 | tf_op jit(solution)/shard_map/pallas_call | solution.py:323
  50.7 9.2 %shard_map.69 = (f32[16,1024]{1,0:T(8,128)S(1)}, f32[192,1024]{1,0:T(8,128)S(1)}) custom-call(bf16[3,128,1024]{2,1,0:T(8,128)(2,1)S(1)} %get-tuple-element.56.q_ref, bf16[512,384]{1,0:T(8,128)(2,1)S(1)} %collective-permute-done.11.refs_0_, f32[16,1024]{1,0:T(8,128)S(1)} %get-tuple-element.57.refs_1_, f32[192,1024]{1,0:T(8,128)S(1)} %get-tuple-element.58.refs_2_), custom_call_target="tpu_custom_call" | custom-call | flops 1572864 | bytes 1024 | tf_op jit(solution)/shard_map/pallas_call | solution.py:323
  59.9 0.4 collective-permute-start.15
  60.5 3.7 %collective-permute-start.13 = (bf16[256,384]{1,0:T(8,128)(2,1)S(1)}, bf16[256,384]{1,0:T(8,128)(2,1)S(1)}, u32[]{:S(2)}, u32[]{:S(2)}) collective-permute-start(bf16[256,384]{1,0:T(8,128)(2,1)S(1)} %slice.7), channel_id=1, source_target_pairs={{0,24},{16,0},{8,16},{24,8},{1,25},{17,1},{9,17},{25,9},{2,26},{18... | collective-permute-start | bytes 589832 | tf_op jit(solution)/shard_map/ppermute | solution.py:31
  64.2 9.2 %shard_map.70 = (f32[16,1024]{1,0:T(8,128)S(1)}, f32[192,1024]{1,0:T(8,128)S(1)}) custom-call(bf16[3,128,1024]{2,1,0:T(8,128)(2,1)S(1)} %get-tuple-element.56.q_ref, bf16[512,384]{1,0:T(8,128)(2,1)S(1)} %collective-permute-done.9.refs_0_, f32[16,1024]{1,0:T(8,128)S(1)} %get-tuple-element.63.refs_1_, f32[192,1024]{1,0:T(8,128)S(1)} %get-tuple-element.64.refs_2_), custom_call_target="tpu_custom_call" | custom-call | flops 1572864 | bytes 1024 | tf_op jit(solution)/shard_map/pallas_call | solution.py:323
  73.4 9.2 %shard_map.71 = (f32[16,1024]{1,0:T(8,128)S(1)}, f32[192,1024]{1,0:T(8,128)S(1)}) custom-call(bf16[3,128,1024]{2,1,0:T(8,128)(2,1)S(1)} %get-tuple-element.56.q_ref, bf16[512,384]{1,0:T(8,128)(2,1)S(1)} %collective-permute-done.15.refs_0_, f32[16,1024]{1,0:T(8,128)S(1)} %get-tuple-element.65.refs_1_, f32[192,1024]{1,0:T(8,128)S(1)} %get-tuple-element.66.refs_2_), custom_call_target="tpu_custom_call" | custom-call | flops 1572864 | bytes 1024 | tf_op jit(solution)/shard_map/pallas_call | solution.py:323
  82.6 9.4 %shard_map.72 = (f32[16,1024]{1,0:T(8,128)S(1)}, f32[192,1024]{1,0:T(8,128)S(1)}) custom-call(bf16[3,128,1024]{2,1,0:T(8,128)(2,1)S(1)} %get-tuple-element.56.q_ref, bf16[512,384]{1,0:T(8,128)(2,1)S(1)} %collective-permute-done.10.refs_0_, f32[16,1024]{1,0:T(8,128)S(1)} %get-tuple-element.67.refs_1_, f32[192,1024]{1,0:T(8,128)S(1)} %get-tuple-element.68.refs_2_), custom_call_target="tpu_custom_call" | custom-call | flops 1572864 | bytes 1024 | tf_op jit(solution)/shard_map/pallas_call | solution.py:323
  92.0 9.2 %shard_map.73 = (f32[16,1024]{1,0:T(8,128)S(1)}, f32[192,1024]{1,0:T(8,128)S(1)}) custom-call(bf16[3,128,1024]{2,1,0:T(8,128)(2,1)S(1)} %get-tuple-element.56.q_ref, bf16[512,384]{1,0:T(8,128)(2,1)S(1)} %collective-permute-done.14.refs_0_, f32[16,1024]{1,0:T(8,128)S(1)} %get-tuple-element.69.refs_1_, f32[192,1024]{1,0:T(8,128)S(1)} %get-tuple-element.70.refs_2_), custom_call_target="tpu_custom_call" | custom-call | flops 1572864 | bytes 1024 | tf_op jit(solution)/shard_map/pallas_call | solution.py:323
  101.2 0.8 collective-permute-start.16
  102.1 9.2 %shard_map.74 = (f32[16,1024]{1,0:T(8,128)S(1)}, f32[192,1024]{1,0:T(8,128)S(1)}) custom-call(bf16[3,128,1024]{2,1,0:T(8,128)(2,1)S(1)} %get-tuple-element.56.q_ref, bf16[256,384]{1,0:T(8,128)(2,1)S(1)} %collective-permute-done.12.refs_0_, bf16[256,384]{1,0:T(8,128)(2,1)S(1)} %collective-permute-done.13.refs_1_, f32[16,1024]{1,0:T(8,128)S(1)} %get-tuple-element.75.refs_2_, ...), custom_call_target="tpu_custom_call" | custom-call | flops 1572864 | bytes 1024 | tf_op jit(solution)/shard_map/pallas_call | solution.py:323
  111.3 9.3 %shard_map.75 = bf16[8,208,128]{2,1,0:T(8,128)(2,1)S(1)} custom-call(bf16[3,128,1024]{2,1,0:T(8,128)(2,1)S(1)} %get-tuple-element.56.q_ref, bf16[256,384]{1,0:T(8,128)(2,1)S(1)} %collective-permute-done.16.refs_0_, bf16[256,384]{1,0:T(8,128)(2,1)S(1)} %collective-permute-done.17.refs_1_, f32[16,1024]{1,0:T(8,128)S(1)} %get-tuple-element.77.refs_2_, ...), custom_call_target="tpu_custom_call" | custom-call | flops 1572864 | bytes 1024 | tf_op jit(solution)/shard_map/pallas_call | solution.py:323
  120.5 10.6 %all_to_all.10.parts_ref = bf16[8,208,128]{2,1,0:T(8,128)(2,1)S(1)} all-to-all(bf16[8,208,128]{2,1,0:T(8,128)(2,1)S(1)} %shard_map.75), channel_id=1, replica_groups=mesh['zq'=4,'zc'=2,'xl'=2,'xh'=2,'y'=4,'core'=2] {'zc','y'}, dimensions={0} | all-to-all | bytes 851968 | tf_op jit(solution)/shard_map/all_to_all | solution.py:399
  131.2 1.2 shard_map.76
  (39 shorter events, 0.5 us)
Async XLA Ops:
  0.0 1.1 copy-start.4
  1.1 0.7 copy-start.5
  1.8 13.0 %copy-start = (bf16[768,2304]{1,0:T(8,128)(2,1)S(1)}, bf16[768,2304]{1,0:T(8,128)(2,1)}, u32[]{:S(2)}) copy-start(bf16[768,2304]{1,0:T(8,128)(2,1)} %w_ref.6) | copy-start | bytes 10616836
  3.6 12.9 %collective-permute-start.2 = (bf16[1,768]{1,0:T(2,128)(2,1)S(1)}, bf16[1,768]{1,0:T(2,128)(2,1)S(1)}, u32[]{:S(2)}, u32[]{:S(2)}) collective-permute-start(bf16[1,768]{1,0:T(2,128)(2,1)S(1)} %get-tuple-element.48), channel_id=1, source_target_pairs={{0,17},{1,18},{2,19},{3,20},{4,21},{5,22},{6,23},{7,24},{8,25},{9,... | collective-permute-start | bytes 4616 | tf_op jit(solution)/shard_map/ppermute | solution.py:42
  9.1 7.4 %collective-permute-start = (bf16[16,768]{1,0:T(8,128)(2,1)S(1)}, bf16[16,768]{1,0:T(8,128)(2,1)S(1)}, u32[]{:S(2)}, u32[]{:S(2)}) collective-permute-start(bf16[16,768]{1,0:T(8,128)(2,1)S(1)} %get-tuple-element.46), channel_id=1, source_target_pairs={{0,16},{16,32},{32,48},{48,64},{64,80},{80,96},{96,112},{112,128},... | collective-permute-start | bytes 73736 | tf_op jit(solution)/shard_map/ppermute | solution.py:36
  12.7 3.9 %collective-permute-start.1 = (bf16[32,768]{1,0:T(8,128)(2,1)S(1)}, bf16[32,768]{1,0:T(8,128)(2,1)S(1)}, u32[]{:S(2)}, u32[]{:S(2)}) collective-permute-start(bf16[32,768]{1,0:T(8,128)(2,1)S(1)} %get-tuple-element.47), channel_id=1, source_target_pairs={{0,1},{1,2},{2,3},{3,4},{4,5},{5,6},{6,7},{7,8},{8,9},{9,10},{10,1... | collective-permute-start | bytes 147464 | tf_op jit(solution)/shard_map/ppermute | solution.py:36
  14.9 1.7 %copy-start.2 = (f32[9,1536]{1,0:T(8,128)S(1)}, f32[9,1536]{1,0:T(8,128)}, u32[]{:S(2)}) copy-start(f32[9,1536]{1,0:T(8,128)} %pool_ref.2) | copy-start | bytes 165892
  16.6 5.8 %copy-start.3 = (f32[9,768]{1,0:T(8,128)S(1)}, f32[9,768]{1,0:T(8,128)}, u32[]{:S(2)}) copy-start(f32[9,768]{1,0:T(8,128)} %pool_ref.3) | copy-start | bytes 82948
  17.2 6.5 %collective-permute-start.3 = (bf16[32,384]{1,0:T(8,128)(2,1)S(1)}, bf16[32,384]{1,0:T(8,128)(2,1)S(1)}, u32[]{:S(2)}, u32[]{:S(2)}) collective-permute-start(bf16[32,384]{1,0:T(8,128)(2,1)S(1)} %get-tuple-element.50), channel_id=1, source_target_pairs={{0,2},{2,4},{4,6},{6,0},{1,3},{3,5},{5,7},{7,1},{8,10},{10,12},{12... | collective-permute-start | bytes 73736 | tf_op jit(solution)/shard_map/ppermute | solution.py:25
  18.6 5.9 %collective-permute-start.4 = (bf16[32,384]{1,0:T(8,128)(2,1)S(1)}, bf16[32,384]{1,0:T(8,128)(2,1)S(1)}, u32[]{:S(2)}, u32[]{:S(2)}) collective-permute-start(bf16[32,384]{1,0:T(8,128)(2,1)S(1)} %get-tuple-element.51), channel_id=1, source_target_pairs={{0,4},{2,6},{4,0},{6,2},{1,5},{3,7},{5,1},{7,3},{8,12},{10,14},{12... | collective-permute-start | bytes 73736 | tf_op jit(solution)/shard_map/ppermute | solution.py:25
  22.3 2.7 %collective-permute-start.5 = (bf16[32,384]{1,0:T(8,128)(2,1)S(1)}, bf16[32,384]{1,0:T(8,128)(2,1)S(1)}, u32[]{:S(2)}, u32[]{:S(2)}) collective-permute-start(bf16[32,384]{1,0:T(8,128)(2,1)S(1)} %get-tuple-element.52), channel_id=1, source_target_pairs={{0,6},{2,0},{4,2},{6,4},{1,7},{3,1},{5,3},{7,5},{8,14},{10,8},{12,... | collective-permute-start | bytes 73736 | tf_op jit(solution)/shard_map/ppermute | solution.py:25
  25.0 15.1 %collective-permute-start.8 = (bf16[128,384]{1,0:T(8,128)(2,1)S(1)}, bf16[128,384]{1,0:T(8,128)(2,1)S(1)}, u32[]{:S(2)}, u32[]{:S(2)}) collective-permute-start(bf16[128,384]{1,0:T(8,128)(2,1)S(1)} %pad_maximum_fusion), channel_id=1, source_target_pairs={{0,192},{64,0},{128,64},{192,128},{1,193},{65,1},{129,65},{193,129... | collective-permute-start | bytes 294920 | tf_op jit(solution)/shard_map/ppermute | solution.py:25
  30.2 9.8 %collective-permute-start.7 = (bf16[128,384]{1,0:T(8,128)(2,1)S(1)}, bf16[128,384]{1,0:T(8,128)(2,1)S(1)}, u32[]{:S(2)}, u32[]{:S(2)}) collective-permute-start(bf16[128,384]{1,0:T(8,128)(2,1)S(1)} %pad_maximum_fusion), channel_id=1, source_target_pairs={{0,64},{64,128},{128,192},{192,0},{1,65},{65,129},{129,193},{193,1... | collective-permute-start | bytes 294920 | tf_op jit(solution)/shard_map/ppermute | solution.py:25
  30.2 9.8 %collective-permute-start.6 = (bf16[128,384]{1,0:T(8,128)(2,1)S(1)}, bf16[128,384]{1,0:T(8,128)(2,1)S(1)}, u32[]{:S(2)}, u32[]{:S(2)}) collective-permute-start(bf16[128,384]{1,0:T(8,128)(2,1)S(1)} %pad_maximum_fusion), channel_id=1, source_target_pairs={{0,128},{64,192},{128,0},{192,64},{1,129},{65,193},{129,1},{193,65... | collective-permute-start | bytes 294920 | tf_op jit(solution)/shard_map/ppermute | solution.py:25
  33.5 13.8 %all-to-all-start = ((bf16[8,192,128]{2,1,0:T(8,128)(2,1)}), bf16[8,192,128]{2,1,0:T(8,128)(2,1)S(1)}, u32[]{:S(2)}, u32[]{:S(2)}) async-start(bf16[8,192,128]{2,1,0:T(8,128)(2,1)} %shard_map.67), calls=%async_computation | async-start | bytes 786432 | tf_op jit(solution)/shard_map/all_to_all | solution.py:384
  40.2 10.5 %collective-permute-start.11 = (bf16[512,384]{1,0:T(8,128)(2,1)S(1)}, bf16[512,384]{1,0:T(8,128)(2,1)S(1)}, u32[]{:S(2)}, u32[]{:S(2)}) collective-permute-start(bf16[512,384]{1,0:T(8,128)(2,1)S(1)} %constant_dynamic-update-slice_fusion.refs_0_), channel_id=1, source_target_pairs={{0,1},{1,0},{2,3},{3,2},{4,5},{5,4},{6,7},{7,6},{8,9},{9,8},{10,11... | collective-permute-start | bytes 1179656 | tf_op jit(solution)/shard_map/ppermute | solution.py:25
  42.7 17.1 %collective-permute-start.10 = (bf16[512,384]{1,0:T(8,128)(2,1)S(1)}, bf16[512,384]{1,0:T(8,128)(2,1)S(1)}, u32[]{:S(2)}, u32[]{:S(2)}) collective-permute-start(bf16[512,384]{1,0:T(8,128)(2,1)S(1)} %constant_dynamic-update-slice_fusion.refs_0_), channel_id=1, source_target_pairs={{0,24},{16,0},{8,16},{24,8},{1,25},{17,1},{9,17},{25,9},{2,26},{18... | collective-permute-start | bytes 1179656 | tf_op jit(solution)/shard_map/ppermute | solution.py:31
  47.3 12.5 %collective-permute-start.9 = (bf16[512,384]{1,0:T(8,128)(2,1)S(1)}, bf16[512,384]{1,0:T(8,128)(2,1)S(1)}, u32[]{:S(2)}, u32[]{:S(2)}) collective-permute-start(bf16[512,384]{1,0:T(8,128)(2,1)S(1)} %constant_dynamic-update-slice_fusion.refs_0_), channel_id=1, source_target_pairs={{0,16},{16,8},{8,24},{24,0},{1,17},{17,9},{9,25},{25,1},{2,18},{18... | collective-permute-start | bytes 1179656 | tf_op jit(solution)/shard_map/ppermute | solution.py:31
  59.9 13.5 %collective-permute-start.15 = (bf16[512,384]{1,0:T(8,128)(2,1)S(1)}, bf16[512,384]{1,0:T(8,128)(2,1)S(1)}, u32[]{:S(2)}, u32[]{:S(2)}) collective-permute-start(bf16[512,384]{1,0:T(8,128)(2,1)S(1)} %collective-permute-done.9.refs_0_), channel_id=1, source_target_pairs={{0,1},{1,0},{2,3},{3,2},{4,5},{5,4},{6,7},{7,6},{8,9},{9,8},{10,11... | collective-permute-start | bytes 1179656 | tf_op jit(solution)/shard_map/ppermute | solution.py:25
  60.3 31.7 %collective-permute-start.14 = (bf16[512,384]{1,0:T(8,128)(2,1)S(1)}, bf16[512,384]{1,0:T(8,128)(2,1)S(1)}, u32[]{:S(2)}, u32[]{:S(2)}) collective-permute-start(bf16[512,384]{1,0:T(8,128)(2,1)S(1)} %collective-permute-done.10.refs_0_), channel_id=1, source_target_pairs={{0,1},{1,0},{2,3},{3,2},{4,5},{5,4},{6,7},{7,6},{8,9},{9,8},{10,11... | collective-permute-start | bytes 1179656 | tf_op jit(solution)/shard_map/ppermute | solution.py:25
  60.5 40.6 %collective-permute-start.13 = (bf16[256,384]{1,0:T(8,128)(2,1)S(1)}, bf16[256,384]{1,0:T(8,128)(2,1)S(1)}, u32[]{:S(2)}, u32[]{:S(2)}) collective-permute-start(bf16[256,384]{1,0:T(8,128)(2,1)S(1)} %slice.7), channel_id=1, source_target_pairs={{0,24},{16,0},{8,16},{24,8},{1,25},{17,1},{9,17},{25,9},{2,26},{18... | collective-permute-start | bytes 589832 | tf_op jit(solution)/shard_map/ppermute | solution.py:31
  64.2 37.0 %collective-permute-start.12 = (bf16[256,384]{1,0:T(8,128)(2,1)S(1)}, bf16[256,384]{1,0:T(8,128)(2,1)S(1)}, u32[]{:S(2)}, u32[]{:S(2)}) collective-permute-start(bf16[256,384]{1,0:T(8,128)(2,1)S(1)} %slice.6), channel_id=1, source_target_pairs={{0,16},{16,8},{8,24},{24,0},{1,17},{17,9},{9,25},{25,1},{2,18},{18... | collective-permute-start | bytes 589832 | tf_op jit(solution)/shard_map/ppermute | solution.py:31
  101.2 10.1 %collective-permute-start.16 = (bf16[256,384]{1,0:T(8,128)(2,1)S(1)}, bf16[256,384]{1,0:T(8,128)(2,1)S(1)}, u32[]{:S(2)}, u32[]{:S(2)}) collective-permute-start(bf16[256,384]{1,0:T(8,128)(2,1)S(1)} %collective-permute-done.12.refs_0_), channel_id=1, source_target_pairs={{0,1},{1,0},{2,3},{3,2},{4,5},{5,4},{6,7},{7,6},{8,9},{9,8},{10,11... | collective-permute-start | bytes 589832 | tf_op jit(solution)/shard_map/ppermute | solution.py:25
  102.0 9.3 %collective-permute-start.17 = (bf16[256,384]{1,0:T(8,128)(2,1)S(1)}, bf16[256,384]{1,0:T(8,128)(2,1)S(1)}, u32[]{:S(2)}, u32[]{:S(2)}) collective-permute-start(bf16[256,384]{1,0:T(8,128)(2,1)S(1)} %collective-permute-done.13.refs_1_), channel_id=1, source_target_pairs={{0,1},{1,0},{2,3},{3,2},{4,5},{5,4},{6,7},{7,6},{8,9},{9,8},{10,11... | collective-permute-start | bytes 589832 | tf_op jit(solution)/shard_map/ppermute | solution.py:25
  111.3 19.9 %copy-start.1 = (bf16[768,768]{1,0:T(8,128)(2,1)S(1)}, bf16[768,768]{1,0:T(8,128)(2,1)}, u32[]{:S(2)}) copy-start(bf16[768,768]{1,0:T(8,128)(2,1)} %w_ref.7) | copy-start | bytes 3538948
